TPU v7x, 128 devices: a whole 4x4x4 slice. The times are simulated.
128 devices in a mesh: pair: 8 (over y, core), fold: 16 (over z, x).
Axes of the slice: x: 4, y: 4, z: 4, core: 2. Of those that a mesh axis runs over, the one named last changes fastest.
Arguments:
- amplitudes: bfloat16 [4, 80, 640, 640], P(None, 'pair', 'fold'), may hold values from -6 to 6
- cycle_block: bfloat16 [640, 80, 16, 640], P('fold', None, 'pair'), may hold values from -0.078125 to 0.078125
- occ_sizes: int32 [8], replicated, may hold values from 1 to 20, 80 in all
- vir_sizes: int32 [8], replicated, may hold values from 1 to 160, 640 in all
- window_i: int32 [4], replicated, may hold values from 0 to 79
- window_occ: int32 [16], replicated, may hold values from 0 to 79
Outputs:
- residual: bfloat16 [4, 640, 16, 640], P(None, 'fold', 'pair')
Inputs may be any that keep to these rules, and one draw needn't show every extreme that they name: `occ_sizes`: the entries sum to 80. `vir_sizes`: the entries sum to 640.
All inputs are finite; a program needn't handle non-finite values.
Results may differ from a plain program's by a relative error of at most 0.001.
Values may be sent and summed in bfloat16 or wider, within the bound.
No kernel may reach another device: no remote copies, remote signals or barrier semaphores. Data moves between devices by JAX's collectives and lax.ppermute only.
A program may use at most 128 MiB of HBM per device.

v0:
```python
import jax
import jax.numpy as jnp
from jax import lax
from jax.sharding import PartitionSpec as P


def irrep_labels(sizes, count):
    boundaries = jnp.cumsum(sizes)
    positions = jnp.arange(count, dtype=jnp.int32)
    return jnp.sum((positions[:, None] >= boundaries[None, :]).astype(jnp.int32), axis=1)


def label_lookup(orbitals, labels, count):
    matches = orbitals[:, None] == jnp.arange(count, dtype=jnp.int32)[None, :]
    return jnp.sum(jnp.where(matches, labels[None, :], 0), axis=1)


def body(amplitudes, cycle_block, occ_sizes, vir_sizes, window_i, window_occ):
    c_local = cycle_block.shape[0]
    occ_total = cycle_block.shape[1]
    j_local = cycle_block.shape[2]
    vir_total = cycle_block.shape[3]
    k_local = amplitudes.shape[1]
    a_rows = amplitudes.shape[2]
    occ_labels = irrep_labels(occ_sizes, occ_total)
    vir_labels = irrep_labels(vir_sizes, vir_total)
    c_labels = lax.dynamic_slice_in_dim(vir_labels, lax.axis_index("fold") * c_local, c_local)
    a_labels = lax.dynamic_slice_in_dim(vir_labels, lax.axis_index("fold") * a_rows, a_rows)
    k_labels = lax.dynamic_slice_in_dim(occ_labels, lax.axis_index("pair") * k_local, k_local)
    i_labels = label_lookup(window_i, occ_labels, occ_total)
    j_orbitals = lax.dynamic_slice_in_dim(window_occ, lax.axis_index("pair") * j_local, j_local)
    j_labels = label_lookup(j_orbitals, occ_labels, occ_total)
    amp_parity = jnp.bitwise_xor(
        jnp.bitwise_xor(i_labels[:, None, None, None], k_labels[None, :, None, None]),
        jnp.bitwise_xor(a_labels[None, None, :, None], vir_labels[None, None, None, :]),
    )
    masked_amps = jnp.where(amp_parity == 0, amplitudes, jnp.zeros_like(amplitudes))
    parity = jnp.bitwise_xor(
        jnp.bitwise_xor(c_labels[:, None, None, None], occ_labels[None, :, None, None]),
        jnp.bitwise_xor(j_labels[None, None, :, None], vir_labels[None, None, None, :]),
    )
    masked = jnp.where(parity == 0, cycle_block, jnp.zeros_like(cycle_block))
    relaid = lax.all_to_all(masked_amps, "fold", split_axis=3, concat_axis=2, tiled=True)
    gathered = lax.all_gather(relaid, "pair", axis=1, tiled=True)
    partial_sum = jnp.einsum(
        "ikac,ckjb->iajb", gathered, masked, preferred_element_type=jnp.float32
    )
    summed = lax.psum(partial_sum, "fold")
    a_local = vir_total // lax.axis_size("fold")
    own_share = lax.dynamic_slice_in_dim(summed, lax.axis_index("fold") * a_local, a_local, 1)
    return own_share.astype(jnp.bfloat16)


def solution(mesh):
    placed = (P(None, "pair", "fold", None), P("fold", None, "pair", None), P(), P(), P(), P())
    return jax.shard_map(
        body, mesh=mesh, in_specs=placed, out_specs=P(None, "fold", "pair", None), check_vma=False
    )
```

profile of v0, /device:TPU:0, one launch (start us, length us, event | category | flops | bytes accessed | tf_op | source)
XLA Modules:
  0.0 537.1 jit_solution(16478220033967384527)
XLA Ops:
  6.5 0.8 reduce-window.16
  7.4 0.1 convert_reduce_fusion.1
  7.5 0.1 dynamic_slice.13
  7.5 0.8 select_reduce_fusion
  8.4 0.8 reduce-window.17
  9.2 0.1 convert_reduce_fusion
  9.3 0.1 dynamic_slice.14
  9.4 0.1 broadcast_xor_fusion
  9.5 15.4 %copy.20 = bf16[4,10,40,640]{2,1,0,3:T(8,128)(2,1)} copy(bf16[4,10,40,640]{3,2,1,0:T(8,128)(2,1)} %param.6) | data formatting | bytes 4096000 | tf_op args[0]
  25.0 11.6 %fusion.11 = bf16[640,4,10,40]{3,2,1,0:T(8,128)(2,1)} fusion(bf16[4,10,40,640]{2,1,0,3:T(8,128)(2,1)} %copy.20, s32[40,640]{0,1:T(8,128)S(1)} %broadcast_xor_fusion, s32[4,10]{1,0:T(4,128)S(1)} %broadcast_xor_fusion.3), kind=kLoop, calls=%fused_computation.22 | loop fusion | flops 3072000 | bytes 4198560
  36.7 15.1 %reshape.185 = bf16[16,2,32000]{2,1,0:T(2,128)(2,1)S(1)} reshape(bf16[640,4,10,40]{3,2,1,0:T(8,128)(2,1)} %fusion.11) | data formatting | bytes 4096000
  51.8 35.7 %all_to_all.18 = bf16[16,2,32000]{2,1,0:T(2,128)(2,1)} all-to-all(bf16[16,2,32000]{2,1,0:T(2,128)(2,1)S(1)} %reshape.185), channel_id=1, replica_groups=mesh['pair'=8,'fold'=16] {'fold'}, dimensions={0} | all-to-all | bytes 4096000 | tf_op jit(solution)/shard_map/all_to_all | solution.py:43
  87.5 15.5 %reshape.186 = bf16[640,4,10,40]{3,2,1,0:T(8,128)(2,1)} reshape(bf16[16,2,32000]{2,1,0:T(2,128)(2,1)} %all_to_all.18) | data formatting | bytes 4096000
  103.1 10.9 %copy.41 = bf16[4,10,40,16,40]{2,3,4,1,0:T(8,128)(2,1)} copy(bf16[4,10,40,16,40]{2,1,0,4,3:T(8,128)(2,1)} %bitcast.27) | data formatting | bytes 4096000 | tf_op jit(solution)/shard_map/all_to_all | solution.py:43
  114.0 9.0 %all_to_all.16 = bf16[4,10,640,40]{2,3,1,0:T(8,128)(2,1)S(1)} reshape(bf16[4,10,16,40,40]{3,2,4,1,0:T(8,128)(2,1)} %bitcast.28) | data formatting | bytes 4096000 | tf_op jit(solution)/shard_map/all_to_all | solution.py:43
  122.9 1.5 copy.22
  124.5 0.1 dynamic_slice.15
  124.5 0.2 fusion.10
  124.9 14.3 %compare_select_fusion = bf16[40,80,2,640]{3,2,1,0:T(2,128)(2,1)} fusion(bf16[40,80,2,640]{3,2,1,0:T(2,128)(2,1)} %param.7, s32[2,640]{1,0:T(2,128)S(1)} %broadcast_xor_fusion.2, s32[40,80]{1,0:T(8,128)S(1)} %broadcast_xor_fusion.1), kind=kLoop, calls=%fused_computation | loop fusion | flops 12288000 | bytes 16401920 | tf_op jit(solution)/shard_map/jit(_where)/select_n | solution.py:42
  139.2 66.4 %all-gather.2.cloned.1.call-done = bf16[4,80,640,40]{2,3,0,1:T(8,128)(2,1)} async-done(((bf16[4,10,640,40]{2,3,0,1:T(8,128)(2,1)}), bf16[4,80,640,40]{2,3,0,1:T(8,128)(2,1)}) %all-gather.2.cloned.1.call-update) | async-done | bytes 16384016 | tf_op jit(solution)/shard_map/all_gather | solution.py:44
  205.5 34.9 %fusion.5 = f32[4,640,2,640]{3,1,2,0:T(8,128)} fusion(bf16[40,80,2,640]{3,2,1,0:T(2,128)(2,1)} %compare_select_fusion, bf16[4,80,640,40]{2,3,0,1:T(8,128)(2,1)} %all-gather.2.cloned.1.call-done), kind=kOutput, calls=%fused_computation.7 | convolution fusion | flops 20971520000 | bytes 37683200 | tf_op jit(solution)/shard_map/ikac,ckjb->iajb/dot_general | solution.py:45
  240.5 287.6 %all-reduce.1 = bf16[4,640,2,640]{3,1,2,0:T(8,128)(2,1)} all-reduce(f32[4,640,2,640]{3,1,2,0:T(8,128)} %fusion.5), channel_id=1, replica_groups=mesh['pair'=8,'fold'=16] {'fold'}, use_global_device_ids=true, to_apply=%region_6.7 | all-reduce | flops 3276800 | bytes 19660800 | tf_op jit(solution)/shard_map/psum | solution.py:48
  528.1 1.0 dynamic-slice_convert_fusion
  529.2 1.1 copy.25
  (7 shorter events, 0.2 us)
Async XLA Ops:
  6.5 199.0 %all-gather.2.cloned.1.call-start = ((), (), s32[]{:S(2)}) async-start(), calls=%async_computation.1 | async-start | bytes 18432000 | tf_op jit(solution)/shard_map/all_gather | solution.py:44
  114.0 10.5 %copy-start = (s32[16]{0:T(128)S(1)}, s32[16]{0:T(128)}, u32[]{:S(2)}) copy-start(s32[16]{0:T(128)} %param.11) | copy-start | bytes 196
Sparse Core Ops, SparseCore 0:
  124.6 80.9 all-gather.1
where the time goes:
time: 538 us; the launch traced here: 537 us
  blocking collectives  323 us (60%)
  local copies, waits for them, and re-layouts  69.8 us (13%)
  waiting for transfers between devices  66.4 us (12%)
  matrix products  34.9 us (6%)
  other arithmetic  29.1 us (5%)
  between operations  13.4 us (2%)
    psum x1, blocking collectives, body(): summed = lax.psum(partial_sum, 'fold')  288 us
    all_gather x1, waiting for transfers between devices, body(): gathered = lax.all_gather(relaid, 'pair', axis=1, tiled=True)  66.4 us
    unnamed x5, local copies, waits for them, and re-layouts  46.1 us
    all_to_all x1, blocking collectives, body(): lax.all_to_all(masked_amps, 'fold', split_axis=3, concat_axis=2, tiled=True)  35.7 us
    dot_general x1, matrix products, body(): jnp.einsum('ikac,ckjb->iajb', gathered, masked, preferred_element_type=jn...  34.9 us
    all_to_all x3, local copies, waits for them, and re-layouts, body(): lax.all_to_all(masked_amps, 'fold', split_axis=3, concat_axis=2, tiled=True)  21.3 us
    select_n x1, other arithmetic, body(): masked = jnp.where(parity == 0, cycle_block, jnp.zeros_like(cycle_block))  14.3 us
    unnamed x1, other arithmetic  11.6 us
  transfers between devices with their start and end apart: 1, of which 1 were waited for; matrix products, arithmetic and copies ran while one was open for 3% of the time, Pallas kernels for 0%

commit v1 on v0

--- a/solution.py
+++ b/solution.py
@@ -5,7 +5,8 @@
 
 
 def irrep_labels(sizes, count):
-    boundaries = jnp.cumsum(sizes)
+    order = jnp.arange(sizes.shape[0], dtype=jnp.int32)
+    boundaries = jnp.sum(jnp.where(order[None, :] <= order[:, None], sizes[None, :], 0), axis=1)
     positions = jnp.arange(count, dtype=jnp.int32)
     return jnp.sum((positions[:, None] >= boundaries[None, :]).astype(jnp.int32), axis=1)
 

time: 538 us -> 538 us (level)
  no operation moved by 1% of the time
where the time goes in v1:
time: 538 us; the launch traced here: 537 us
  blocking collectives  323 us (60%)
  local copies, waits for them, and re-layouts  69.8 us (13%)
  waiting for transfers between devices  66.4 us (12%)
  matrix products  34.9 us (6%)
  other arithmetic  29 us (5%)
  between operations  13.4 us (2%)
    psum x1, blocking collectives, body(): summed = lax.psum(partial_sum, 'fold')  288 us
    all_gather x1, waiting for transfers between devices, body(): gathered = lax.all_gather(relaid, 'pair', axis=1, tiled=True)  66.4 us
    unnamed x5, local copies, waits for them, and re-layouts  46.1 us
    all_to_all x1, blocking collectives, body(): lax.all_to_all(masked_amps, 'fold', split_axis=3, concat_axis=2, tiled=True)  35.7 us
    dot_general x1, matrix products, body(): jnp.einsum('ikac,ckjb->iajb', gathered, masked, preferred_element_type=jn...  34.9 us
    all_to_all x3, local copies, waits for them, and re-layouts, body(): lax.all_to_all(masked_amps, 'fold', split_axis=3, concat_axis=2, tiled=True)  21.3 us
    select_n x1, other arithmetic, body(): masked = jnp.where(parity == 0, cycle_block, jnp.zeros_like(cycle_block))  14.3 us
    unnamed x1, other arithmetic  11.6 us
  transfers between devices with their start and end apart: 1, of which 1 were waited for; matrix products, arithmetic and copies ran while one was open for 3% of the time, Pallas kernels for 0%

profile of v1, /device:TPU:0, one launch (start us, length us, event | category | flops | bytes accessed | tf_op | source)
XLA Modules:
  0.0 537.0 jit_solution(14902203011356756765)
XLA Ops:
  6.5 0.8 select_reduce_fusion.1
  7.3 0.1 convert_reduce_fusion.1
  7.4 0.1 dynamic_slice.13
  7.5 0.8 select_reduce_fusion.2
  8.3 0.8 select_reduce_fusion
  9.1 0.1 convert_reduce_fusion
  9.2 0.1 dynamic_slice.14
  9.3 0.1 broadcast_xor_fusion
  9.4 15.4 %copy.20 = bf16[4,10,40,640]{2,1,0,3:T(8,128)(2,1)} copy(bf16[4,10,40,640]{3,2,1,0:T(8,128)(2,1)} %param.6) | data formatting | bytes 4096000 | tf_op args[0]
  24.9 11.6 %fusion.11 = bf16[640,4,10,40]{3,2,1,0:T(8,128)(2,1)} fusion(bf16[4,10,40,640]{2,1,0,3:T(8,128)(2,1)} %copy.20, s32[40,640]{0,1:T(8,128)S(1)} %broadcast_xor_fusion, s32[4,10]{1,0:T(4,128)S(1)} %broadcast_xor_fusion.3), kind=kLoop, calls=%fused_computation.25 | loop fusion | flops 3072000 | bytes 4198560
  36.5 15.1 %reshape.137 = bf16[16,2,32000]{2,1,0:T(2,128)(2,1)S(1)} reshape(bf16[640,4,10,40]{3,2,1,0:T(8,128)(2,1)} %fusion.11) | data formatting | bytes 4096000
  51.7 35.7 %all_to_all.18 = bf16[16,2,32000]{2,1,0:T(2,128)(2,1)} all-to-all(bf16[16,2,32000]{2,1,0:T(2,128)(2,1)S(1)} %reshape.137), channel_id=1, replica_groups=mesh['pair'=8,'fold'=16] {'fold'}, dimensions={0} | all-to-all | bytes 4096000 | tf_op jit(solution)/shard_map/all_to_all | solution.py:44
  87.4 15.5 %reshape.138 = bf16[640,4,10,40]{3,2,1,0:T(8,128)(2,1)} reshape(bf16[16,2,32000]{2,1,0:T(2,128)(2,1)} %all_to_all.18) | data formatting | bytes 4096000
  103.0 10.9 %copy.41 = bf16[4,10,40,16,40]{2,3,4,1,0:T(8,128)(2,1)} copy(bf16[4,10,40,16,40]{2,1,0,4,3:T(8,128)(2,1)} %bitcast.23) | data formatting | bytes 4096000 | tf_op jit(solution)/shard_map/all_to_all | solution.py:44
  113.8 9.0 %all_to_all.16 = bf16[4,10,640,40]{2,3,1,0:T(8,128)(2,1)S(1)} reshape(bf16[4,10,16,40,40]{3,2,4,1,0:T(8,128)(2,1)} %bitcast.24) | data formatting | bytes 4096000 | tf_op jit(solution)/shard_map/all_to_all | solution.py:44
  122.8 1.5 copy.22
  124.4 0.1 dynamic_slice.15
  124.4 0.2 fusion.10
  124.8 14.3 %compare_select_fusion = bf16[40,80,2,640]{3,2,1,0:T(2,128)(2,1)} fusion(bf16[40,80,2,640]{3,2,1,0:T(2,128)(2,1)} %param.7, s32[2,640]{1,0:T(2,128)S(1)} %broadcast_xor_fusion.2, s32[40,80]{1,0:T(8,128)S(1)} %broadcast_xor_fusion.1), kind=kLoop, calls=%fused_computation | loop fusion | flops 12288000 | bytes 16401920 | tf_op jit(solution)/shard_map/jit(_where)/select_n | solution.py:43
  139.0 66.4 %all-gather.2.cloned.1.call-done = bf16[4,80,640,40]{2,3,0,1:T(8,128)(2,1)} async-done(((bf16[4,10,640,40]{2,3,0,1:T(8,128)(2,1)}), bf16[4,80,640,40]{2,3,0,1:T(8,128)(2,1)}) %all-gather.2.cloned.1.call-update) | async-done | bytes 16384016 | tf_op jit(solution)/shard_map/all_gather | solution.py:45
  205.4 34.9 %fusion.5 = f32[4,640,2,640]{3,1,2,0:T(8,128)} fusion(bf16[40,80,2,640]{3,2,1,0:T(2,128)(2,1)} %compare_select_fusion, bf16[4,80,640,40]{2,3,0,1:T(8,128)(2,1)} %all-gather.2.cloned.1.call-done), kind=kOutput, calls=%fused_computation.7 | convolution fusion | flops 20971520000 | bytes 37683200 | tf_op jit(solution)/shard_map/ikac,ckjb->iajb/dot_general | solution.py:46
  240.4 287.6 %all-reduce.1 = bf16[4,640,2,640]{3,1,2,0:T(8,128)(2,1)} all-reduce(f32[4,640,2,640]{3,1,2,0:T(8,128)} %fusion.5), channel_id=1, replica_groups=mesh['pair'=8,'fold'=16] {'fold'}, use_global_device_ids=true, to_apply=%region_6.7 | all-reduce | flops 3276800 | bytes 19660800 | tf_op jit(solution)/shard_map/psum | solution.py:49
  528.0 1.0 dynamic-slice_convert_fusion
  529.0 1.1 copy.25
  (7 shorter events, 0.2 us)
Async XLA Ops:
  6.5 198.9 %all-gather.2.cloned.1.call-start = ((), (), s32[]{:S(2)}) async-start(), calls=%async_computation.1 | async-start | bytes 18432000 | tf_op jit(solution)/shard_map/all_gather | solution.py:45
  113.8 10.5 %copy-start = (s32[16]{0:T(128)S(1)}, s32[16]{0:T(128)}, u32[]{:S(2)}) copy-start(s32[16]{0:T(128)} %param.11) | copy-start | bytes 196
Sparse Core Ops, SparseCore 0:
  124.5 80.9 all-gather.1

commit v2 on v0

v2 whole, which is shorter than its diff:
```python
import jax
import jax.numpy as jnp
from jax import lax
from jax.sharding import PartitionSpec as P

BF16, F32 = jnp.bfloat16, jnp.float32


def prefix_sums(sizes):
    order = jnp.arange(sizes.shape[0], dtype=jnp.int32)
    return jnp.sum(jnp.where(order[None, :] <= order[:, None], sizes[None, :], 0), axis=1)


def irrep_labels(sizes, count):
    ends = prefix_sums(sizes)
    positions = jnp.arange(count, dtype=jnp.int32)
    after = positions[:, None] >= ends[None, :]
    labels = jnp.sum(after.astype(jnp.int32), axis=1)
    places = positions - jnp.sum(jnp.where(after, sizes[None, :], 0), axis=1)
    return labels, places


def label_lookup(orbitals, labels, count):
    matches = orbitals[:, None] == jnp.arange(count, dtype=jnp.int32)[None, :]
    return jnp.sum(jnp.where(matches, labels[None, :], 0), axis=1)


def one_hot_rows(places, width):
    return (jnp.arange(width, dtype=jnp.int32)[:, None] == places[None, :]).astype(BF16)


def pick(x, spec, y):
    return jnp.einsum(spec, x, y, preferred_element_type=F32).astype(BF16)


def body(amplitudes, cycle_block, occ_sizes, vir_sizes, window_i, window_occ):
    irreps = occ_sizes.shape[0]
    n_fold, n_pair = lax.axis_size("fold"), lax.axis_size("pair")
    fold, pair = lax.axis_index("fold"), lax.axis_index("pair")
    c_local, occ_total, j_local, vir_total = cycle_block.shape
    n_i, k_local, a_local, _ = amplitudes.shape
    vmax, omax = vir_total // 4, occ_total // 4
    halves = n_pair // n_i
    a_part = a_local // halves

    occ, occ_place = irrep_labels(occ_sizes, occ_total)
    vir, vir_place = irrep_labels(vir_sizes, vir_total)
    to_place = one_hot_rows(vir_place, vmax)
    to_kappa = one_hot_rows(occ_place, omax)
    own_vir = lax.dynamic_slice_in_dim(vir, fold * c_local, c_local)
    k_own = lax.dynamic_slice_in_dim(occ, pair * k_local, k_local)
    i_labels = label_lookup(window_i, occ, occ_total)
    j_labels = label_lookup(lax.dynamic_slice_in_dim(window_occ, pair * j_local, j_local), occ, occ_total)

    x = i_labels[:, None, None] ^ k_own[None, :, None] ^ own_vir[None, None, :]
    masked = jnp.where(x[..., None] == vir, amplitudes, jnp.zeros_like(amplitudes))
    narrow = pick(masked, "ikac,tc->ikat", to_place)
    narrow = narrow.reshape(n_i, k_local, halves, a_part, vmax).transpose(0, 2, 1, 3, 4)
    narrow = narrow.reshape(n_pair, k_local, a_part, vmax)
    narrow = lax.all_to_all(narrow, "pair", split_axis=0, concat_axis=0, tiled=True)
    narrow = narrow.reshape(occ_total, a_part, vmax)

    i_mine = lax.dynamic_index_in_dim(i_labels, pair // halves, keepdims=False)
    a_mine = lax.dynamic_slice_in_dim(vir, fold * a_local + (pair % halves) * a_part, a_part)
    wide = pick(narrow, "kat,tc->akc", to_place)
    x = i_mine ^ occ[None, :, None] ^ a_mine[:, None, None] ^ vir[None, None, :]
    wide = jnp.where(x == 0, wide, jnp.zeros_like(wide))
    short = pick(to_kappa, "qk,akc->aqc", wide)
    short = short.reshape(a_part, omax, n_fold, c_local).transpose(2, 0, 1, 3)
    short = short.reshape(n_fold, a_part, omax * c_local)
    short = lax.all_to_all(short, "fold", split_axis=0, concat_axis=0, tiled=True)
    lhs = lax.all_gather(short, "pair", axis=0)

    x = own_vir[:, None, None] ^ occ[None, :, None] ^ j_labels[None, None, :]
    masked = jnp.where(x[..., None] == vir, cycle_block, jnp.zeros_like(cycle_block))
    rhs = pick(masked, "ckjb,tb->ckjt", to_place)
    classes = jnp.arange(irreps, dtype=jnp.int32)
    x = classes[:, None, None] == (occ[None, :, None] ^ own_vir[None, None, :])
    chosen = jnp.where(x[:, None], to_kappa[None, :, :, None], jnp.zeros((), BF16))
    rhs = pick(chosen, "rqkc,ckjt->rqcjt", rhs)
    rhs = rhs.reshape(irreps * omax * c_local, j_local * vmax)

    a_class = vir.reshape(n_fold, halves, a_part)
    row = i_labels[:, None, None, None] ^ a_class.transpose(1, 0, 2)[None]
    row = row.reshape(n_pair, n_fold, a_part)
    spread = jnp.where(
        row[..., None, None] == classes[:, None], lhs[:, :, :, None, :], jnp.zeros((), BF16)
    ).reshape(n_pair, n_fold, a_part, -1)
    partial_sum = jnp.einsum("pfak,kn->fpan", spread, rhs, preferred_element_type=F32)
    shares = lax.all_to_all(partial_sum, "fold", split_axis=0, concat_axis=0, tiled=True)
    total = jnp.sum(shares, axis=0).astype(BF16)
    total = total.reshape(n_i, a_local, j_local, vmax)
    spread_b = pick(total, "iajt,tb->iajb", to_place)
    x = i_labels[:, None, None] ^ own_vir[None, :, None] ^ j_labels[None, None, :]
    return jnp.where(x[..., None] == vir, spread_b, jnp.zeros_like(spread_b))


def solution(mesh):
    placed = (P(None, "pair", "fold", None), P("fold", None, "pair", None), P(), P(), P(), P())
    return jax.shard_map(
        body, mesh=mesh, in_specs=placed, out_specs=P(None, "fold", "pair", None), check_vma=False
    )
```

time: 538 us -> 299 us (0.56)
  blocking collectives: 323 us -> 20.8 us
  local copies, waits for them, and re-layouts: 69.8 us -> 99.9 us
  other arithmetic: 29.1 us -> 39.8 us
  matrix products: 34.9 us -> 45 us
  starting transfers between devices: 0.01 us -> 9.1 us
    psum x1 -> x0, blocking collectives: 288 us -> none  [body(): summed = lax.psum(partial_sum, 'fold')]
    all_to_all x0 -> x2, waiting for transfers between devices: none -> 69 us  [the longest x1 55.2 us: body(): lax.all_to_all(partial_sum, 'fold', split_axis=0, concat_axis=0, tiled=True)]
    all_gather x1, waiting for transfers between devices: 66.4 us -> 0.02 us  [body(): lhs = lax.all_gather(short, 'pair', axis=0)]
    select_n x0 -> x2, local copies, waits for them, and re-layouts: none -> 59.1 us  [the longest x1 58.1 us: body(): jnp.where(row[..., None, None] == classes[:, None], lhs[:, :, :, None, :]...]
    unnamed x5 -> x2, local copies, waits for them, and re-layouts: 46.1 us -> 0.01 us
    reshape x0 -> x6, local copies, waits for them, and re-layouts: none -> 21 us  [the longest x1 14.4 us: body(): rhs = rhs.reshape(irreps * omax * c_local, j_local * vmax)]
    all_to_all x3 -> x1, local copies, waits for them, and re-layouts: 21.3 us -> 0.87 us  [body(): lax.all_to_all(short, 'fold', split_axis=0, concat_axis=0, tiled=True)]
    select_n x1 -> x2, other arithmetic: 14.3 us -> 30 us  [the longest x1 16.1 us: body(): jnp.where(x[..., None] == vir, cycle_block, jnp.zeros_like(cycle_block))]
  transfers between devices with their start and end apart: 1 -> 3, of which waited for: 1 -> 2; matrix products, arithmetic and copies ran while one was open for 3% -> 20% of each run, Pallas kernels for 0% -> 0%
where the time goes in v2:
time: 299 us; the launch traced here: 297 us
  local copies, waits for them, and re-layouts  99.9 us (33%)
  waiting for transfers between devices  69 us (23%)
  matrix products  45 us (15%)
  other arithmetic  39.8 us (13%)
  blocking collectives  20.8 us (7%)
  between operations  13.6 us (5%)
  starting transfers between devices  9.1 us (3%)
    select_n x1, local copies, waits for them, and re-layouts, body(): jnp.where(row[..., None, None] == classes[:, None], lhs[:, :, :, None, :]...  58.1 us
    all_to_all x1, waiting for transfers between devices, body(): lax.all_to_all(partial_sum, 'fold', split_axis=0, concat_axis=0, tiled=True)  55.2 us
    dot_general x1, matrix products, body(): jnp.einsum('pfak,kn->fpan', spread, rhs, preferred_element_type=F32)  28.8 us
    all_to_all x1, blocking collectives, body(): lax.all_to_all(short, 'fold', split_axis=0, concat_axis=0, tiled=True)  20.8 us
    dot_general x4, matrix products, pick(): return jnp.einsum(spec, x, y, preferred_element_type=F32).astype(BF16)  16.2 us
    select_n x1, other arithmetic, body(): jnp.where(x[..., None] == vir, cycle_block, jnp.zeros_like(cycle_block))  16.1 us
    reshape x1, local copies, waits for them, and re-layouts, body(): rhs = rhs.reshape(irreps * omax * c_local, j_local * vmax)  14.4 us
    select_n x1, other arithmetic, body(): jnp.where(row[..., None, None] == classes[:, None], lhs[:, :, :, None, :]...  13.8 us
  transfers between devices with their start and end apart: 3, of which 2 were waited for; matrix products, arithmetic and copies ran while one was open for 20% of the time, Pallas kernels for 0%

profile of v2, /device:TPU:0, one launch (start us, length us, event | category | flops | bytes accessed | tf_op | source)
XLA Modules:
  0.0 297.1 jit_solution(2965070127442279412)
XLA Ops:
  8.1 0.8 select_reduce_fusion.4
  9.0 0.8 select_reduce_fusion.2
  10.7 2.7 fusion.32
  13.7 1.1 pad_maximum_fusion
  14.8 4.6 %all-to-all-start = ((bf16[8,10,20,160]{3,2,1,0:T(8,128)(2,1)}), bf16[8,10,20,160]{3,2,1,0:T(8,128)(2,1)S(1)}, u32[]{:S(2)}, u32[]{:S(2)}) async-start(bf16[8,10,20,160]{3,2,1,0:T(8,128)(2,1)} %bitcast.13), calls=%async_computation | async-start | bytes 1966080 | tf_op jit(solution)/shard_map/all_to_all | solution.py:60
  20.8 13.8 %all-to-all-done = bf16[8,10,20,160]{3,2,1,0:T(8,128)(2,1)S(1)} async-done(((bf16[8,10,20,160]{3,2,1,0:T(8,128)(2,1)}), bf16[8,10,20,160]{3,2,1,0:T(8,128)(2,1)S(1)}, u32[]{:S(2)}, u32[]{:S(2)}) %all-to-all-start) | async-done | bytes 512032 | tf_op jit(solution)/shard_map/all_to_all | solution.py:60
  34.6 1.2 fusion.36
  35.8 3.3 %reshape.270 = bf16[20,20,16,40]{3,2,1,0:T(8,128)(2,1)} reshape(bf16[20,20,640]{2,1,0:T(8,128)(2,1)S(1)} %fusion.36) | data formatting | bytes 1024000 | tf_op jit(solution)/shard_map/reshape | solution.py:69
  39.1 1.9 copy.91
  41.1 1.2 reshape.271
  42.4 20.8 %all_to_all.15 = bf16[16,20,800]{2,1,0:T(8,128)(2,1)S(1)} all-to-all(bf16[16,20,800]{2,1,0:T(8,128)(2,1)S(1)} %copy.59), channel_id=1, replica_groups=mesh['pair'=8,'fold'=16] {'fold'}, dimensions={0} | all-to-all | bytes 1024000 | tf_op jit(solution)/shard_map/all_to_all | solution.py:71
  63.2 0.9 copy.60
  65.4 16.1 %compare_select_fusion = bf16[40,80,2,640]{3,2,1,0:T(2,128)(2,1)} fusion(bf16[40,80,2,640]{3,2,1,0:T(2,128)(2,1)} %param.7, s32[640]{0:T(1024)S(1)} %get-tuple-element.8, s32[40,80,2]{2,1,0:T(8,128)S(1)} %broadcast_xor_fusion), kind=kLoop, calls=%fused_computation.3 | loop fusion | flops 8192000 | bytes 16412160 | tf_op jit(solution)/shard_map/jit(_where)/select_n | solution.py:75
  81.5 11.9 %convert_bitcast_fusion = bf16[8,20,40,2,160]{4,1,0,3,2:T(8,128)(2,1)} fusion(bf16[40,80,2,640]{3,2,1,0:T(2,128)(2,1)} %compare_select_fusion, pred[8,80,40]{1,0,2:T(8,128)(4,1)S(1)} %iota_compare_fusion.2, bf16[20,80]{1,0:T(8,128)(2,1)S(1)} %fusion.62, s32[640]{0:T(1024)S(1)} %iota_subtract_fusion), kind=kOutput, calls=%fused_computation.6 | convolution fusion | flops 1642086400 | bytes 12319360 | tf_op jit(solution)/shard_map/rqkc,ckjt->rqcjt/dot_general | solution.py:33
  93.5 13.2 %copy.55 = bf16[8,20,40,2,160]{4,3,2,1,0:T(2,128)(2,1)} copy(bf16[8,20,40,2,160]{4,1,0,3,2:T(8,128)(2,1)} %convert_bitcast_fusion) | data formatting | bytes 8192000 | tf_op jit(solution)/shard_map/convert_element_type | solution.py:33
  106.6 14.4 %reshape.266 = bf16[6400,320]{1,0:T(8,128)(2,1)} reshape(bf16[8,20,40,2,160]{4,3,2,1,0:T(2,128)(2,1)} %copy.55) | data formatting | bytes 8192000 | tf_op jit(solution)/shard_map/reshape | solution.py:81
  121.6 13.8 %broadcast_select_fusion = bf16[8,16,20,8,800]{4,3,1,2,0:T(8,128)(2,1)} fusion(pred[8,16,20,8]{3,1,2,0:T(8,128)(4,1)S(1)} %iota_compare_fusion, bf16[8,16,20,800]{3,1,0,2:T(8,128)(2,1)} %bitcast.62), kind=kLoop, calls=%fused_computation.2 | loop fusion | flops 16384000 | bytes 36884480 | tf_op jit(solution)/shard_map/jit(_where)/select_n | solution.py:86
  135.5 58.1 %select_n.102 = bf16[8,16,20,6400]{3,1,2,0:T(8,128)(2,1)} reshape(bf16[8,16,20,8,800]{4,3,1,2,0:T(8,128)(2,1)} %broadcast_select_fusion) | data formatting | bytes 65536000 | tf_op jit(solution)/shard_map/jit(_where)/select_n | solution.py:86
  193.5 28.8 %fusion.12 = f32[16,8,20,320]{3,2,0,1:T(8,128)S(1)} fusion(bf16[8,16,20,6400]{3,1,2,0:T(8,128)(2,1)} %select_n.102, bf16[6400,320]{1,0:T(8,128)(2,1)} %reshape.266), kind=kOutput, calls=%fused_computation.13 | convolution fusion | flops 10485760000 | bytes 40140800 | tf_op jit(solution)/shard_map/pfak,kn->fpan/dot_general | solution.py:89
  222.3 4.2 %copy.64 = f32[16,8,20,320]{3,1,2,0:T(8,128)} copy(f32[16,8,20,320]{3,2,0,1:T(8,128)S(1)} %fusion.12) | data formatting | bytes 6553600 | tf_op jit(solution)/shard_map/pfak,kn->fpan/transpose | solution.py:89
  226.5 4.5 %all-to-all-start.2 = ((f32[16,8,20,320]{3,1,2,0:T(8,128)}), f32[16,8,20,320]{3,1,2,0:T(8,128)}, u32[]{:S(2)}, u32[]{:S(2)}) async-start(f32[16,8,20,320]{3,1,2,0:T(8,128)} %copy.64), calls=%async_computation.2 | async-start | bytes 7864320 | tf_op jit(solution)/shard_map/all_to_all | solution.py:90
  231.2 55.2 %all-to-all-done.2 = f32[16,8,20,320]{3,1,2,0:T(8,128)} async-done(((f32[16,8,20,320]{3,1,2,0:T(8,128)}), f32[16,8,20,320]{3,1,2,0:T(8,128)}, u32[]{:S(2)}, u32[]{:S(2)}) %all-to-all-start.2) | async-done | bytes 3276832 | tf_op jit(solution)/shard_map/all_to_all | solution.py:90
  286.3 2.3 reduce_sum.89
  289.2 1.1 copy.67
  (37 shorter events, 6.8 us)
Async XLA Ops:
  14.8 19.8 %all-to-all-start = ((bf16[8,10,20,160]{3,2,1,0:T(8,128)(2,1)}), bf16[8,10,20,160]{3,2,1,0:T(8,128)(2,1)S(1)}, u32[]{:S(2)}, u32[]{:S(2)}) async-start(bf16[8,10,20,160]{3,2,1,0:T(8,128)(2,1)} %bitcast.13), calls=%async_computation | async-start | bytes 1966080 | tf_op jit(solution)/shard_map/all_to_all | solution.py:60
  19.4 102.3 %all-gather.3.cloned.1.call-start = ((), (), s32[]{:S(2)}) async-start(), calls=%async_computation.3 | async-start | bytes 5160960 | tf_op jit(solution)/shard_map/all_gather | solution.py:72
  39.1 25.3 %copy-start = (s32[16]{0:T(128)S(1)}, s32[16]{0:T(128)}, u32[]{:S(2)}) copy-start(s32[16]{0:T(128)} %param.11) | copy-start | bytes 196
  226.5 59.8 %all-to-all-start.2 = ((f32[16,8,20,320]{3,1,2,0:T(8,128)}), f32[16,8,20,320]{3,1,2,0:T(8,128)}, u32[]{:S(2)}, u32[]{:S(2)}) async-start(f32[16,8,20,320]{3,1,2,0:T(8,128)} %copy.64), calls=%async_computation.2 | async-start | bytes 7864320 | tf_op jit(solution)/shard_map/all_to_all | solution.py:90
Sparse Core Ops, SparseCore 0:
  64.2 29.4 all-gather.2

commit v3 on v2

--- a/solution.py
+++ b/solution.py
@@ -1,6 +1,10 @@
+import functools
+
 import jax
 import jax.numpy as jnp
 from jax import lax
+from jax.experimental import pallas as pl
+from jax.experimental.pallas import tpu as pltpu
 from jax.sharding import PartitionSpec as P
 
 BF16, F32 = jnp.bfloat16, jnp.float32
@@ -31,6 +35,76 @@
 
 def pick(x, spec, y):
     return jnp.einsum(spec, x, y, preferred_element_type=F32).astype(BF16)
+
+
+def grouped_kernel(scalars, lhs, rhs, c_label, out, rows, block, total, *, irreps, halves, window, c_local):
+    step = pl.program_id(0)
+    groups, n_rows, depth = lhs.shape
+    n_i, n_j, width = groups // halves, rhs.shape[1], rhs.shape[3]
+    k_starts = n_i + 2
+    bounds = k_starts + irreps
+
+    def place(h, _):
+        k = scalars[k_starts + (step ^ h)]
+        odd = k % 2
+        first = pl.multiple_of(k * c_local + odd * (c_local % 16), 16)
+        chosen = c_label[...] == h.astype(F32).astype(BF16)
+        for j in range(n_j):
+            block[j] = jnp.where(chosen, rhs[odd, j, pl.ds(first, depth), :], block[j])
+        return 0
+
+    lax.fori_loop(scalars[n_i], scalars[n_i + 1] + 1, place, 0)
+
+    spans = []
+    for g in range(groups):
+        at = bounds + (g % halves) * (irreps + 1) + (step ^ scalars[g // halves])
+        low, high = scalars[at], scalars[at + 1]
+        base = pl.multiple_of(jnp.minimum(low // 16 * 16, n_rows - window), 16)
+        rows[g * window:(g + 1) * window, :] = lhs[g, pl.ds(base, window), :]
+        spans.append((low, high, base))
+    for j in range(n_j):
+        product = jnp.dot(rows[...], block[j], preferred_element_type=F32)
+        for g, (low, high, base) in enumerate(spans):
+            piece = product[g * window:(g + 1) * window]
+            row = base + lax.broadcasted_iota(jnp.int32, piece.shape, 0)
+            own = (row >= low) & (row < high)
+            lane = (g % halves * n_j + j) * width
+            spot = (g // halves, pl.ds(base, window), slice(lane, lane + width))
+            total[spot] = jnp.where(own, piece, total[spot])
+
+    @pl.when(step == irreps - 1)
+    def _():
+        part = n_rows // out.shape[0]
+        for f in range(out.shape[0]):
+            for i in range(n_i):
+                out[f, i * part:(i + 1) * part, :] = total[i, f * part:(f + 1) * part, :]
+
+
+def grouped_product(scalars, lhs, rhs, c_label, n_fold, *, irreps, halves, window, c_local):
+    groups, n_rows, depth = lhs.shape
+    _, n_j, _, width = rhs.shape
+    n_i = groups // halves
+    out_shape = (n_fold, n_i * n_rows // n_fold, halves * n_j * width)
+    whole = lambda shape: pl.BlockSpec(shape, lambda r, s: (0,) * len(shape))
+    return pl.pallas_call(
+        functools.partial(grouped_kernel, irreps=irreps, halves=halves, window=window, c_local=c_local),
+        out_shape=jax.ShapeDtypeStruct(out_shape, F32),
+        grid_spec=pltpu.PrefetchScalarGridSpec(
+            num_scalar_prefetch=1,
+            grid=(irreps,),
+            in_specs=[whole(lhs.shape), whole(rhs.shape), whole(c_label.shape)],
+            out_specs=whole(out_shape),
+            scratch_shapes=[
+                pltpu.VMEM((groups * window, depth), BF16),
+                pltpu.VMEM((n_j, depth, width), BF16),
+                pltpu.VMEM((n_i, n_rows, halves * n_j * width), F32),
+            ],
+        ),
+        compiler_params=pltpu.CompilerParams(vmem_limit_bytes=56 * 2**20),
+        cost_estimate=pl.CostEstimate(
+            flops=2 * irreps * groups * window * depth * n_j * width, bytes_accessed=16 * 2**20, transcendentals=0
+        ),
+    )(scalars, lhs, rhs, c_label)
 
 
 def body(amplitudes, cycle_block, occ_sizes, vir_sizes, window_i, window_occ):
@@ -69,27 +143,33 @@
     short = short.reshape(a_part, omax, n_fold, c_local).transpose(2, 0, 1, 3)
     short = short.reshape(n_fold, a_part, omax * c_local)
     short = lax.all_to_all(short, "fold", split_axis=0, concat_axis=0, tiled=True)
+    short = short.reshape(n_fold * a_part, omax * c_local)
     lhs = lax.all_gather(short, "pair", axis=0)
 
     x = own_vir[:, None, None] ^ occ[None, :, None] ^ j_labels[None, None, :]
     masked = jnp.where(x[..., None] == vir, cycle_block, jnp.zeros_like(cycle_block))
-    rhs = pick(masked, "ckjb,tb->ckjt", to_place)
-    classes = jnp.arange(irreps, dtype=jnp.int32)
-    x = classes[:, None, None] == (occ[None, :, None] ^ own_vir[None, None, :])
-    chosen = jnp.where(x[:, None], to_kappa[None, :, :, None], jnp.zeros((), BF16))
-    rhs = pick(chosen, "rqkc,ckjt->rqcjt", rhs)
-    rhs = rhs.reshape(irreps * omax * c_local, j_local * vmax)
+    rhs = pick(masked, "ckjb,tb->jkct", to_place).reshape(j_local, occ_total * c_local, vmax)
+    half = c_local % 16
+    beyond = omax * c_local
+    rhs = jnp.stack([
+        jnp.pad(rhs, ((0, 0), (0, beyond + 16), (0, 0))),
+        jnp.pad(rhs, ((0, 0), (half, beyond + 16 - half), (0, 0))),
+    ])
+    c_label = jnp.tile(own_vir.astype(F32)[:, None], (omax, vmax)).astype(BF16)
 
-    a_class = vir.reshape(n_fold, halves, a_part)
-    row = i_labels[:, None, None, None] ^ a_class.transpose(1, 0, 2)[None]
-    row = row.reshape(n_pair, n_fold, a_part)
-    spread = jnp.where(
-        row[..., None, None] == classes[:, None], lhs[:, :, :, None, :], jnp.zeros((), BF16)
-    ).reshape(n_pair, n_fold, a_part, -1)
-    partial_sum = jnp.einsum("pfak,kn->fpan", spread, rhs, preferred_element_type=F32)
+    starts = jnp.concatenate([jnp.zeros((1,), jnp.int32), prefix_sums(vir_sizes)])
+    inside = starts % a_local
+    bounds = [starts // a_local * a_part + jnp.clip(inside - h * a_part, 0, a_part) for h in range(halves)]
+    k_starts = prefix_sums(occ_sizes) - occ_sizes
+    scalars = jnp.concatenate([i_labels, own_vir[:1], own_vir[-1:], k_starts] + bounds).astype(jnp.int32)
+    most = min(vmax, -(-vmax // a_local) * a_part)
+    window = min(-(-(most + 15) // 16) * 16, n_fold * a_part)
+    partial_sum = grouped_product(
+        scalars, lhs, rhs, c_label, n_fold, irreps=irreps, halves=halves, window=window, c_local=c_local
+    )
     shares = lax.all_to_all(partial_sum, "fold", split_axis=0, concat_axis=0, tiled=True)
-    total = jnp.sum(shares, axis=0).astype(BF16)
-    total = total.reshape(n_i, a_local, j_local, vmax)
+    total = jnp.sum(shares, axis=0).astype(BF16).reshape(n_i, a_part, halves, j_local, vmax)
+    total = total.transpose(0, 2, 1, 3, 4).reshape(n_i, a_local, j_local, vmax)
     spread_b = pick(total, "iajt,tb->iajb", to_place)
     x = i_labels[:, None, None] ^ own_vir[None, :, None] ^ j_labels[None, None, :]
     return jnp.where(x[..., None] == vir, spread_b, jnp.zeros_like(spread_b))

time: 299 us -> 193 us (0.65)
  local copies, waits for them, and re-layouts: 99.9 us -> 22.4 us
  matrix products: 45 us -> 7.27 us
  Pallas kernels: 0 us -> 31.8 us
  other arithmetic: 39.8 us -> 29.5 us
  waiting for transfers between devices: 69 us -> 59.1 us
    select_n x1 -> x0, local copies, waits for them, and re-layouts: 58.1 us -> none  [body(): jnp.where(row[..., None, None] == classes[:, None], lhs[:, :, :, None, :]...]
    pallas_call x0 -> x1, Pallas kernels: none -> 31.8 us  [grouped_product(): pl.pallas_call(functools.partial(grouped_kernel, irreps=irreps, halves=ha...]
    dot_general x1 -> x0, matrix products: 28.8 us -> none  [body(): jnp.einsum('pfak,kn->fpan', spread, rhs, preferred_element_type=F32)]
    reshape x2 -> x0, local copies, waits for them, and re-layouts: 14.5 us -> none  [the longest x1 14.4 us: body(): rhs = rhs.reshape(irreps * omax * c_local, j_local * vmax)]
    select_n x1 -> x0, other arithmetic: 13.8 us -> none  [body(): jnp.where(row[..., None, None] == classes[:, None], lhs[:, :, :, None, :]...]
    all_to_all x1, waiting for transfers between devices: 55.2 us -> 45.3 us  [body(): lax.all_to_all(partial_sum, 'fold', split_axis=0, concat_axis=0, tiled=True)]
    convert_element_type x1, local copies, waits for them, and re-layouts: 13.2 us -> 3.57 us  [pick(): return jnp.einsum(spec, x, y, preferred_element_type=F32).astype(BF16)]
    dot_general x4, matrix products: 16.2 us -> 7.27 us  [pick(): return jnp.einsum(spec, x, y, preferred_element_type=F32).astype(BF16)]
where the time goes in v3:
time: 193 us
  waiting for transfers between devices  59.1 us (31%)
  Pallas kernels  31.8 us (16%)
  other arithmetic  29.5 us (15%)
  local copies, waits for them, and re-layouts  22.4 us (12%)
  blocking collectives  20.8 us (11%)
  between operations  13.6 us (7%)
  starting transfers between devices  8.33 us (4%)
  matrix products  7.27 us (4%)
    all_to_all x1, waiting for transfers between devices, body(): lax.all_to_all(partial_sum, 'fold', split_axis=0, concat_axis=0, tiled=True)  45.3 us
    pallas_call x1, Pallas kernels, grouped_product(): pl.pallas_call(functools.partial(grouped_kernel, irreps=irreps, halves=ha...  31.8 us
    all_to_all x1, blocking collectives, body(): lax.all_to_all(short, 'fold', split_axis=0, concat_axis=0, tiled=True)  20.8 us
    select_n x1, other arithmetic, body(): jnp.where(x[..., None] == vir, cycle_block, jnp.zeros_like(cycle_block))  15.4 us
    all_to_all x1, waiting for transfers between devices, body(): lax.all_to_all(narrow, 'pair', split_axis=0, concat_axis=0, tiled=True)  13.8 us
    dot_general x4, matrix products, pick(): return jnp.einsum(spec, x, y, preferred_element_type=F32).astype(BF16)  7.27 us
    another operation x1, other arithmetic, body(): jnp.stack([jnp.pad(rhs, ((0, 0), (0, beyond + 16), (0, 0))), jnp.pad(rhs,...  7.03 us
    another operation x1, local copies, waits for them, and re-layouts, body(): jnp.stack([jnp.pad(rhs, ((0, 0), (0, beyond + 16), (0, 0))), jnp.pad(rhs,...  5.41 us
  transfers between devices with their start and end apart: 3, of which 2 were waited for; matrix products, arithmetic and copies ran while one was open for 20% of the time, Pallas kernels for 0%

profile of v3, /device:TPU:0, one launch (start us, length us, event | category | flops | bytes accessed | tf_op | source)
XLA Modules:
  0.0 192.8 jit_solution(14927533596587471919)
XLA Ops:
  6.5 0.8 select_reduce_fusion.3
  8.1 0.8 select_reduce_fusion.4
  9.0 0.8 select_reduce_fusion.2
  10.7 2.7 %fusion.17 = bf16[4,10,40,160]{3,2,1,0:T(8,128)(2,1)S(1)} fusion(bf16[4,10,40,640]{3,2,1,0:T(8,128)(2,1)} %param.6, s32[640]{0:T(1024)S(1)} %get-tuple-element.8, s32[4,10,40]{2,1,0:T(8,128)S(1)} %broadcast_xor_fusion.1, s32[640]{0:T(1024)S(1)} %iota_subtract_fusion), kind=kOutput, calls=%fused_computation.21 | convolution fusion | flops 330086400 | bytes 2571520 | tf_op jit(solution)/shard_map/ikac,tc->ikat/dot_general | solution.py:37
  13.7 1.1 pad_maximum_fusion.1
  14.8 4.6 %all-to-all-start = ((bf16[8,10,20,160]{3,2,1,0:T(8,128)(2,1)}), bf16[8,10,20,160]{3,2,1,0:T(8,128)(2,1)S(1)}, u32[]{:S(2)}, u32[]{:S(2)}) async-start(bf16[8,10,20,160]{3,2,1,0:T(8,128)(2,1)} %bitcast.4), calls=%async_computation | async-start | bytes 1966080 | tf_op jit(solution)/shard_map/all_to_all | solution.py:134
  20.8 13.8 %all-to-all-done = bf16[8,10,20,160]{3,2,1,0:T(8,128)(2,1)S(1)} async-done(((bf16[8,10,20,160]{3,2,1,0:T(8,128)(2,1)}), bf16[8,10,20,160]{3,2,1,0:T(8,128)(2,1)S(1)}, u32[]{:S(2)}, u32[]{:S(2)}) %all-to-all-start) | async-done | bytes 512032 | tf_op jit(solution)/shard_map/all_to_all | solution.py:134
  34.6 1.2 fusion.21
  35.8 3.3 %reshape.187 = bf16[20,20,16,40]{3,2,1,0:T(8,128)(2,1)} reshape(bf16[20,20,640]{2,1,0:T(8,128)(2,1)S(1)} %fusion.21) | data formatting | bytes 1024000 | tf_op jit(solution)/shard_map/reshape | solution.py:143
  39.1 1.9 copy.53
  41.1 1.2 reshape.188
  42.4 20.8 %all_to_all.15 = bf16[16,20,800]{2,1,0:T(8,128)(2,1)S(1)} all-to-all(bf16[16,20,800]{2,1,0:T(8,128)(2,1)S(1)} %copy.36), channel_id=1, replica_groups=mesh['pair'=8,'fold'=16] {'fold'}, dimensions={0} | all-to-all | bytes 1024000 | tf_op jit(solution)/shard_map/all_to_all | solution.py:145
  63.2 1.1 all_gather_reshape.3
  65.1 15.4 %compare_select_fusion = bf16[40,80,2,640]{3,2,1,0:T(2,128)(2,1)S(1)} fusion(bf16[40,80,2,640]{3,2,1,0:T(2,128)(2,1)} %param.7, s32[640]{0:T(1024)S(1)} %get-tuple-element.8, s32[40,80,2]{2,1,0:T(8,128)S(1)} %broadcast_xor_fusion), kind=kLoop, calls=%fused_computation | loop fusion | flops 8192000 | bytes 16412160 | tf_op jit(solution)/shard_map/jit(_where)/select_n | solution.py:150
  80.5 3.0 %convert_bitcast_fusion = bf16[2,80,40,160]{3,1,0,2:T(8,128)(2,1)S(1)} fusion(bf16[40,80,2,640]{3,2,1,0:T(2,128)(2,1)S(1)} %compare_select_fusion, s32[640]{0:T(1024)S(1)} %iota_subtract_fusion), kind=kOutput, calls=%fused_computation.9 | convolution fusion | flops 1311846400 | bytes 10242560 | tf_op jit(solution)/shard_map/ckjb,tb->jkct/dot_general | solution.py:37
  83.5 3.6 %copy.38 = bf16[2,80,40,160]{3,2,1,0:T(8,128)(2,1)} copy(bf16[2,80,40,160]{3,1,0,2:T(8,128)(2,1)S(1)} %convert_bitcast_fusion) | data formatting | bytes 4096000 | tf_op jit(solution)/shard_map/convert_element_type | solution.py:37
  87.9 1.9 concatenate.10.scalars
  89.8 5.4 %pad_bitcast_fusion.1 = (bf16[1,2,4016,160]{3,2,1,0:T(8,128)(2,1)S(1)}, bf16[1,2,4016,160]{3,2,1,0:T(8,128)(2,1)}) fusion(bf16[2,3200,160]{2,1,0:T(8,128)(2,1)} %bitcast.42), kind=kLoop, calls=%fused_computation.5 | loop fusion | bytes 7188480 | tf_op jit(solution)/shard_map/stack | solution.py:154
  95.2 7.0 %pad_maximum_fusion.rhs = bf16[2,2,4016,160]{3,2,1,0:T(8,128)(2,1)} fusion(bf16[1,2,4016,160]{3,2,1,0:T(8,128)(2,1)} %get-tuple-element.15, bf16[1,2,4016,160]{3,2,1,0:T(8,128)(2,1)S(1)} %get-tuple-element.14), kind=kLoop, calls=%fused_computation.1 | loop fusion | flops 2570240 | bytes 10280960 | tf_op jit(solution)/shard_map/stack | solution.py:154
  102.2 0.9 tile.9.c_label
  103.1 31.8 %shard_map.64 = f32[16,80,640]{2,1,0:T(8,128)} custom-call(s32[32]{0:T(128)} %concatenate.10.scalars, bf16[8,320,800]{2,1,0:T(8,128)(2,1)} %all-gather.2.cloned.1.call-done.lhs, bf16[2,2,4016,160]{3,2,1,0:T(8,128)(2,1)} %pad_maximum_fusion.rhs, bf16[800,160]{1,0:T(8,128)(2,1)} %tile.9.c_label), custom_call_target="tpu_custom_call" | custom-call | flops 3145728000 | bytes 16777216 | tf_op jit(solution)/shard_map/pallas_call | solution.py:89
  134.9 3.7 %all-to-all-start.2 = ((f32[16,80,640]{2,1,0:T(8,128)}), f32[16,80,640]{2,1,0:T(8,128)S(1)}, u32[]{:S(2)}, u32[]{:S(2)}) async-start(f32[16,80,640]{2,1,0:T(8,128)} %shard_map.64), calls=%async_computation.2 | async-start | bytes 6553600 | tf_op jit(solution)/shard_map/all_to_all | solution.py:170
  138.8 45.3 %all-to-all-done.2 = f32[16,80,640]{2,1,0:T(8,128)S(1)} async-done(((f32[16,80,640]{2,1,0:T(8,128)}), f32[16,80,640]{2,1,0:T(8,128)S(1)}, u32[]{:S(2)}, u32[]{:S(2)}) %all-to-all-start.2) | async-done | bytes 3276832 | tf_op jit(solution)/shard_map/all_to_all | solution.py:170
  184.9 1.1 copy.41
  (36 shorter events, 6.1 us)
Async XLA Ops:
  14.8 19.8 %all-to-all-start = ((bf16[8,10,20,160]{3,2,1,0:T(8,128)(2,1)}), bf16[8,10,20,160]{3,2,1,0:T(8,128)(2,1)S(1)}, u32[]{:S(2)}, u32[]{:S(2)}) async-start(bf16[8,10,20,160]{3,2,1,0:T(8,128)(2,1)} %bitcast.4), calls=%async_computation | async-start | bytes 1966080 | tf_op jit(solution)/shard_map/all_to_all | solution.py:134
  19.4 82.8 %all-gather.2.cloned.1.call-start = ((), (), s32[]{:S(2)}) async-start(), calls=%async_computation.3 | async-start | bytes 5160960 | tf_op jit(solution)/shard_map/all_gather | solution.py:147
  41.1 23.2 %copy-start = (s32[8]{0:T(128)S(1)}, s32[8]{0:T(128)}, u32[]{:S(2)}) copy-start(s32[8]{0:T(128)} %param.8) | copy-start | bytes 100
  41.1 23.2 %copy-start.1 = (s32[16]{0:T(128)S(1)}, s32[16]{0:T(128)}, u32[]{:S(2)}) copy-start(s32[16]{0:T(128)} %param.11) | copy-start | bytes 196
  134.9 49.2 %all-to-all-start.2 = ((f32[16,80,640]{2,1,0:T(8,128)}), f32[16,80,640]{2,1,0:T(8,128)S(1)}, u32[]{:S(2)}, u32[]{:S(2)}) async-start(f32[16,80,640]{2,1,0:T(8,128)} %shard_map.64), calls=%async_computation.2 | async-start | bytes 6553600 | tf_op jit(solution)/shard_map/all_to_all | solution.py:170
Sparse Core Ops, SparseCore 0:
  64.4 29.4 all-gather.1

commit v4 on v2

v4 whole, which is shorter than its diff:
```python
import functools
import math

import jax
import jax.numpy as jnp
from jax import lax
from jax.experimental import pallas as pl
from jax.experimental.pallas import tpu as pltpu
from jax.sharding import PartitionSpec as P

BF16, F32 = jnp.bfloat16, jnp.float32


def irrep_labels(sizes, count):
    positions = jnp.arange(count, dtype=jnp.int32)
    starts = [jnp.int32(0)]
    for g in range(sizes.shape[0]):
        starts.append(starts[-1] + sizes[g])
    labels, opened = jnp.zeros_like(positions), jnp.zeros_like(positions)
    for g in range(1, sizes.shape[0] + 1):
        after = positions >= starts[g]
        labels = jnp.where(after, g, labels)
        opened = jnp.where(after, starts[g], opened)
    return labels, positions - opened, jnp.stack(starts)


def label_lookup(orbitals, labels, count):
    matches = orbitals[:, None] == jnp.arange(count, dtype=jnp.int32)[None, :]
    return jnp.sum(jnp.where(matches, labels[None, :], 0), axis=1)


def one_hot_rows(places, width):
    return (jnp.arange(width, dtype=jnp.int32)[:, None] == places[None, :]).astype(BF16)


def pick(x, spec, y):
    return jnp.einsum(spec, x, y, preferred_element_type=F32).astype(BF16)


def block_kernel(scalars, cycle, c_label, code, out, chosen, picks, *, n_i, irreps, width):
    step = pl.program_id(0)
    n_j = cycle.shape[0]
    depth, vir_total = c_label.shape[0], cycle.shape[2]
    lane = lax.broadcasted_iota(jnp.int32, (vir_total, n_j * width), 1)
    for j in range(n_j):
        wanted = (step ^ scalars[n_i + 2 + irreps + j]) * width + lane - j * width
        own = (lane >= j * width) & (lane < (j + 1) * width) & (code[...] == wanted)
        picks[j * vir_total:(j + 1) * vir_total, :] = own.astype(F32).astype(BF16)

    def place(h, _):
        first = pl.multiple_of(scalars[n_i + 2 + (step ^ h)], 16)
        label = h.astype(F32).astype(BF16)
        for j in range(n_j):
            for at in range(0, vir_total, c_label.shape[1]):
                lanes = slice(at, at + c_label.shape[1])
                spot = slice(j * vir_total + at, j * vir_total + at + c_label.shape[1])
                chosen[:, spot] = jnp.where(
                    c_label[...] == label, cycle[j, pl.ds(first, depth), lanes], chosen[:, spot]
                )
        return 0

    lax.fori_loop(scalars[n_i], scalars[n_i + 1] + 1, place, 0)
    out[0] = jnp.dot(chosen[...], picks[...], preferred_element_type=F32).astype(BF16)


def class_blocks(scalars, cycle, c_label, code, *, n_i, irreps, width):
    n_j, _, vir_total = cycle.shape
    depth = c_label.shape[0]
    return pl.pallas_call(
        functools.partial(block_kernel, n_i=n_i, irreps=irreps, width=width),
        out_shape=jax.ShapeDtypeStruct((irreps, depth, n_j * width), BF16),
        grid_spec=pltpu.PrefetchScalarGridSpec(
            num_scalar_prefetch=1,
            grid=(irreps,),
            in_specs=[whole(cycle.shape), whole(c_label.shape), whole(code.shape)],
            out_specs=pl.BlockSpec((1, depth, n_j * width), lambda r, s: (r, 0, 0)),
            scratch_shapes=[
                pltpu.VMEM((depth, n_j * vir_total), BF16),
                pltpu.VMEM((n_j * vir_total, n_j * width), BF16),
            ],
        ),
        compiler_params=pltpu.CompilerParams(vmem_limit_bytes=48 * 2**20),
        cost_estimate=pl.CostEstimate(
            flops=2 * irreps * depth * n_j * vir_total * n_j * width, bytes_accessed=14 * 2**20, transcendentals=0
        ),
    )(scalars, cycle, c_label, code)


def grouped_kernel(scalars, lhs, block, first, second, rows, total, *, bounds, irreps, halves, window, side):
    step = pl.program_id(0)
    groups, n_rows, _ = lhs.shape
    n_i, width = groups // halves, block.shape[2]
    spans = []
    for g in range(groups):
        at = bounds + (g % halves) * (irreps + 1) + (step ^ scalars[g // halves])
        low, high = scalars[at], scalars[at + 1]
        base = pl.multiple_of(jnp.minimum(low // 16 * 16, n_rows - window), 16)
        rows[g * window:(g + 1) * window, :] = lhs[g, pl.ds(base, window), :]
        spans.append((low, high, base))
    product = jnp.dot(rows[...], block[0], preferred_element_type=F32)
    for g, (low, high, base) in enumerate(spans):
        piece = product[g * window:(g + 1) * window]
        row = base + lax.broadcasted_iota(jnp.int32, piece.shape, 0)
        spot = (g, pl.ds(base, window), slice(None))
        total[spot] = jnp.where((row >= low) & (row < high), piece, total[spot])

    @pl.when(step == irreps - 1)
    def _():
        n_fold = side[0] * side[1]
        part = n_rows // n_fold
        z, x = scalars[bounds - 2], scalars[bounds - 1]
        for f in range(n_fold):
            dz = lax.rem(f // side[1] - z + side[0], side[0])
            dx = lax.rem(f % side[1] - x + side[1], side[1])
            for g in range(groups):
                i, lane = g // halves, g % halves * width
                at = (i % (n_i // 2)) * part
                out, spot = (first, (dz, dx)) if i < n_i // 2 else (second, (dx, dz))
                out[spot + (slice(at, at + part), slice(lane, lane + width))] = total[g, f * part:(f + 1) * part, :]


def whole(shape):
    return pl.BlockSpec(shape, lambda r, s: (0,) * len(shape))


def grouped_product(scalars, lhs, block, *, bounds, irreps, halves, window, side):
    groups, n_rows, depth = lhs.shape
    width = block.shape[2]
    n_i = groups // halves
    tail = (n_i // 2 * n_rows // (side[0] * side[1]), halves * width)
    shapes = [(side[0], side[1]) + tail, (side[1], side[0]) + tail]
    return pl.pallas_call(
        functools.partial(
            grouped_kernel, bounds=bounds, irreps=irreps, halves=halves, window=window, side=side
        ),
        out_shape=[jax.ShapeDtypeStruct(shape, F32) for shape in shapes],
        grid_spec=pltpu.PrefetchScalarGridSpec(
            num_scalar_prefetch=1,
            grid=(irreps,),
            in_specs=[whole(lhs.shape), pl.BlockSpec((1, depth, width), lambda r, s: (r, 0, 0))],
            out_specs=[whole(shape) for shape in shapes],
            scratch_shapes=[pltpu.VMEM((groups * window, depth), BF16), pltpu.VMEM((groups, n_rows, width), F32)],
        ),
        compiler_params=pltpu.CompilerParams(vmem_limit_bytes=48 * 2**20),
        cost_estimate=pl.CostEstimate(
            flops=2 * irreps * groups * window * depth * width, bytes_accessed=13 * 2**20, transcendentals=0
        ),
    )(scalars, lhs, block)


def ring(side, along, step):
    pairs = []
    for z in range(side[0]):
        for x in range(side[1]):
            to = ((z + step) % side[0], x) if along == 0 else (z, (x + step) % side[1])
            pairs.append((z * side[1] + x, to[0] * side[1] + to[1]))
    return pairs


def ring_sums(parts, side, alongs):
    def send(v, along, step):
        return lax.ppermute(v, "fold", ring(side, along, step))

    halfway = [p.shape[1] // 2 if p.ndim > 3 else -(-p.shape[1] // 16) * 8 for p in parts]
    up = [send(p[2, :h], a, 1) for p, h, a in zip(parts, halfway, alongs)]
    down = [send(p[2, h:], a, -1) for p, h, a in zip(parts, halfway, alongs)]
    sums = []
    for p, u, d, h, a in zip(parts, up, down, halfway, alongs):
        right = send(jnp.concatenate([p[1, :h] + u, p[1, h:]]), a, 1)
        left = send(jnp.concatenate([p[3, :h], p[3, h:] + d]), a, -1)
        sums.append((p[0], right, left))
    return [p + r + l for p, r, l in sums]


def body(amplitudes, cycle_block, occ_sizes, vir_sizes, window_i, window_occ):
    irreps = occ_sizes.shape[0]
    n_fold, n_pair = lax.axis_size("fold"), lax.axis_size("pair")
    fold, pair = lax.axis_index("fold"), lax.axis_index("pair")
    c_local, occ_total, j_local, vir_total = cycle_block.shape
    n_i, k_local, a_local, _ = amplitudes.shape
    vmax, omax = vir_total // 4, occ_total // 4
    halves = n_pair // n_i
    a_part = a_local // halves

    occ, _, occ_starts = irrep_labels(occ_sizes, occ_total)
    vir, vir_place, starts = irrep_labels(vir_sizes, vir_total)
    to_place = one_hot_rows(vir_place, vmax)
    kappas = omax + 2 - omax % 2
    k_from = jnp.minimum(occ_starts[:irreps] // 2 * 2, occ_total - kappas)
    kappa = jnp.arange(occ_total, dtype=jnp.int32)
    for g in range(irreps):
        kappa = kappa - jnp.where(occ == g, k_from[g], 0)
    to_kappa = one_hot_rows(kappa, kappas)
    own_vir = lax.dynamic_slice_in_dim(vir, fold * c_local, c_local)
    k_own = lax.dynamic_slice_in_dim(occ, pair * k_local, k_local)
    i_labels = label_lookup(window_i, occ, occ_total)
    j_labels = label_lookup(lax.dynamic_slice_in_dim(window_occ, pair * j_local, j_local), occ, occ_total)

    x = i_labels[:, None, None] ^ k_own[None, :, None] ^ own_vir[None, None, :]
    masked = jnp.where(x[..., None] == vir, amplitudes, jnp.zeros_like(amplitudes))
    narrow = pick(masked, "ikac,tc->ikat", to_place)
    narrow = narrow.reshape(n_i, k_local, halves, a_part, vmax).transpose(0, 2, 1, 3, 4)
    narrow = narrow.reshape(n_pair, k_local, a_part, vmax)
    narrow = lax.all_to_all(narrow, "pair", split_axis=0, concat_axis=0, tiled=True)
    narrow = narrow.reshape(occ_total, a_part, vmax)

    i_mine = lax.dynamic_index_in_dim(i_labels, pair // halves, keepdims=False)
    a_mine = lax.dynamic_slice_in_dim(vir, fold * a_local + (pair % halves) * a_part, a_part)
    wide = pick(narrow, "kat,tc->akc", to_place)
    x = i_mine ^ occ[None, :, None] ^ a_mine[:, None, None] ^ vir[None, None, :]
    wide = jnp.where(x == 0, wide, jnp.zeros_like(wide))
    short = pick(to_kappa, "qk,akc->aqc", wide)
    short = short.reshape(a_part, kappas, n_fold, c_local).transpose(2, 0, 1, 3)
    short = short.reshape(n_fold, a_part, kappas * c_local)
    short = lax.all_to_all(short, "fold", split_axis=0, concat_axis=0, tiled=True)
    short = short.reshape(n_fold * a_part, kappas * c_local)
    lhs = lax.all_gather(short, "pair", axis=0)

    side = (4, 4) if n_fold == 16 else (n_fold, 1)
    inside = starts % a_local
    bounds = [starts // a_local * a_part + jnp.clip(inside - h * a_part, 0, a_part) for h in range(halves)]
    scalars = jnp.concatenate(
        [i_labels, own_vir[:1], own_vir[-1:], k_from * c_local, j_labels]
        + [jnp.stack([fold // side[1], fold % side[1]])] + bounds
    ).astype(jnp.int32)
    cycle = cycle_block.transpose(2, 1, 0, 3).reshape(j_local, occ_total * c_local, vir_total)
    lanes = math.gcd(vir_total, 128)
    c_label = jnp.tile(own_vir.astype(F32)[:, None], (kappas, lanes)).astype(BF16)
    code = jnp.broadcast_to((vir * vmax + vir_place)[:, None], (vir_total, j_local * vmax))
    blocks = class_blocks(scalars, cycle, c_label, code, n_i=n_i, irreps=irreps, width=vmax)

    most = min(vmax, -(-vmax // a_local) * a_part)
    window = min(-(-(most + 15) // 16) * 16, n_fold * a_part)
    first, second = grouped_product(
        scalars, lhs, blocks, bounds=n_i + irreps + j_local + 4, irreps=irreps, halves=halves, window=window, side=side
    )
    if side == (4, 4):
        first, second = ring_sums([first, second], side, (0, 1))
        first, second = ring_sums([first, second], side, (1, 0))
    else:
        order = lax.rem(jnp.arange(n_fold) - fold + n_fold, n_fold)
        both = jnp.concatenate([first[:, 0][order], second[0][order]], axis=1)
        shares = jnp.sum(lax.all_to_all(both, "fold", split_axis=0, concat_axis=0, tiled=True), axis=0)
        first, second = jnp.split(shares, 2)
    total = jnp.concatenate([first, second]).astype(BF16).reshape(n_i, a_part, halves, j_local, vmax)
    total = total.transpose(0, 2, 1, 3, 4).reshape(n_i, a_local, j_local, vmax)
    spread_b = pick(total, "iajt,tb->iajb", to_place)
    x = i_labels[:, None, None] ^ own_vir[None, :, None] ^ j_labels[None, None, :]
    return jnp.where(x[..., None] == vir, spread_b, jnp.zeros_like(spread_b))


def solution(mesh):
    placed = (P(None, "pair", "fold", None), P("fold", None, "pair", None), P(), P(), P(), P())
    return jax.shard_map(
        body, mesh=mesh, in_specs=placed, out_specs=P(None, "fold", "pair", None), check_vma=False
    )
```

time: 299 us -> 186 us (0.62)
  local copies, waits for them, and re-layouts: 99.9 us -> 27.8 us
  waiting for transfers between devices: 69 us -> 26 us
  matrix products: 45 us -> 4.26 us
  Pallas kernels: 0 us -> 36 us
  other arithmetic: 39.8 us -> 10.6 us
  starting transfers between devices: 9.1 us -> 35.2 us
  between operations: 13.6 us -> 23.7 us
    select_n x1 -> x0, local copies, waits for them, and re-layouts: 58.1 us -> none  [body(): jnp.where(row[..., None, None] == classes[:, None], lhs[:, :, :, None, :]...]
    all_to_all x1 -> x0, waiting for transfers between devices: 55.2 us -> none  [body(): lax.all_to_all(partial_sum, 'fold', split_axis=0, concat_axis=0, tiled=True)]
    pallas_call x0 -> x2, Pallas kernels: none -> 36 us  [the longest x1 24 us: class_blocks(): pl.pallas_call(functools.partial(block_kernel, n_i=n_i, irreps=irreps, wi...]
    ppermute x0 -> x16, starting transfers between devices: none -> 30.7 us  [send(): return lax.ppermute(v, 'fold', ring(side, along, step))]
    select_n x2 -> x1, other arithmetic: 30 us -> 0.64 us  [irrep_labels(): labels = jnp.where(after, g, labels)]
    dot_general x1 -> x0, matrix products: 28.8 us -> none  [body(): jnp.einsum('pfak,kn->fpan', spread, rhs, preferred_element_type=F32)]
    reshape x6 -> x4, local copies, waits for them, and re-layouts: 21 us -> 6.99 us  [the longest x2 5.62 us: body(): short = short.reshape(a_part, kappas, n_fold, c_local).transpose(2, 0, 1, 3)]
    convert_element_type x3, local copies, waits for them, and re-layouts: 13.3 us -> 0.37 us  [the longest x2 0.28 us: body(): jnp.concatenate([first, second]).astype(BF16)]
  transfers between devices with their start and end apart: 3 -> 18, of which waited for: 2 -> 8; matrix products, arithmetic and copies ran while one was open for 20% -> 8% of each run, Pallas kernels for 0% -> 13%
where the time goes in v4:
time: 186 us; the launch traced here: 184 us
  Pallas kernels  36 us (19%)
  starting transfers between devices  35.2 us (19%)
  local copies, waits for them, and re-layouts  27.8 us (15%)
  waiting for transfers between devices  26 us (14%)
  between operations  23.7 us (13%)
  blocking collectives  20.8 us (11%)
  other arithmetic  10.6 us (6%)
  matrix products  4.26 us (2%)
    ppermute x16, starting transfers between devices, send(): return lax.ppermute(v, 'fold', ring(side, along, step))  30.7 us
    pallas_call x1, Pallas kernels, class_blocks(): pl.pallas_call(functools.partial(block_kernel, n_i=n_i, irreps=irreps, wi...  24 us
    all_to_all x1, blocking collectives, body(): lax.all_to_all(short, 'fold', split_axis=0, concat_axis=0, tiled=True)  20.8 us
    all_to_all x1, waiting for transfers between devices, body(): lax.all_to_all(narrow, 'pair', split_axis=0, concat_axis=0, tiled=True)  13.8 us
    ppermute x16, waiting for transfers between devices, send(): return lax.ppermute(v, 'fold', ring(side, along, step))  12.1 us
    pallas_call x1, Pallas kernels, grouped_product(): pl.pallas_call(functools.partial(grouped_kernel, bounds=bounds, irreps=ir...  12 us
    transpose x1, local copies, waits for them, and re-layouts, body(): cycle_block.transpose(2, 1, 0, 3)  9.43 us
    reshape x2, local copies, waits for them, and re-layouts, body(): short = short.reshape(a_part, kappas, n_fold, c_local).transpose(2, 0, 1, 3)  5.62 us
  transfers between devices with their start and end apart: 18, of which 8 were waited for; matrix products, arithmetic and copies ran while one was open for 8% of the time, Pallas kernels for 13%

profile of v4, /device:TPU:0, one launch (start us, length us, event | category | flops | bytes accessed | tf_op | source)
XLA Modules:
  0.0 184.3 jit_solution(17211865979518720879)
XLA Ops:
  6.5 1.6 fusion.69
  14.5 1.6 fusion.67
  22.4 5.6 %fusion.59 = (s32[80]{0:T(128)S(1)}, s32[80]{0:T(128)S(1)}) fusion(s32[]{:T(128)} %bitcast.45, s32[]{:T(128)} %bitcast.44, s32[]{:T(128)} %bitcast.43, s32[]{:T(128)} %bitcast.42, s32[]{:T(128)} %bitcast.41, s32[]{:T(128)} %bitcast.40, s32[]{:T(128)} %bitcast.39, s32[]{:T(128)} %bitcast.38, s32[]{:T(128)} %bitcast, s32[]{:T(128)} %add.140, s32[]{:T(128)} %add.141, ...), kind=kLoop, calls=%fused_computation.131 | loop fusion | flops 3200 | bytes 704 | tf_op jit(solution)/shard_map/sub | solution.py:192
  29.1 2.7 %fusion.13 = bf16[4,10,40,160]{3,2,1,0:T(8,128)(2,1)S(1)} fusion(bf16[4,10,40,640]{3,2,1,0:T(8,128)(2,1)} %param.6, s32[640]{0:T(1024)S(1)} %select_select_fusion, s32[4,10,40]{2,1,0:T(8,128)S(1)} %broadcast_xor_fusion, s32[640]{0:T(1024)S(1)} %get-tuple-element.66), kind=kOutput, calls=%fused_computation.14 | convolution fusion | flops 330086400 | bytes 2571520 | tf_op jit(solution)/shard_map/ikac,tc->ikat/dot_general | solution.py:37
  33.2 4.6 %all-to-all-start = ((bf16[8,10,20,160]{3,2,1,0:T(8,128)(2,1)}), bf16[8,10,20,160]{3,2,1,0:T(8,128)(2,1)S(1)}, u32[]{:S(2)}, u32[]{:S(2)}) async-start(bf16[8,10,20,160]{3,2,1,0:T(8,128)(2,1)} %bitcast.35), calls=%async_computation | async-start | bytes 1966080 | tf_op jit(solution)/shard_map/all_to_all | solution.py:204
  39.2 13.8 %all-to-all-done = bf16[8,10,20,160]{3,2,1,0:T(8,128)(2,1)S(1)} async-done(((bf16[8,10,20,160]{3,2,1,0:T(8,128)(2,1)}), bf16[8,10,20,160]{3,2,1,0:T(8,128)(2,1)S(1)}, u32[]{:S(2)}, u32[]{:S(2)}) %all-to-all-start) | async-done | bytes 512032 | tf_op jit(solution)/shard_map/all_to_all | solution.py:204
  54.2 3.6 %reshape.332 = bf16[20,22,16,40]{3,2,1,0:T(8,128)(2,1)} reshape(bf16[20,22,640]{2,1,0:T(8,128)(2,1)S(1)} %fusion.17) | data formatting | bytes 1126400 | tf_op jit(solution)/shard_map/reshape | solution.py:213
  57.9 2.0 %copy.45 = bf16[20,22,16,40]{3,1,2,0:T(8,128)(2,1)S(1)} copy(bf16[20,22,16,40]{3,2,1,0:T(8,128)(2,1)} %reshape.332) | data formatting | bytes 1126400 | tf_op jit(solution)/shard_map/reshape | solution.py:213
  61.3 20.8 %all_to_all.10 = bf16[16,20,880]{2,1,0:T(8,128)(2,1)S(1)} all-to-all(bf16[16,20,880]{2,1,0:T(8,128)(2,1)S(1)} %copy.33), channel_id=1, replica_groups=mesh['pair'=8,'fold'=16] {'fold'}, dimensions={0} | all-to-all | bytes 1126400 | tf_op jit(solution)/shard_map/all_to_all | solution.py:215
  83.2 9.4 %copy.34 = bf16[2,80,40,640]{3,2,1,0:T(8,128)(2,1)} copy(bf16[2,80,40,640]{3,0,1,2:T(2,128)(2,1)} %bitcast.156) | data formatting | bytes 16384000 | tf_op jit(solution)/shard_map/transpose | solution.py:226
  96.1 24.0 %shard_map.64.block = bf16[8,880,320]{2,1,0:T(8,128)(2,1)} custom-call(s32[36]{0:T(128)S(1)} %concatenate.34.scalars, bf16[2,3200,640]{2,1,0:T(8,128)(2,1)} %bitcast.157, bf16[880,128]{1,0:T(8,128)(2,1)S(1)} %tile.9.c_label, s32[640,320]{1,0:T(8,128)S(1)} %broadcast_in_dim.185.code), custom_call_target="tpu_custom_call" | custom-call | flops 5767168000 | bytes 14680064 | tf_op jit(solution)/shard_map/pallas_call | solution.py:69
  120.2 12.0 %shard_map.65 = (f32[4,4,40,640]{3,2,1,0:T(8,128)S(1)}, f32[4,4,40,640]{3,2,1,0:T(8,128)S(1)}) custom-call(s32[36]{0:T(128)S(1)} %concatenate.34.scalars, bf16[8,320,880]{2,1,0:T(8,128)(2,1)} %all-gather.2.cloned.1.call-done.lhs, bf16[8,880,320]{2,1,0:T(8,128)(2,1)} %shard_map.64.block), custom_call_target="tpu_custom_call" | custom-call | flops 3460300800 | bytes 13631488 | tf_op jit(solution)/shard_map/pallas_call | solution.py:132
  132.5 8.1 %collective-permute-start.2 = (f32[2,40,640]{2,1,0:T(8,128)S(1)}, f32[2,40,640]{2,1,0:T(8,128)S(1)}, u32[]{:S(2)}, u32[]{:S(2)}) collective-permute-start(f32[2,40,640]{2,1,0:T(8,128)S(1)} %get-tuple-element.20), channel_id=1, source_target_pairs={{0,12},{1,13},{2,14},{3,15},{4,0},{5,1},{6,2},{7,3},{8,4},{9,5},{1... | collective-permute-start | bytes 614408 | tf_op jit(solution)/shard_map/ppermute | solution.py:162
  142.8 1.5 collective-permute-done
  145.9 2.0 %collective-permute-start.3 = (f32[4,40,640]{2,1,0:T(8,128)S(1)}, f32[4,40,640]{2,1,0:T(8,128)S(1)}, u32[]{:S(2)}, u32[]{:S(2)}) collective-permute-start(f32[4,40,640]{2,1,0:T(8,128)S(1)} %pad_maximum_fusion.2), channel_id=1, source_target_pairs={{0,12},{1,13},{2,14},{3,15},{4,0},{5,1},{6,2},{7,3},{8,4},{9,5},{1... | collective-permute-start | bytes 1228808 | tf_op jit(solution)/shard_map/ppermute | solution.py:162
  150.2 1.9 %collective-permute-start.11 = (f32[4,40,640]{2,1,0:T(8,128)S(1)}, f32[4,40,640]{2,1,0:T(8,128)S(1)}, u32[]{:S(2)}, u32[]{:S(2)}) collective-permute-start(f32[4,40,640]{2,1,0:T(8,128)S(1)} %pad_maximum_fusion.4), channel_id=1, source_target_pairs={{0,3},{1,0},{2,1},{3,2},{4,7},{5,4},{6,5},{7,6},{8,11},{9,8},{10,9... | collective-permute-start | bytes 1228808 | tf_op jit(solution)/shard_map/ppermute | solution.py:162
  152.1 2.3 %collective-permute-done.1 = f32[4,40,640]{2,1,0:T(8,128)S(1)} collective-permute-done((f32[4,40,640]{2,1,0:T(8,128)S(1)}, f32[4,40,640]{2,1,0:T(8,128)S(1)}, u32[]{:S(2)}, u32[]{:S(2)}) %collective-permute-start.1) | collective-permute-done | bytes 409632 | tf_op jit(solution)/shard_map/ppermute | solution.py:162
  154.5 2.2 %collective-permute-start.6 = (f32[16,640]{1,0:T(8,128)S(1)}, f32[16,640]{1,0:T(8,128)S(1)}, u32[]{:S(2)}, u32[]{:S(2)}) collective-permute-start(f32[16,640]{1,0:T(8,128)S(1)} %get-tuple-element.34), channel_id=1, source_target_pairs={{0,3},{1,0},{2,1},{3,2},{4,7},{5,4},{6,5},{7,6},{8,11},{9,8},{10,9... | collective-permute-start | bytes 122888 | tf_op jit(solution)/shard_map/ppermute | solution.py:162
  160.6 2.2 %collective-permute-start.14 = (f32[16,640]{1,0:T(8,128)S(1)}, f32[16,640]{1,0:T(8,128)S(1)}, u32[]{:S(2)}, u32[]{:S(2)}) collective-permute-start(f32[16,640]{1,0:T(8,128)S(1)} %get-tuple-element.38), channel_id=1, source_target_pairs={{0,12},{1,13},{2,14},{3,15},{4,0},{5,1},{6,2},{7,3},{8,4},{9,5},{1... | collective-permute-start | bytes 122888 | tf_op jit(solution)/shard_map/ppermute | solution.py:162
  162.8 2.4 %collective-permute-start.7 = (f32[40,640]{1,0:T(8,128)S(1)}, f32[40,640]{1,0:T(8,128)S(1)}, u32[]{:S(2)}, u32[]{:S(2)}) collective-permute-start(f32[40,640]{1,0:T(8,128)S(1)} %pad_maximum_fusion.6), channel_id=1, source_target_pairs={{0,3},{1,0},{2,1},{3,2},{4,7},{5,4},{6,5},{7,6},{8,11},{9,8},{10,9... | collective-permute-start | bytes 307208 | tf_op jit(solution)/shard_map/ppermute | solution.py:162
  165.2 2.9 %collective-permute-start.15 = (f32[40,640]{1,0:T(8,128)S(1)}, f32[40,640]{1,0:T(8,128)S(1)}, u32[]{:S(2)}, u32[]{:S(2)}) collective-permute-start(f32[40,640]{1,0:T(8,128)S(1)} %pad_maximum_fusion.8), channel_id=1, source_target_pairs={{0,12},{1,13},{2,14},{3,15},{4,0},{5,1},{6,2},{7,3},{8,4},{9,5},{1... | collective-permute-start | bytes 307208 | tf_op jit(solution)/shard_map/ppermute | solution.py:162
  168.1 1.6 collective-permute-start.5
  169.9 4.2 %collective-permute-done.5 = f32[40,640]{1,0:T(8,128)S(1)} collective-permute-done((f32[40,640]{1,0:T(8,128)S(1)}, f32[40,640]{1,0:T(8,128)S(1)}, u32[]{:S(2)}, u32[]{:S(2)}) %collective-permute-start.5) | collective-permute-done | bytes 102432 | tf_op jit(solution)/shard_map/ppermute | solution.py:162
  174.1 1.6 collective-permute-done.13
  (87 shorter events, 26.0 us)
Async XLA Ops:
  33.2 19.8 %all-to-all-start = ((bf16[8,10,20,160]{3,2,1,0:T(8,128)(2,1)}), bf16[8,10,20,160]{3,2,1,0:T(8,128)(2,1)S(1)}, u32[]{:S(2)}, u32[]{:S(2)}) async-start(bf16[8,10,20,160]{3,2,1,0:T(8,128)(2,1)} %bitcast.35), calls=%async_computation | async-start | bytes 1966080 | tf_op jit(solution)/shard_map/all_to_all | solution.py:204
  37.8 82.4 %all-gather.2.cloned.1.call-start = ((), (), s32[]{:S(2)}) async-start(), calls=%async_computation.2 | async-start | bytes 5160960 | tf_op jit(solution)/shard_map/all_gather | solution.py:217
  83.2 9.4 %copy-start = (s32[16]{0:T(128)S(1)}, s32[16]{0:T(128)}, u32[]{:S(2)}) copy-start(s32[16]{0:T(128)} %param.11) | copy-start | bytes 196
  132.2 12.0 %collective-permute-start = (f32[2,40,640]{2,1,0:T(8,128)S(1)}, f32[2,40,640]{2,1,0:T(8,128)S(1)}, u32[]{:S(2)}, u32[]{:S(2)}) collective-permute-start(f32[2,40,640]{2,1,0:T(8,128)S(1)} %get-tuple-element.19), channel_id=1, source_target_pairs={{0,4},{1,5},{2,6},{3,7},{4,8},{5,9},{6,10},{7,11},{8,12},{9,13},{1... | collective-permute-start | bytes 614408 | tf_op jit(solution)/shard_map/ppermute | solution.py:162
  132.5 11.8 %collective-permute-start.2 = (f32[2,40,640]{2,1,0:T(8,128)S(1)}, f32[2,40,640]{2,1,0:T(8,128)S(1)}, u32[]{:S(2)}, u32[]{:S(2)}) collective-permute-start(f32[2,40,640]{2,1,0:T(8,128)S(1)} %get-tuple-element.20), channel_id=1, source_target_pairs={{0,12},{1,13},{2,14},{3,15},{4,0},{5,1},{6,2},{7,3},{8,4},{9,5},{1... | collective-permute-start | bytes 614408 | tf_op jit(solution)/shard_map/ppermute | solution.py:162
  140.7 7.2 %collective-permute-start.10 = (f32[2,40,640]{2,1,0:T(8,128)S(1)}, f32[2,40,640]{2,1,0:T(8,128)S(1)}, u32[]{:S(2)}, u32[]{:S(2)}) collective-permute-start(f32[2,40,640]{2,1,0:T(8,128)S(1)} %get-tuple-element.26), channel_id=1, source_target_pairs={{0,3},{1,0},{2,1},{3,2},{4,7},{5,4},{6,5},{7,6},{8,11},{9,8},{10,9... | collective-permute-start | bytes 614408 | tf_op jit(solution)/shard_map/ppermute | solution.py:162
  141.7 7.0 %collective-permute-start.8 = (f32[2,40,640]{2,1,0:T(8,128)S(1)}, f32[2,40,640]{2,1,0:T(8,128)S(1)}, u32[]{:S(2)}, u32[]{:S(2)}) collective-permute-start(f32[2,40,640]{2,1,0:T(8,128)S(1)} %get-tuple-element.25), channel_id=1, source_target_pairs={{0,1},{1,2},{2,3},{3,0},{4,5},{5,6},{6,7},{7,4},{8,9},{9,10},{10,1... | collective-permute-start | bytes 614408 | tf_op jit(solution)/shard_map/ppermute | solution.py:162
  144.4 10.1 %collective-permute-start.1 = (f32[4,40,640]{2,1,0:T(8,128)S(1)}, f32[4,40,640]{2,1,0:T(8,128)S(1)}, u32[]{:S(2)}, u32[]{:S(2)}) collective-permute-start(f32[4,40,640]{2,1,0:T(8,128)S(1)} %pad_maximum_fusion.1), channel_id=1, source_target_pairs={{0,4},{1,5},{2,6},{3,7},{4,8},{5,9},{6,10},{7,11},{8,12},{9,13},{1... | collective-permute-start | bytes 1228808 | tf_op jit(solution)/shard_map/ppermute | solution.py:162
  145.9 8.6 %collective-permute-start.3 = (f32[4,40,640]{2,1,0:T(8,128)S(1)}, f32[4,40,640]{2,1,0:T(8,128)S(1)}, u32[]{:S(2)}, u32[]{:S(2)}) collective-permute-start(f32[4,40,640]{2,1,0:T(8,128)S(1)} %pad_maximum_fusion.2), channel_id=1, source_target_pairs={{0,12},{1,13},{2,14},{3,15},{4,0},{5,1},{6,2},{7,3},{8,4},{9,5},{1... | collective-permute-start | bytes 1228808 | tf_op jit(solution)/shard_map/ppermute | solution.py:162
  148.7 9.4 %collective-permute-start.9 = (f32[4,40,640]{2,1,0:T(8,128)S(1)}, f32[4,40,640]{2,1,0:T(8,128)S(1)}, u32[]{:S(2)}, u32[]{:S(2)}) collective-permute-start(f32[4,40,640]{2,1,0:T(8,128)S(1)} %pad_maximum_fusion.3), channel_id=1, source_target_pairs={{0,1},{1,2},{2,3},{3,0},{4,5},{5,6},{6,7},{7,4},{8,9},{9,10},{10,1... | collective-permute-start | bytes 1228808 | tf_op jit(solution)/shard_map/ppermute | solution.py:162
  150.2 8.2 %collective-permute-start.11 = (f32[4,40,640]{2,1,0:T(8,128)S(1)}, f32[4,40,640]{2,1,0:T(8,128)S(1)}, u32[]{:S(2)}, u32[]{:S(2)}) collective-permute-start(f32[4,40,640]{2,1,0:T(8,128)S(1)} %pad_maximum_fusion.4), channel_id=1, source_target_pairs={{0,3},{1,0},{2,1},{3,2},{4,7},{5,4},{6,5},{7,6},{8,11},{9,8},{10,9... | collective-permute-start | bytes 1228808 | tf_op jit(solution)/shard_map/ppermute | solution.py:162
  154.5 8.3 %collective-permute-start.6 = (f32[16,640]{1,0:T(8,128)S(1)}, f32[16,640]{1,0:T(8,128)S(1)}, u32[]{:S(2)}, u32[]{:S(2)}) collective-permute-start(f32[16,640]{1,0:T(8,128)S(1)} %get-tuple-element.34), channel_id=1, source_target_pairs={{0,3},{1,0},{2,1},{3,2},{4,7},{5,4},{6,5},{7,6},{8,11},{9,8},{10,9... | collective-permute-start | bytes 122888 | tf_op jit(solution)/shard_map/ppermute | solution.py:162
  158.6 9.5 %collective-permute-start.4 = (f32[24,640]{1,0:T(8,128)S(1)}, f32[24,640]{1,0:T(8,128)S(1)}, u32[]{:S(2)}, u32[]{:S(2)}) collective-permute-start(f32[24,640]{1,0:T(8,128)S(1)} %get-tuple-element.31), channel_id=1, source_target_pairs={{0,1},{1,2},{2,3},{3,0},{4,5},{5,6},{6,7},{7,4},{8,9},{9,10},{10,1... | collective-permute-start | bytes 184328 | tf_op jit(solution)/shard_map/ppermute | solution.py:162
  159.6 10.2 %collective-permute-start.12 = (f32[24,640]{1,0:T(8,128)S(1)}, f32[24,640]{1,0:T(8,128)S(1)}, u32[]{:S(2)}, u32[]{:S(2)}) collective-permute-start(f32[24,640]{1,0:T(8,128)S(1)} %get-tuple-element.35), channel_id=1, source_target_pairs={{0,4},{1,5},{2,6},{3,7},{4,8},{5,9},{6,10},{7,11},{8,12},{9,13},{1... | collective-permute-start | bytes 184328 | tf_op jit(solution)/shard_map/ppermute | solution.py:162
  160.6 4.6 %collective-permute-start.14 = (f32[16,640]{1,0:T(8,128)S(1)}, f32[16,640]{1,0:T(8,128)S(1)}, u32[]{:S(2)}, u32[]{:S(2)}) collective-permute-start(f32[16,640]{1,0:T(8,128)S(1)} %get-tuple-element.38), channel_id=1, source_target_pairs={{0,12},{1,13},{2,14},{3,15},{4,0},{5,1},{6,2},{7,3},{8,4},{9,5},{1... | collective-permute-start | bytes 122888 | tf_op jit(solution)/shard_map/ppermute | solution.py:162
  162.8 7.0 %collective-permute-start.7 = (f32[40,640]{1,0:T(8,128)S(1)}, f32[40,640]{1,0:T(8,128)S(1)}, u32[]{:S(2)}, u32[]{:S(2)}) collective-permute-start(f32[40,640]{1,0:T(8,128)S(1)} %pad_maximum_fusion.6), channel_id=1, source_target_pairs={{0,3},{1,0},{2,1},{3,2},{4,7},{5,4},{6,5},{7,6},{8,11},{9,8},{10,9... | collective-permute-start | bytes 307208 | tf_op jit(solution)/shard_map/ppermute | solution.py:162
  165.2 8.9 %collective-permute-start.15 = (f32[40,640]{1,0:T(8,128)S(1)}, f32[40,640]{1,0:T(8,128)S(1)}, u32[]{:S(2)}, u32[]{:S(2)}) collective-permute-start(f32[40,640]{1,0:T(8,128)S(1)} %pad_maximum_fusion.8), channel_id=1, source_target_pairs={{0,12},{1,13},{2,14},{3,15},{4,0},{5,1},{6,2},{7,3},{8,4},{9,5},{1... | collective-permute-start | bytes 307208 | tf_op jit(solution)/shard_map/ppermute | solution.py:162
  168.1 5.9 %collective-permute-start.5 = (f32[40,640]{1,0:T(8,128)S(1)}, f32[40,640]{1,0:T(8,128)S(1)}, u32[]{:S(2)}, u32[]{:S(2)}) collective-permute-start(f32[40,640]{1,0:T(8,128)S(1)} %pad_maximum_fusion.5), channel_id=1, source_target_pairs={{0,1},{1,2},{2,3},{3,0},{4,5},{5,6},{6,7},{7,4},{8,9},{9,10},{10,1... | collective-permute-start | bytes 307208 | tf_op jit(solution)/shard_map/ppermute | solution.py:162
  169.8 5.9 %collective-permute-start.13 = (f32[40,640]{1,0:T(8,128)S(1)}, f32[40,640]{1,0:T(8,128)S(1)}, u32[]{:S(2)}, u32[]{:S(2)}) collective-permute-start(f32[40,640]{1,0:T(8,128)S(1)} %pad_maximum_fusion.7), channel_id=1, source_target_pairs={{0,4},{1,5},{2,6},{3,7},{4,8},{5,9},{6,10},{7,11},{8,12},{9,13},{1... | collective-permute-start | bytes 307208 | tf_op jit(solution)/shard_map/ppermute | solution.py:162
Sparse Core Ops, SparseCore 0:
  83.2 29.4 all-gather.1

commit v5 on v4

--- a/solution.py
+++ b/solution.py
@@ -9,19 +9,17 @@
 from jax.sharding import PartitionSpec as P
 
 BF16, F32 = jnp.bfloat16, jnp.float32
+TOP = 32767.0
 
 
 def irrep_labels(sizes, count):
+    order = jnp.arange(sizes.shape[0], dtype=jnp.int32)
     positions = jnp.arange(count, dtype=jnp.int32)
-    starts = [jnp.int32(0)]
-    for g in range(sizes.shape[0]):
-        starts.append(starts[-1] + sizes[g])
-    labels, opened = jnp.zeros_like(positions), jnp.zeros_like(positions)
-    for g in range(1, sizes.shape[0] + 1):
-        after = positions >= starts[g]
-        labels = jnp.where(after, g, labels)
-        opened = jnp.where(after, starts[g], opened)
-    return labels, positions - opened, jnp.stack(starts)
+    ends = jnp.sum(jnp.where(order[None, :] <= order[:, None], sizes[None, :], 0), axis=1)
+    after = positions[:, None] >= ends[None, :]
+    labels = jnp.sum(after.astype(jnp.int32), axis=1)
+    places = positions - jnp.sum(jnp.where(after, sizes[None, :], 0), axis=1)
+    return labels, places, jnp.concatenate([jnp.zeros((1,), jnp.int32), ends])
 
 
 def label_lookup(orbitals, labels, count):
@@ -86,7 +84,7 @@
     )(scalars, cycle, c_label, code)
 
 
-def grouped_kernel(scalars, lhs, block, first, second, rows, total, *, bounds, irreps, halves, window, side):
+def grouped_kernel(scalars, lhs, block, out, rows, total, packed, *, bounds, irreps, halves, window):
     step = pl.program_id(0)
     groups, n_rows, _ = lhs.shape
     n_i, width = groups // halves, block.shape[2]
@@ -106,70 +104,51 @@
 
     @pl.when(step == irreps - 1)
     def _():
-        n_fold = side[0] * side[1]
+        n_fold = out.shape[0]
         part = n_rows // n_fold
-        z, x = scalars[bounds - 2], scalars[bounds - 1]
         for f in range(n_fold):
-            dz = lax.rem(f // side[1] - z + side[0], side[0])
-            dx = lax.rem(f % side[1] - x + side[1], side[1])
             for g in range(groups):
-                i, lane = g // halves, g % halves * width
-                at = (i % (n_i // 2)) * part
-                out, spot = (first, (dz, dx)) if i < n_i // 2 else (second, (dx, dz))
-                out[spot + (slice(at, at + part), slice(lane, lane + width))] = total[g, f * part:(f + 1) * part, :]
+                at, lane = g // halves * part, g % halves * width
+                packed[at:at + part, lane:lane + width] = total[g, f * part:(f + 1) * part, :]
+            values = packed[...]
+            most = jnp.maximum(jnp.max(jnp.abs(values), axis=0, keepdims=True), 1e-30)
+            scale = jnp.ceil(jnp.log2(most) * 4.0)
+            code = jnp.clip(jnp.round(values * (TOP * jnp.exp2(scale * -0.25))), -TOP, TOP)
+            code = jnp.concatenate([code, jnp.broadcast_to(scale, (8, scale.shape[1]))])
+            out[f] = code.astype(jnp.int32).astype(jnp.int16)
 
 
 def whole(shape):
     return pl.BlockSpec(shape, lambda r, s: (0,) * len(shape))
 
 
-def grouped_product(scalars, lhs, block, *, bounds, irreps, halves, window, side):
+def grouped_product(scalars, lhs, block, n_fold, *, bounds, irreps, halves, window):
     groups, n_rows, depth = lhs.shape
     width = block.shape[2]
     n_i = groups // halves
-    tail = (n_i // 2 * n_rows // (side[0] * side[1]), halves * width)
-    shapes = [(side[0], side[1]) + tail, (side[1], side[0]) + tail]
+    share = (n_i * n_rows // n_fold, halves * width)
+    shape = (n_fold, share[0] + 8, share[1])
     return pl.pallas_call(
         functools.partial(
-            grouped_kernel, bounds=bounds, irreps=irreps, halves=halves, window=window, side=side
-        ),
-        out_shape=[jax.ShapeDtypeStruct(shape, F32) for shape in shapes],
+            grouped_kernel, bounds=bounds, irreps=irreps, halves=halves, window=window
+        ),
+        out_shape=jax.ShapeDtypeStruct(shape, jnp.int16),
         grid_spec=pltpu.PrefetchScalarGridSpec(
             num_scalar_prefetch=1,
             grid=(irreps,),
             in_specs=[whole(lhs.shape), pl.BlockSpec((1, depth, width), lambda r, s: (r, 0, 0))],
-            out_specs=[whole(shape) for shape in shapes],
-            scratch_shapes=[pltpu.VMEM((groups * window, depth), BF16), pltpu.VMEM((groups, n_rows, width), F32)],
+            out_specs=whole(shape),
+            scratch_shapes=[
+                pltpu.VMEM((groups * window, depth), BF16),
+                pltpu.VMEM((groups, n_rows, width), F32),
+                pltpu.VMEM(share, F32),
+            ],
         ),
         compiler_params=pltpu.CompilerParams(vmem_limit_bytes=48 * 2**20),
         cost_estimate=pl.CostEstimate(
             flops=2 * irreps * groups * window * depth * width, bytes_accessed=13 * 2**20, transcendentals=0
         ),
     )(scalars, lhs, block)
-
-
-def ring(side, along, step):
-    pairs = []
-    for z in range(side[0]):
-        for x in range(side[1]):
-            to = ((z + step) % side[0], x) if along == 0 else (z, (x + step) % side[1])
-            pairs.append((z * side[1] + x, to[0] * side[1] + to[1]))
-    return pairs
-
-
-def ring_sums(parts, side, alongs):
-    def send(v, along, step):
-        return lax.ppermute(v, "fold", ring(side, along, step))
-
-    halfway = [p.shape[1] // 2 if p.ndim > 3 else -(-p.shape[1] // 16) * 8 for p in parts]
-    up = [send(p[2, :h], a, 1) for p, h, a in zip(parts, halfway, alongs)]
-    down = [send(p[2, h:], a, -1) for p, h, a in zip(parts, halfway, alongs)]
-    sums = []
-    for p, u, d, h, a in zip(parts, up, down, halfway, alongs):
-        right = send(jnp.concatenate([p[1, :h] + u, p[1, h:]]), a, 1)
-        left = send(jnp.concatenate([p[3, :h], p[3, h:] + d]), a, -1)
-        sums.append((p[0], right, left))
-    return [p + r + l for p, r, l in sums]
 
 
 def body(amplitudes, cycle_block, occ_sizes, vir_sizes, window_i, window_occ):
@@ -187,9 +166,8 @@
     to_place = one_hot_rows(vir_place, vmax)
     kappas = omax + 2 - omax % 2
     k_from = jnp.minimum(occ_starts[:irreps] // 2 * 2, occ_total - kappas)
-    kappa = jnp.arange(occ_total, dtype=jnp.int32)
-    for g in range(irreps):
-        kappa = kappa - jnp.where(occ == g, k_from[g], 0)
+    own_from = jnp.where(occ[:, None] == jnp.arange(irreps)[None, :], k_from[None, :], 0)
+    kappa = jnp.arange(occ_total, dtype=jnp.int32) - jnp.sum(own_from, axis=1)
     to_kappa = one_hot_rows(kappa, kappas)
     own_vir = lax.dynamic_slice_in_dim(vir, fold * c_local, c_local)
     k_own = lax.dynamic_slice_in_dim(occ, pair * k_local, k_local)
@@ -202,6 +180,8 @@
     narrow = narrow.reshape(n_i, k_local, halves, a_part, vmax).transpose(0, 2, 1, 3, 4)
     narrow = narrow.reshape(n_pair, k_local, a_part, vmax)
     narrow = lax.all_to_all(narrow, "pair", split_axis=0, concat_axis=0, tiled=True)
+    cycle = cycle_block.transpose(2, 1, 0, 3).reshape(j_local, occ_total * c_local, vir_total)
+    narrow, cycle = lax.optimization_barrier((narrow, cycle))
     narrow = narrow.reshape(occ_total, a_part, vmax)
 
     i_mine = lax.dynamic_index_in_dim(i_labels, pair // halves, keepdims=False)
@@ -216,14 +196,12 @@
     short = short.reshape(n_fold * a_part, kappas * c_local)
     lhs = lax.all_gather(short, "pair", axis=0)
 
-    side = (4, 4) if n_fold == 16 else (n_fold, 1)
     inside = starts % a_local
     bounds = [starts // a_local * a_part + jnp.clip(inside - h * a_part, 0, a_part) for h in range(halves)]
     scalars = jnp.concatenate(
         [i_labels, own_vir[:1], own_vir[-1:], k_from * c_local, j_labels]
-        + [jnp.stack([fold // side[1], fold % side[1]])] + bounds
+        + bounds
     ).astype(jnp.int32)
-    cycle = cycle_block.transpose(2, 1, 0, 3).reshape(j_local, occ_total * c_local, vir_total)
     lanes = math.gcd(vir_total, 128)
     c_label = jnp.tile(own_vir.astype(F32)[:, None], (kappas, lanes)).astype(BF16)
     code = jnp.broadcast_to((vir * vmax + vir_place)[:, None], (vir_total, j_local * vmax))
@@ -231,18 +209,12 @@
 
     most = min(vmax, -(-vmax // a_local) * a_part)
     window = min(-(-(most + 15) // 16) * 16, n_fold * a_part)
-    first, second = grouped_product(
-        scalars, lhs, blocks, bounds=n_i + irreps + j_local + 4, irreps=irreps, halves=halves, window=window, side=side
+    coded = grouped_product(
+        scalars, lhs, blocks, n_fold, bounds=n_i + irreps + j_local + 2, irreps=irreps, halves=halves, window=window
     )
-    if side == (4, 4):
-        first, second = ring_sums([first, second], side, (0, 1))
-        first, second = ring_sums([first, second], side, (1, 0))
-    else:
-        order = lax.rem(jnp.arange(n_fold) - fold + n_fold, n_fold)
-        both = jnp.concatenate([first[:, 0][order], second[0][order]], axis=1)
-        shares = jnp.sum(lax.all_to_all(both, "fold", split_axis=0, concat_axis=0, tiled=True), axis=0)
-        first, second = jnp.split(shares, 2)
-    total = jnp.concatenate([first, second]).astype(BF16).reshape(n_i, a_part, halves, j_local, vmax)
+    coded = lax.all_to_all(coded, "fold", split_axis=0, concat_axis=0, tiled=True).astype(F32)
+    shares = coded[:, :-8] * (jnp.exp2(coded[:, -8:-7] * 0.25) / TOP)
+    total = jnp.sum(shares, axis=0).astype(BF16).reshape(n_i, a_part, halves, j_local, vmax)
     total = total.transpose(0, 2, 1, 3, 4).reshape(n_i, a_local, j_local, vmax)
     spread_b = pick(total, "iajt,tb->iajb", to_place)
     x = i_labels[:, None, None] ^ own_vir[None, :, None] ^ j_labels[None, None, :]

time: 186 us -> 154 us (0.83); the launches traced: 184 us -> 155 us
  starting transfers between devices: 35.2 us -> 18.4 us
  between operations: 23.7 us -> 13.6 us
  local copies, waits for them, and re-layouts: 27.8 us -> 22.2 us
  waiting for transfers between devices: 26 us -> 31.4 us
  other arithmetic: 10.6 us -> 6.64 us
  Pallas kernels: 36 us -> 38.1 us
    ppermute x16 -> x0, starting transfers between devices: 30.7 us -> none  [send(): return lax.ppermute(v, 'fold', ring(side, along, step))]
    all_to_all x0 -> x1, waiting for transfers between devices: none -> 24.7 us  [body(): lax.all_to_all(coded, 'fold', split_axis=0, concat_axis=0, tiled=True)]
    all_to_all x0 -> x1, starting transfers between devices: none -> 13.8 us  [body(): lax.all_to_all(coded, 'fold', split_axis=0, concat_axis=0, tiled=True)]
    ppermute x16 -> x0, waiting for transfers between devices: 12.1 us -> none  [send(): return lax.ppermute(v, 'fold', ring(side, along, step))]
    all_to_all x1, waiting for transfers between devices: 13.8 us -> 4.2 us  [body(): lax.all_to_all(narrow, 'pair', split_axis=0, concat_axis=0, tiled=True)]
    sub x1, other arithmetic: 5.58 us -> 0.01 us  [body(): kappa = jnp.arange(occ_total, dtype=jnp.int32) - jnp.sum(own_from, axis=1)]
    slice x4 -> x1, local copies, waits for them, and re-layouts: 4.11 us -> 0.22 us  [the longest x2 3.23 us: irrep_labels(): starts.append(starts[-1] + sizes[g])]
    reduce_sum x0 -> x6, other arithmetic: none -> 2.68 us  [the longest x2 1.54 us: irrep_labels(): jnp.sum(jnp.where(order[None, :] <= order[:, None], sizes[None, :], 0), a...]
  transfers between devices with their start and end apart: 18 -> 3, of which waited for: 8 -> 3; matrix products, arithmetic and copies ran while one was open for 8% -> 9% of each run, Pallas kernels for 13% -> 16%
where the time goes in v5:
time: 154 us; the launch traced here: 155 us
  Pallas kernels  38.1 us (25%)
  waiting for transfers between devices  31.4 us (20%)
  local copies, waits for them, and re-layouts  22.2 us (14%)
  blocking collectives  20.8 us (14%)
  starting transfers between devices  18.4 us (12%)
  between operations  13.6 us (9%)
  other arithmetic  6.64 us (4%)
  matrix products  4.25 us (3%)
    all_to_all x1, waiting for transfers between devices, body(): lax.all_to_all(coded, 'fold', split_axis=0, concat_axis=0, tiled=True)  24.7 us
    pallas_call x1, Pallas kernels, class_blocks(): pl.pallas_call(functools.partial(block_kernel, n_i=n_i, irreps=irreps, wi...  24.5 us
    all_to_all x1, blocking collectives, body(): lax.all_to_all(short, 'fold', split_axis=0, concat_axis=0, tiled=True)  20.8 us
    all_to_all x1, starting transfers between devices, body(): lax.all_to_all(coded, 'fold', split_axis=0, concat_axis=0, tiled=True)  13.8 us
    pallas_call x1, Pallas kernels, grouped_product(): pl.pallas_call(functools.partial(grouped_kernel, bounds=bounds, irreps=ir...  13.6 us
    transpose x1, local copies, waits for them, and re-layouts, body(): cycle_block.transpose(2, 1, 0, 3)  9.39 us
    reshape x2, local copies, waits for them, and re-layouts, body(): short = short.reshape(a_part, kappas, n_fold, c_local).transpose(2, 0, 1, 3)  5.64 us
    all_to_all x1, starting transfers between devices, body(): lax.all_to_all(narrow, 'pair', split_axis=0, concat_axis=0, tiled=True)  4.55 us
  transfers between devices with their start and end apart: 3, of which 3 were waited for; matrix products, arithmetic and copies ran while one was open for 9% of the time, Pallas kernels for 16%

profile of v5, /device:TPU:0, one launch (start us, length us, event | category | flops | bytes accessed | tf_op | source)
XLA Modules:
  0.0 155.4 jit_solution(18191717885365731053)
XLA Ops:
  6.5 0.8 select_reduce_fusion.3
  7.5 0.8 select_reduce_fusion.4
  8.3 0.8 select_reduce_fusion.2
  9.1 0.7 select_reduce_fusion
  10.1 2.7 %fusion.14 = bf16[4,10,40,160]{3,2,1,0:T(8,128)(2,1)S(1)} fusion(bf16[4,10,40,640]{3,2,1,0:T(8,128)(2,1)} %param.6, s32[640]{0:T(1024)S(1)} %get-tuple-element.10, s32[4,10,40]{2,1,0:T(8,128)S(1)} %broadcast_xor_fusion, s32[640]{0:T(1024)S(1)} %get-tuple-element.21), kind=kOutput, calls=%fused_computation.16 | convolution fusion | flops 330086400 | bytes 2571520 | tf_op jit(solution)/shard_map/ikac,tc->ikat/dot_general | solution.py:35
  13.0 1.2 pad_maximum_fusion
  14.2 4.6 %all-to-all-start = ((bf16[8,10,20,160]{3,2,1,0:T(8,128)(2,1)}), bf16[8,10,20,160]{3,2,1,0:T(8,128)(2,1)S(1)}, u32[]{:S(2)}, u32[]{:S(2)}) async-start(bf16[8,10,20,160]{3,2,1,0:T(8,128)(2,1)} %bitcast.4), calls=%async_computation | async-start | bytes 1966080 | tf_op jit(solution)/shard_map/all_to_all | solution.py:182
  18.8 9.4 %copy.30 = bf16[2,80,40,640]{3,2,1,0:T(8,128)(2,1)} copy(bf16[2,80,40,640]{3,0,1,2:T(2,128)(2,1)} %bitcast.39) | data formatting | bytes 16384000 | tf_op jit(solution)/shard_map/transpose | solution.py:183
  28.4 0.6 dynamic_slice.18
  28.9 0.6 broadcast_xor_fusion.5
  29.8 4.2 %all-to-all-done = bf16[8,10,20,160]{3,2,1,0:T(8,128)(2,1)S(1)} async-done(((bf16[8,10,20,160]{3,2,1,0:T(8,128)(2,1)}), bf16[8,10,20,160]{3,2,1,0:T(8,128)(2,1)S(1)}, u32[]{:S(2)}, u32[]{:S(2)}) %all-to-all-start) | async-done | bytes 512032 | tf_op jit(solution)/shard_map/all_to_all | solution.py:182
  34.0 1.2 fusion.18
  35.2 3.6 %reshape.167 = bf16[20,22,16,40]{3,2,1,0:T(8,128)(2,1)} reshape(bf16[20,22,640]{2,1,0:T(8,128)(2,1)S(1)} %fusion.18) | data formatting | bytes 1126400 | tf_op jit(solution)/shard_map/reshape | solution.py:193
  38.9 2.0 %copy.46 = bf16[20,22,16,40]{3,1,2,0:T(8,128)(2,1)S(1)} copy(bf16[20,22,16,40]{3,2,1,0:T(8,128)(2,1)} %reshape.167) | data formatting | bytes 1126400 | tf_op jit(solution)/shard_map/reshape | solution.py:193
  40.9 1.3 reshape.168
  42.3 20.8 %all_to_all.15 = bf16[16,20,880]{2,1,0:T(8,128)(2,1)S(1)} all-to-all(bf16[16,20,880]{2,1,0:T(8,128)(2,1)S(1)} %copy.33), channel_id=1, replica_groups=mesh['pair'=8,'fold'=16] {'fold'}, dimensions={0} | all-to-all | bytes 1126400 | tf_op jit(solution)/shard_map/all_to_all | solution.py:195
  63.1 1.1 all_gather_reshape.3
  65.1 1.4 concatenate.14.scalars
  66.8 24.5 %shard_map.64.block = bf16[8,880,320]{2,1,0:T(8,128)(2,1)} custom-call(s32[34]{0:T(128)S(1)} %concatenate.14.scalars, bf16[2,3200,640]{2,1,0:T(8,128)(2,1)} %bitcast.40, bf16[880,128]{1,0:T(8,128)(2,1)S(1)} %tile.9.c_label, s32[640,320]{1,0:T(8,128)S(1)} %broadcast_in_dim.131.code), custom_call_target="tpu_custom_call" | custom-call | flops 5767168000 | bytes 14680064 | tf_op jit(solution)/shard_map/pallas_call | solution.py:67
  91.3 2.5 %all-gather.2.cloned.1.call-done.lhs = bf16[8,320,880]{2,1,0:T(8,128)(2,1)} async-done(((bf16[1,320,880]{2,1,0:T(8,128)(2,1)}), bf16[8,320,880]{2,1,0:T(8,128)(2,1)}) %all-gather.2.cloned.1.call-update) | async-done | bytes 4505616 | tf_op jit(solution)/shard_map/all_gather | solution.py:197
  93.8 13.6 %shard_map.65 = s16[16,88,640]{2,1,0:T(8,128)(2,1)} custom-call(s32[34]{0:T(128)S(1)} %concatenate.14.scalars, bf16[8,320,880]{2,1,0:T(8,128)(2,1)} %all-gather.2.cloned.1.call-done.lhs, bf16[8,880,320]{2,1,0:T(8,128)(2,1)} %shard_map.64.block), custom_call_target="tpu_custom_call" | custom-call | flops 3460300800 | bytes 13631488 | tf_op jit(solution)/shard_map/pallas_call | solution.py:131
  107.4 13.8 %all-to-all-start.2 = ((s16[16,88,640]{2,1,0:T(8,128)(2,1)}), s16[16,88,640]{2,1,0:T(8,128)(2,1)S(1)}, u32[]{:S(2)}, u32[]{:S(2)}) async-start(s16[16,88,640]{2,1,0:T(8,128)(2,1)} %shard_map.65), calls=%async_computation.2 | async-start | bytes 3604480 | tf_op jit(solution)/shard_map/all_to_all | solution.py:215
  121.4 24.7 %all-to-all-done.2 = s16[16,88,640]{2,1,0:T(8,128)(2,1)S(1)} async-done(((s16[16,88,640]{2,1,0:T(8,128)(2,1)}), s16[16,88,640]{2,1,0:T(8,128)(2,1)S(1)}, u32[]{:S(2)}, u32[]{:S(2)}) %all-to-all-start.2) | async-done | bytes 1802272 | tf_op jit(solution)/shard_map/all_to_all | solution.py:215
  147.5 1.1 copy.36
  (35 shorter events, 3.9 us)
Async XLA Ops:
  14.2 19.8 %all-to-all-start = ((bf16[8,10,20,160]{3,2,1,0:T(8,128)(2,1)}), bf16[8,10,20,160]{3,2,1,0:T(8,128)(2,1)S(1)}, u32[]{:S(2)}, u32[]{:S(2)}) async-start(bf16[8,10,20,160]{3,2,1,0:T(8,128)(2,1)} %bitcast.4), calls=%async_computation | async-start | bytes 1966080 | tf_op jit(solution)/shard_map/all_to_all | solution.py:182
  18.8 75.0 %all-gather.2.cloned.1.call-start = ((), (), s32[]{:S(2)}) async-start(), calls=%async_computation.3 | async-start | bytes 5160960 | tf_op jit(solution)/shard_map/all_gather | solution.py:197
  40.9 23.4 %copy-start = (s32[16]{0:T(128)S(1)}, s32[16]{0:T(128)}, u32[]{:S(2)}) copy-start(s32[16]{0:T(128)} %param.11) | copy-start | bytes 196
  107.4 38.7 %all-to-all-start.2 = ((s16[16,88,640]{2,1,0:T(8,128)(2,1)}), s16[16,88,640]{2,1,0:T(8,128)(2,1)S(1)}, u32[]{:S(2)}, u32[]{:S(2)}) async-start(s16[16,88,640]{2,1,0:T(8,128)(2,1)} %shard_map.65), calls=%async_computation.2 | async-start | bytes 3604480 | tf_op jit(solution)/shard_map/all_to_all | solution.py:215
Sparse Core Ops, SparseCore 0:
  64.3 29.4 all-gather.1

commit v6 on v5

--- a/solution.py
+++ b/solution.py
@@ -13,13 +13,13 @@
 
 
 def irrep_labels(sizes, count):
-    order = jnp.arange(sizes.shape[0], dtype=jnp.int32)
+    order = jnp.arange(sizes.shape[1], dtype=jnp.int32)
     positions = jnp.arange(count, dtype=jnp.int32)
-    ends = jnp.sum(jnp.where(order[None, :] <= order[:, None], sizes[None, :], 0), axis=1)
-    after = positions[:, None] >= ends[None, :]
-    labels = jnp.sum(after.astype(jnp.int32), axis=1)
-    places = positions - jnp.sum(jnp.where(after, sizes[None, :], 0), axis=1)
-    return labels, places, jnp.concatenate([jnp.zeros((1,), jnp.int32), ends])
+    ends = jnp.sum(jnp.where(order[None, None, :] <= order[None, :, None], sizes[:, None, :], 0), axis=2)
+    after = positions[None, :, None] >= ends[:, None, :]
+    labels = jnp.sum(after.astype(jnp.int32), axis=2)
+    places = positions - jnp.sum(jnp.where(after, sizes[:, None, :], 0), axis=2)
+    return labels, places, jnp.concatenate([jnp.zeros((sizes.shape[0], 1), jnp.int32), ends], axis=1)
 
 
 def label_lookup(orbitals, labels, count):
@@ -118,6 +118,81 @@
             out[f] = code.astype(jnp.int32).astype(jnp.int16)
 
 
+def narrow_c_kernel(x, row_label, label, to_place, out, line, *, a_local):
+    masked = jnp.where(row_label[0] == label[...], x[0].astype(F32), 0.0).astype(BF16)
+    narrow = lax.dot_general(
+        to_place[...], masked, (((1,), (1,)), ((), ())), preferred_element_type=F32
+    )
+    halves, rows = out.shape[0], out.shape[2]
+    part = a_local // halves
+    for h in range(halves):
+        for k in range(rows // part):
+            line[:, k * part:(k + 1) * part] = narrow[:, k * a_local + h * part:k * a_local + (h + 1) * part]
+        out[h] = line[...].astype(BF16)
+
+
+def narrow_c(x, row_label, label, to_place, halves, a_local):
+    n_i, rows, vir_total = x.shape
+    width = to_place.shape[0]
+    return pl.pallas_call(
+        functools.partial(narrow_c_kernel, a_local=a_local),
+        out_shape=jax.ShapeDtypeStruct((n_i * halves, width, rows // halves), BF16),
+        grid=(n_i,),
+        in_specs=[
+            pl.BlockSpec((1, rows, vir_total), lambda i: (i, 0, 0)),
+            pl.BlockSpec((1, rows, 1), lambda i: (i, 0, 0)),
+            pl.BlockSpec(label.shape, lambda i: (0, 0)),
+            pl.BlockSpec(to_place.shape, lambda i: (0, 0)),
+        ],
+        out_specs=pl.BlockSpec((halves, width, rows // halves), lambda i: (i, 0, 0)),
+        scratch_shapes=[pltpu.VMEM((width, rows // halves), F32)],
+        compiler_params=pltpu.CompilerParams(vmem_limit_bytes=32 * 2**20),
+        cost_estimate=pl.CostEstimate(
+            flops=2 * x.size * width, bytes_accessed=3 * 2**20, transcendentals=0
+        ),
+    )(x, row_label, label, to_place)
+
+
+def narrow_k_kernel(x, to_place, row_label, label, to_row, out, wide, short, line):
+    n_fold, a_part, depth = out.shape
+    a_rows = line.shape[0]
+    c_local = wide.shape[1] // n_fold
+    sources, _, rows = x.shape
+    room = wide.shape[0] // sources
+    for p in range(sources):
+        spread = lax.dot_general(x[p], to_place[...], (((0,), (0,)), ((), ())), preferred_element_type=F32)
+        spread = jnp.where(row_label[p] == label[...], spread, 0.0)
+        if room > rows:
+            spread = jnp.concatenate([spread, jnp.zeros((room - rows, spread.shape[1]), F32)])
+        wide[p * room:(p + 1) * room, :] = spread.astype(BF16)
+    short[...] = jnp.dot(to_row[...], wide[...], preferred_element_type=F32)
+    for f in range(n_fold):
+        for q in range(depth // c_local):
+            line[:, q * c_local:(q + 1) * c_local] = (
+                short[q * a_rows:(q + 1) * a_rows, f * c_local:(f + 1) * c_local]
+            )
+        out[f] = line[:a_part, :].astype(BF16)
+
+
+def narrow_k(x, to_place, row_label, label, to_row, n_fold, a_part, c_local):
+    vir_total = label.shape[1]
+    a_rows = -(-a_part // 8) * 8
+    depth = to_row.shape[0] // a_rows * c_local
+    return pl.pallas_call(
+        narrow_k_kernel,
+        out_shape=jax.ShapeDtypeStruct((n_fold, a_part, depth), BF16),
+        scratch_shapes=[
+            pltpu.VMEM((to_row.shape[1], vir_total), BF16),
+            pltpu.VMEM((to_row.shape[0], vir_total), F32),
+            pltpu.VMEM((a_rows, depth), F32),
+        ],
+        compiler_params=pltpu.CompilerParams(vmem_limit_bytes=32 * 2**20),
+        cost_estimate=pl.CostEstimate(
+            flops=2 * to_row.size * vir_total, bytes_accessed=3 * 2**20, transcendentals=0
+        ),
+    )(x, to_place, row_label, label, to_row)
+
+
 def whole(shape):
     return pl.BlockSpec(shape, lambda r, s: (0,) * len(shape))
 
@@ -161,8 +236,9 @@
     halves = n_pair // n_i
     a_part = a_local // halves
 
-    occ, _, occ_starts = irrep_labels(occ_sizes, occ_total)
-    vir, vir_place, starts = irrep_labels(vir_sizes, vir_total)
+    labels, places, all_starts = irrep_labels(jnp.stack([occ_sizes, vir_sizes]), vir_total)
+    occ, vir, vir_place = labels[0, :occ_total], labels[1], places[1]
+    occ_starts, starts = all_starts[0], all_starts[1]
     to_place = one_hot_rows(vir_place, vmax)
     kappas = omax + 2 - omax % 2
     k_from = jnp.minimum(occ_starts[:irreps] // 2 * 2, occ_total - kappas)
@@ -174,24 +250,23 @@
     i_labels = label_lookup(window_i, occ, occ_total)
     j_labels = label_lookup(lax.dynamic_slice_in_dim(window_occ, pair * j_local, j_local), occ, occ_total)
 
-    x = i_labels[:, None, None] ^ k_own[None, :, None] ^ own_vir[None, None, :]
-    masked = jnp.where(x[..., None] == vir, amplitudes, jnp.zeros_like(amplitudes))
-    narrow = pick(masked, "ikac,tc->ikat", to_place)
-    narrow = narrow.reshape(n_i, k_local, halves, a_part, vmax).transpose(0, 2, 1, 3, 4)
-    narrow = narrow.reshape(n_pair, k_local, a_part, vmax)
+    x = (i_labels[:, None, None] ^ k_own[None, :, None] ^ own_vir[None, None, :]).reshape(n_i, -1, 1)
+    narrow = narrow_c(amplitudes.reshape(n_i, -1, vir_total), x, vir[None, :], to_place, halves, a_local)
     narrow = lax.all_to_all(narrow, "pair", split_axis=0, concat_axis=0, tiled=True)
     cycle = cycle_block.transpose(2, 1, 0, 3).reshape(j_local, occ_total * c_local, vir_total)
     narrow, cycle = lax.optimization_barrier((narrow, cycle))
-    narrow = narrow.reshape(occ_total, a_part, vmax)
 
     i_mine = lax.dynamic_index_in_dim(i_labels, pair // halves, keepdims=False)
     a_mine = lax.dynamic_slice_in_dim(vir, fold * a_local + (pair % halves) * a_part, a_part)
-    wide = pick(narrow, "kat,tc->akc", to_place)
-    x = i_mine ^ occ[None, :, None] ^ a_mine[:, None, None] ^ vir[None, None, :]
-    wide = jnp.where(x == 0, wide, jnp.zeros_like(wide))
-    short = pick(to_kappa, "qk,akc->aqc", wide)
-    short = short.reshape(a_part, kappas, n_fold, c_local).transpose(2, 0, 1, 3)
-    short = short.reshape(n_fold, a_part, kappas * c_local)
+    x = (i_mine ^ occ[:, None] ^ a_mine[None, :]).reshape(n_pair, k_local * a_part, 1)
+    a_rows = -(-a_part // 8) * 8
+    room = -(-k_local * a_part // 16) * 16
+    row = jnp.arange(kappas * a_rows, dtype=jnp.int32)[:, None]
+    k_kappa = jnp.repeat(kappa, a_part).reshape(n_pair, -1)
+    k_kappa = jnp.pad(k_kappa, ((0, 0), (0, room - k_kappa.shape[1])), constant_values=-1).reshape(1, -1)
+    column = jnp.arange(n_pair * room, dtype=jnp.int32)[None, :] % room % a_part
+    to_row = ((row // a_rows == k_kappa) & (row % a_rows == column)).astype(BF16)
+    short = narrow_k(narrow, to_place, x, vir[None, :], to_row, n_fold, a_part, c_local)
     short = lax.all_to_all(short, "fold", split_axis=0, concat_axis=0, tiled=True)
     short = short.reshape(n_fold * a_part, kappas * c_local)
     lhs = lax.all_gather(short, "pair", axis=0)

time: 154 us -> 151 us (0.981)
  Pallas kernels: 38.1 us -> 45.2 us
  local copies, waits for them, and re-layouts: 22.2 us -> 17.2 us
  matrix products: 4.25 us -> 0.32 us
    pallas_call x0 -> x2, Pallas kernels: none -> 7.38 us  [the longest x1 3.73 us: narrow_c(): pl.pallas_call(functools.partial(narrow_c_kernel, a_local=a_local), out_s...]
    reshape x4 -> x0, local copies, waits for them, and re-layouts: 7.02 us -> none  [the longest x2 5.64 us: body(): short = short.reshape(a_part, kappas, n_fold, c_local).transpose(2, 0, 1, 3)]
    dot_general x3 -> x1, matrix products: 4.25 us -> 0.32 us  [pick(): return jnp.einsum(spec, x, y, preferred_element_type=F32).astype(BF16)]
    all_to_all x1, waiting for transfers between devices: 4.2 us -> 0.4 us  [body(): lax.all_to_all(narrow, 'pair', split_axis=0, concat_axis=0, tiled=True)]
    all_gather x1, waiting for transfers between devices: 2.47 us -> 4.63 us  [body(): lhs = lax.all_gather(short, 'pair', axis=0)]
    reduce_sum x4 -> x2, other arithmetic: 2.37 us -> 0.25 us  [the longest x1 0.14 us: irrep_labels(): jnp.sum(jnp.where(order[None, None, :] <= order[None, :, None], sizes[:,...]
    xor x0 -> x11, local copies, waits for them, and re-layouts: none -> 2.01 us  [the longest x5 1.41 us: body(): i_labels[:, None, None] ^ k_own[None, :, None] ^ own_vir[None, None, :]]
where the time goes in v6:
time: 151 us; the launch traced here: 152 us
  Pallas kernels  45.2 us (30%)
  waiting for transfers between devices  30.9 us (20%)
  blocking collectives  21.2 us (14%)
  local copies, waits for them, and re-layouts  17.2 us (11%)
  starting transfers between devices  17 us (11%)
  between operations  13.6 us (9%)
  other arithmetic  6.24 us (4%)
    all_to_all x1, waiting for transfers between devices, body(): lax.all_to_all(coded, 'fold', split_axis=0, concat_axis=0, tiled=True)  25.8 us
    pallas_call x1, Pallas kernels, class_blocks(): pl.pallas_call(functools.partial(block_kernel, n_i=n_i, irreps=irreps, wi...  24.2 us
    all_to_all x1, blocking collectives, body(): lax.all_to_all(short, 'fold', split_axis=0, concat_axis=0, tiled=True)  21.2 us
    pallas_call x1, Pallas kernels, grouped_product(): pl.pallas_call(functools.partial(grouped_kernel, bounds=bounds, irreps=ir...  13.6 us
    all_to_all x1, starting transfers between devices, body(): lax.all_to_all(coded, 'fold', split_axis=0, concat_axis=0, tiled=True)  12.4 us
    transpose x1, local copies, waits for them, and re-layouts, body(): cycle_block.transpose(2, 1, 0, 3)  9.39 us
    all_gather x1, waiting for transfers between devices, body(): lhs = lax.all_gather(short, 'pair', axis=0)  4.63 us
    all_to_all x1, starting transfers between devices, body(): lax.all_to_all(narrow, 'pair', split_axis=0, concat_axis=0, tiled=True)  4.56 us
  transfers between devices with their start and end apart: 3, of which 3 were waited for; matrix products, arithmetic and copies ran while one was open for 9% of the time, Pallas kernels for 16%

profile of v6, /device:TPU:0, one launch (start us, length us, event | category | flops | bytes accessed | tf_op | source)
XLA Modules:
  0.0 151.6 jit_solution(11784869067434498804)
XLA Ops:
  6.5 0.8 pad_add_fusion
  7.6 0.8 select_reduce_fusion.3
  8.5 0.6 dynamic_slice.19
  9.1 0.7 xor_reduce_fusion
  10.0 1.2 xor.152
  11.4 1.3 broadcast_xor_fusion.1.row_label
  12.7 3.7 %shard_map.64 = bf16[8,160,200]{2,1,0:T(8,128)(2,1)} custom-call(bf16[4,400,640]{2,1,0:T(8,128)(2,1)S(1)} %bitcast.57, s32[4,400,1]{2,1,0:T(8,128)S(1)} %broadcast_xor_fusion.1.row_label, s32[1,640]{1,0:T(1,128)S(1)} %get-tuple-element.18.label, bf16[160,640]{1,0:T(8,128)(2,1)S(1)} %fusion.3.to_place), custom_call_target="tpu_custom_call" | custom-call | flops 327680000 | bytes 3145728 | tf_op jit(solution)/shard_map/pallas_call | solution.py:137
  16.4 4.6 %all-to-all-start = ((bf16[8,160,200]{2,1,0:T(8,128)(2,1)}), bf16[8,160,200]{2,1,0:T(8,128)(2,1)S(1)}, u32[]{:S(2)}, u32[]{:S(2)}) async-start(bf16[8,160,200]{2,1,0:T(8,128)(2,1)} %shard_map.64), calls=%async_computation | async-start | bytes 1310720 | tf_op jit(solution)/shard_map/all_to_all | solution.py:255
  21.1 9.4 %copy.29 = bf16[2,80,40,640]{3,2,1,0:T(8,128)(2,1)} copy(bf16[2,80,40,640]{3,0,1,2:T(2,128)(2,1)} %bitcast.58) | data formatting | bytes 16384000 | tf_op jit(solution)/shard_map/transpose | solution.py:256
  31.7 0.6 and_convert_fusion.to_row
  32.3 0.4 all-to-all-done.x
  32.7 3.6 %shard_map.65 = bf16[16,20,880]{2,1,0:T(8,128)(2,1)S(1)} custom-call(bf16[8,160,200]{2,1,0:T(8,128)(2,1)S(1)} %all-to-all-done.x, bf16[160,640]{1,0:T(8,128)(2,1)S(1)} %fusion.3.to_place, s32[8,200,1]{2,1,0:T(8,128)S(1)} %broadcast_xor_fusion.row_label, s32[1,640]{1,0:T(1,128)S(1)} %get-tuple-element.18.label, bf16[528,1664]{1,0:T(8,128)(2,1)S(1)} %and_convert_fusion.to_row), custom_call_target="tpu_custom_call" | custom-call | flops 1124597760 | bytes 3145728 | tf_op jit(solution)/shard_map/pallas_call | solution.py:181
  36.4 21.2 %all_to_all.15 = bf16[16,20,880]{2,1,0:T(8,128)(2,1)S(1)} all-to-all(bf16[16,20,880]{2,1,0:T(8,128)(2,1)S(1)} %shard_map.65), channel_id=1, replica_groups=mesh['pair'=8,'fold'=16] {'fold'}, dimensions={0} | all-to-all | bytes 1126400 | tf_op jit(solution)/shard_map/all_to_all | solution.py:270
  57.5 1.1 all_gather_reshape.3
  59.0 0.6 fusion.31
  59.8 1.4 concatenate.7.scalars
  61.5 24.2 %shard_map.66.block = bf16[8,880,320]{2,1,0:T(8,128)(2,1)} custom-call(s32[34]{0:T(128)S(1)} %concatenate.7.scalars, bf16[2,3200,640]{2,1,0:T(8,128)(2,1)} %bitcast.59, bf16[880,128]{1,0:T(8,128)(2,1)S(1)} %tile.9.c_label, s32[640,320]{1,0:T(8,128)S(1)} %broadcast_in_dim.125.code), custom_call_target="tpu_custom_call" | custom-call | flops 5767168000 | bytes 14680064 | tf_op jit(solution)/shard_map/pallas_call | solution.py:67
  85.6 4.6 %all-gather.2.cloned.1.call-done.lhs = bf16[8,320,880]{2,1,0:T(8,128)(2,1)} async-done(((bf16[1,320,880]{2,1,0:T(8,128)(2,1)}), bf16[8,320,880]{2,1,0:T(8,128)(2,1)}) %all-gather.2.cloned.1.call-update) | async-done | bytes 4505616 | tf_op jit(solution)/shard_map/all_gather | solution.py:272
  90.3 13.6 %shard_map.67 = s16[16,88,640]{2,1,0:T(8,128)(2,1)} custom-call(s32[34]{0:T(128)S(1)} %concatenate.7.scalars, bf16[8,320,880]{2,1,0:T(8,128)(2,1)} %all-gather.2.cloned.1.call-done.lhs, bf16[8,880,320]{2,1,0:T(8,128)(2,1)} %shard_map.66.block), custom_call_target="tpu_custom_call" | custom-call | flops 3460300800 | bytes 13631488 | tf_op jit(solution)/shard_map/pallas_call | solution.py:206
  103.9 12.4 %all-to-all-start.2 = ((s16[16,88,640]{2,1,0:T(8,128)(2,1)}), s16[16,88,640]{2,1,0:T(8,128)(2,1)S(1)}, u32[]{:S(2)}, u32[]{:S(2)}) async-start(s16[16,88,640]{2,1,0:T(8,128)(2,1)} %shard_map.67), calls=%async_computation.2 | async-start | bytes 3604480 | tf_op jit(solution)/shard_map/all_to_all | solution.py:290
  116.4 25.8 %all-to-all-done.2 = s16[16,88,640]{2,1,0:T(8,128)(2,1)S(1)} async-done(((s16[16,88,640]{2,1,0:T(8,128)(2,1)}), s16[16,88,640]{2,1,0:T(8,128)(2,1)S(1)}, u32[]{:S(2)}, u32[]{:S(2)}) %all-to-all-start.2) | async-done | bytes 1802272 | tf_op jit(solution)/shard_map/all_to_all | solution.py:290
  142.2 0.5 convert_element_type.40
  143.3 0.3 fusion.1
  143.6 1.1 copy.34
  (52 shorter events, 3.6 us)
Async XLA Ops:
  6.5 6.1 %copy-start = (bf16[4,10,40,640]{3,2,1,0:T(8,128)(2,1)S(1)}, bf16[4,10,40,640]{3,2,1,0:T(8,128)(2,1)}, u32[]{:S(2)}) copy-start(bf16[4,10,40,640]{3,2,1,0:T(8,128)(2,1)} %param.6) | copy-start | bytes 6144004
  16.4 16.3 %all-to-all-start = ((bf16[8,160,200]{2,1,0:T(8,128)(2,1)}), bf16[8,160,200]{2,1,0:T(8,128)(2,1)S(1)}, u32[]{:S(2)}, u32[]{:S(2)}) async-start(bf16[8,160,200]{2,1,0:T(8,128)(2,1)} %shard_map.64), calls=%async_computation | async-start | bytes 1310720 | tf_op jit(solution)/shard_map/all_to_all | solution.py:255
  20.9 69.3 %all-gather.2.cloned.1.call-start = ((), (), s32[]{:S(2)}) async-start(), calls=%async_computation.3 | async-start | bytes 5160960 | tf_op jit(solution)/shard_map/all_gather | solution.py:272
  32.7 26.0 %copy-start.1 = (s32[16]{0:T(128)S(1)}, s32[16]{0:T(128)}, u32[]{:S(2)}) copy-start(s32[16]{0:T(128)} %param.11) | copy-start | bytes 196
  103.9 38.3 %all-to-all-start.2 = ((s16[16,88,640]{2,1,0:T(8,128)(2,1)}), s16[16,88,640]{2,1,0:T(8,128)(2,1)S(1)}, u32[]{:S(2)}, u32[]{:S(2)}) async-start(s16[16,88,640]{2,1,0:T(8,128)(2,1)} %shard_map.67), calls=%async_computation.2 | async-start | bytes 3604480 | tf_op jit(solution)/shard_map/all_to_all | solution.py:290
Sparse Core Ops, SparseCore 0:
  58.8 31.4 all-gather.1

commit v7 on v6

--- a/solution.py
+++ b/solution.py
@@ -35,53 +35,67 @@
     return jnp.einsum(spec, x, y, preferred_element_type=F32).astype(BF16)
 
 
-def block_kernel(scalars, cycle, c_label, code, out, chosen, picks, *, n_i, irreps, width):
+def tile_spans(c_local):
+    spans = []
+    for first in range(0, 2 * c_local, 16):
+        runs = []
+        for row in range(first, first + 16):
+            c = row % c_local
+            if runs and c == runs[-1][1] + 1:
+                runs[-1][1] = c
+            else:
+                runs.append([c, c])
+        spans.append(runs)
+    return spans
+
+
+def block_kernel(scalars, cycle, c_label, picks, out, chosen, *, n_i, irreps, owns):
     step = pl.program_id(0)
-    n_j = cycle.shape[0]
-    depth, vir_total = c_label.shape[0], cycle.shape[2]
-    lane = lax.broadcasted_iota(jnp.int32, (vir_total, n_j * width), 1)
+    n_j, _, pair_rows, vir_total = cycle.shape
+    k_pairs, width = chosen.shape[1], picks.shape[2]
+    for tile, runs in enumerate(tile_spans(pair_rows // 2)):
+        rows = slice(16 * tile, 16 * tile + 16)
+
+        def place(h, _):
+            first = scalars[n_i + (step ^ h)]
+            own = c_label[rows, :] == h.astype(F32).astype(BF16)
+            own = jnp.broadcast_to(own[None], (k_pairs,) + own.shape)
+            for j in range(n_j):
+                chosen[j, :, rows, :] = jnp.where(
+                    own, cycle[j, pl.ds(first, k_pairs), rows, :], chosen[j, :, rows, :]
+                )
+            return 0
+
+        for low, high in runs:
+            lax.fori_loop(scalars[owns + low], scalars[owns + high] + 1, place, 0)
     for j in range(n_j):
-        wanted = (step ^ scalars[n_i + 2 + irreps + j]) * width + lane - j * width
-        own = (lane >= j * width) & (lane < (j + 1) * width) & (code[...] == wanted)
-        picks[j * vir_total:(j + 1) * vir_total, :] = own.astype(F32).astype(BF16)
-
-    def place(h, _):
-        first = pl.multiple_of(scalars[n_i + 2 + (step ^ h)], 16)
-        label = h.astype(F32).astype(BF16)
-        for j in range(n_j):
-            for at in range(0, vir_total, c_label.shape[1]):
-                lanes = slice(at, at + c_label.shape[1])
-                spot = slice(j * vir_total + at, j * vir_total + at + c_label.shape[1])
-                chosen[:, spot] = jnp.where(
-                    c_label[...] == label, cycle[j, pl.ds(first, depth), lanes], chosen[:, spot]
-                )
-        return 0
-
-    lax.fori_loop(scalars[n_i], scalars[n_i + 1] + 1, place, 0)
-    out[0] = jnp.dot(chosen[...], picks[...], preferred_element_type=F32).astype(BF16)
-
-
-def class_blocks(scalars, cycle, c_label, code, *, n_i, irreps, width):
-    n_j, _, vir_total = cycle.shape
-    depth = c_label.shape[0]
+        narrow = jnp.dot(
+            chosen[j].reshape(k_pairs * pair_rows, vir_total),
+            picks[step ^ scalars[n_i + irreps + j]],
+            preferred_element_type=F32,
+        )
+        out[0, :, j * width:(j + 1) * width] = narrow.astype(BF16)
+
+
+def class_blocks(scalars, cycle, c_label, picks, *, n_i, irreps, owns, k_pairs):
+    n_j, _, pair_rows, vir_total = cycle.shape
+    width = picks.shape[2]
+    depth = k_pairs * pair_rows
     return pl.pallas_call(
-        functools.partial(block_kernel, n_i=n_i, irreps=irreps, width=width),
+        functools.partial(block_kernel, n_i=n_i, irreps=irreps, owns=owns),
         out_shape=jax.ShapeDtypeStruct((irreps, depth, n_j * width), BF16),
         grid_spec=pltpu.PrefetchScalarGridSpec(
             num_scalar_prefetch=1,
             grid=(irreps,),
-            in_specs=[whole(cycle.shape), whole(c_label.shape), whole(code.shape)],
+            in_specs=[whole(cycle.shape), whole(c_label.shape), whole(picks.shape)],
             out_specs=pl.BlockSpec((1, depth, n_j * width), lambda r, s: (r, 0, 0)),
-            scratch_shapes=[
-                pltpu.VMEM((depth, n_j * vir_total), BF16),
-                pltpu.VMEM((n_j * vir_total, n_j * width), BF16),
-            ],
+            scratch_shapes=[pltpu.VMEM((n_j, k_pairs, pair_rows, vir_total), BF16)],
         ),
         compiler_params=pltpu.CompilerParams(vmem_limit_bytes=48 * 2**20),
         cost_estimate=pl.CostEstimate(
-            flops=2 * irreps * depth * n_j * vir_total * n_j * width, bytes_accessed=14 * 2**20, transcendentals=0
-        ),
-    )(scalars, cycle, c_label, code)
+            flops=2 * irreps * depth * n_j * vir_total * width, bytes_accessed=14 * 2**20, transcendentals=0
+        ),
+    )(scalars, cycle, c_label, picks)
 
 
 def grouped_kernel(scalars, lhs, block, out, rows, total, packed, *, bounds, irreps, halves, window):
@@ -118,10 +132,15 @@
             out[f] = code.astype(jnp.int32).astype(jnp.int16)
 
 
-def narrow_c_kernel(x, row_label, label, to_place, out, line, *, a_local):
-    masked = jnp.where(row_label[0] == label[...], x[0].astype(F32), 0.0).astype(BF16)
+def narrow_c_kernel(scalars, x, a_label, label, to_place, out, masked, line, *, n_i, a_local):
+    i_label = scalars[pl.program_id(0)]
+    between = a_label[...] ^ label[...]
+    for k in range(masked.shape[0] // a_local):
+        rows = slice(k * a_local, (k + 1) * a_local)
+        own = between == (i_label ^ scalars[n_i + k])
+        masked[rows, :] = jnp.where(own, x[0, k].astype(F32), 0.0)
     narrow = lax.dot_general(
-        to_place[...], masked, (((1,), (1,)), ((), ())), preferred_element_type=F32
+        to_place[...], masked[...].astype(BF16), (((1,), (1,)), ((), ())), preferred_element_type=F32
     )
     halves, rows = out.shape[0], out.shape[2]
     part = a_local // halves
@@ -131,26 +150,30 @@
         out[h] = line[...].astype(BF16)
 
 
-def narrow_c(x, row_label, label, to_place, halves, a_local):
-    n_i, rows, vir_total = x.shape
+def narrow_c(scalars, x, a_label, label, to_place, halves):
+    n_i, k_local, a_local, vir_total = x.shape
     width = to_place.shape[0]
+    rows = k_local * a_local
     return pl.pallas_call(
-        functools.partial(narrow_c_kernel, a_local=a_local),
+        functools.partial(narrow_c_kernel, n_i=n_i, a_local=a_local),
         out_shape=jax.ShapeDtypeStruct((n_i * halves, width, rows // halves), BF16),
-        grid=(n_i,),
-        in_specs=[
-            pl.BlockSpec((1, rows, vir_total), lambda i: (i, 0, 0)),
-            pl.BlockSpec((1, rows, 1), lambda i: (i, 0, 0)),
-            pl.BlockSpec(label.shape, lambda i: (0, 0)),
-            pl.BlockSpec(to_place.shape, lambda i: (0, 0)),
-        ],
-        out_specs=pl.BlockSpec((halves, width, rows // halves), lambda i: (i, 0, 0)),
-        scratch_shapes=[pltpu.VMEM((width, rows // halves), F32)],
+        grid_spec=pltpu.PrefetchScalarGridSpec(
+            num_scalar_prefetch=1,
+            grid=(n_i,),
+            in_specs=[
+                pl.BlockSpec((1, k_local, a_local, vir_total), lambda i, s: (i, 0, 0, 0)),
+                whole(a_label.shape),
+                whole(label.shape),
+                whole(to_place.shape),
+            ],
+            out_specs=pl.BlockSpec((halves, width, rows // halves), lambda i, s: (i, 0, 0)),
+            scratch_shapes=[pltpu.VMEM((rows, vir_total), F32), pltpu.VMEM((width, rows // halves), F32)],
+        ),
         compiler_params=pltpu.CompilerParams(vmem_limit_bytes=32 * 2**20),
         cost_estimate=pl.CostEstimate(
             flops=2 * x.size * width, bytes_accessed=3 * 2**20, transcendentals=0
         ),
-    )(x, row_label, label, to_place)
+    )(scalars, x, a_label, label, to_place)
 
 
 def narrow_k_kernel(x, to_place, row_label, label, to_row, out, wide, short, line):
@@ -250,11 +273,15 @@
     i_labels = label_lookup(window_i, occ, occ_total)
     j_labels = label_lookup(lax.dynamic_slice_in_dim(window_occ, pair * j_local, j_local), occ, occ_total)
 
-    x = (i_labels[:, None, None] ^ k_own[None, :, None] ^ own_vir[None, None, :]).reshape(n_i, -1, 1)
-    narrow = narrow_c(amplitudes.reshape(n_i, -1, vir_total), x, vir[None, :], to_place, halves, a_local)
+    narrow = narrow_c(
+        jnp.concatenate([i_labels, k_own]), amplitudes, own_vir[:, None], vir[None, :], to_place, halves
+    )
     narrow = lax.all_to_all(narrow, "pair", split_axis=0, concat_axis=0, tiled=True)
-    cycle = cycle_block.transpose(2, 1, 0, 3).reshape(j_local, occ_total * c_local, vir_total)
-    narrow, cycle = lax.optimization_barrier((narrow, cycle))
+    cycle = cycle_block.transpose(2, 1, 0, 3).reshape(j_local, occ_total // 2, 2 * c_local, vir_total)
+    code = (vir * vmax + vir_place)[None, :, None]
+    spots = jnp.arange(irreps * vmax, dtype=jnp.int32).reshape(irreps, 1, vmax)
+    picks = (code == spots).astype(BF16)
+    narrow, cycle, picks = lax.optimization_barrier((narrow, cycle, picks))
 
     i_mine = lax.dynamic_index_in_dim(i_labels, pair // halves, keepdims=False)
     a_mine = lax.dynamic_slice_in_dim(vir, fold * a_local + (pair % halves) * a_part, a_part)
@@ -273,19 +300,17 @@
 
     inside = starts % a_local
     bounds = [starts // a_local * a_part + jnp.clip(inside - h * a_part, 0, a_part) for h in range(halves)]
-    scalars = jnp.concatenate(
-        [i_labels, own_vir[:1], own_vir[-1:], k_from * c_local, j_labels]
-        + bounds
-    ).astype(jnp.int32)
-    lanes = math.gcd(vir_total, 128)
-    c_label = jnp.tile(own_vir.astype(F32)[:, None], (kappas, lanes)).astype(BF16)
-    code = jnp.broadcast_to((vir * vmax + vir_place)[:, None], (vir_total, j_local * vmax))
-    blocks = class_blocks(scalars, cycle, c_label, code, n_i=n_i, irreps=irreps, width=vmax)
+    scalars = jnp.concatenate([i_labels, k_from // 2, j_labels] + bounds + [own_vir]).astype(jnp.int32)
+    low = n_i + irreps + j_local
+    c_label = jnp.broadcast_to(jnp.tile(own_vir.astype(F32), 2)[:, None], (2 * c_local, vir_total)).astype(BF16)
+    blocks = class_blocks(
+        scalars, cycle, c_label, picks, n_i=n_i, irreps=irreps, owns=low + halves * (irreps + 1), k_pairs=kappas // 2
+    )
 
     most = min(vmax, -(-vmax // a_local) * a_part)
     window = min(-(-(most + 15) // 16) * 16, n_fold * a_part)
     coded = grouped_product(
-        scalars, lhs, blocks, n_fold, bounds=n_i + irreps + j_local + 2, irreps=irreps, halves=halves, window=window
+        scalars, lhs, blocks, n_fold, bounds=low, irreps=irreps, halves=halves, window=window
     )
     coded = lax.all_to_all(coded, "fold", split_axis=0, concat_axis=0, tiled=True).astype(F32)
     shares = coded[:, :-8] * (jnp.exp2(coded[:, -8:-7] * 0.25) / TOP)

time: 151 us -> 156 us (1.033)
  waiting for transfers between devices: 30.9 us -> 42.1 us
  Pallas kernels: 45.2 us -> 39 us
  starting transfers between devices: 17 us -> 11.5 us
  other arithmetic: 6.24 us -> 8.69 us
  local copies, waits for them, and re-layouts: 17.2 us -> 18.9 us
    all_gather x1, waiting for transfers between devices: 4.63 us -> 13.4 us  [body(): lhs = lax.all_gather(short, 'pair', axis=0)]
    pallas_call x2, Pallas kernels: 27.9 us -> 21.7 us  [the longest x1 17.5 us: class_blocks(): pl.pallas_call(functools.partial(block_kernel, n_i=n_i, irreps=irreps, ow...]
    all_to_all x1, starting transfers between devices: 12.4 us -> 6.94 us  [body(): lax.all_to_all(coded, 'fold', split_axis=0, concat_axis=0, tiled=True)]
    unnamed x5 -> x9, local copies, waits for them, and re-layouts: 0.01 us -> 4.19 us
    all_to_all x1, waiting for transfers between devices: 25.8 us -> 28.6 us  [body(): lax.all_to_all(coded, 'fold', split_axis=0, concat_axis=0, tiled=True)]
    xor x2, other arithmetic: 0.78 us -> 2.84 us  [body(): i_mine ^ occ[:, None] ^ a_mine[None, :]]
  transfers between devices with their start and end apart: 3 -> 3, of which waited for: 3 -> 2; matrix products, arithmetic and copies ran while one was open for 9% -> 11% of each run, Pallas kernels for 16% -> 11%
where the time goes in v7:
time: 156 us
  waiting for transfers between devices  42.1 us (27%)
  Pallas kernels  39 us (25%)
  blocking collectives  21.6 us (14%)
  local copies, waits for them, and re-layouts  18.9 us (12%)
  between operations  13.6 us (9%)
  starting transfers between devices  11.5 us (7%)
  other arithmetic  8.69 us (6%)
    all_to_all x1, waiting for transfers between devices, body(): lax.all_to_all(coded, 'fold', split_axis=0, concat_axis=0, tiled=True)  28.6 us
    all_to_all x1, blocking collectives, body(): lax.all_to_all(short, 'fold', split_axis=0, concat_axis=0, tiled=True)  21.6 us
    pallas_call x1, Pallas kernels, class_blocks(): pl.pallas_call(functools.partial(block_kernel, n_i=n_i, irreps=irreps, ow...  17.5 us
    pallas_call x1, Pallas kernels, grouped_product(): pl.pallas_call(functools.partial(grouped_kernel, bounds=bounds, irreps=ir...  13.6 us
    all_gather x1, waiting for transfers between devices, body(): lhs = lax.all_gather(short, 'pair', axis=0)  13.4 us
    transpose x1, local copies, waits for them, and re-layouts, body(): cycle_block.transpose(2, 1, 0, 3)  9.39 us
    all_to_all x1, starting transfers between devices, body(): lax.all_to_all(coded, 'fold', split_axis=0, concat_axis=0, tiled=True)  6.94 us
    all_to_all x1, starting transfers between devices, body(): lax.all_to_all(narrow, 'pair', split_axis=0, concat_axis=0, tiled=True)  4.55 us
  transfers between devices with their start and end apart: 3, of which 2 were waited for; matrix products, arithmetic and copies ran while one was open for 11% of the time, Pallas kernels for 11%

profile of v7, /device:TPU:0, one launch (start us, length us, event | category | flops | bytes accessed | tf_op | source)
XLA Modules:
  0.0 155.7 jit_solution(13418407372973485278)
XLA Ops:
  6.5 0.7 pad_add_fusion
  7.5 0.8 select_reduce_fusion.3
  8.3 0.6 dynamic_slice.22
  8.9 0.7 xor_reduce_fusion
  10.0 1.6 %copy-done = bf16[4,10,40,640]{3,2,1,0:T(8,128)(2,1)S(1)} copy-done((bf16[4,10,40,640]{3,2,1,0:T(8,128)(2,1)S(1)}, bf16[4,10,40,640]{3,2,1,0:T(8,128)(2,1)}, u32[]{:S(2)}) %copy-start) | copy-done | bytes 2048024
  11.6 4.3 %shard_map.64 = bf16[8,160,200]{2,1,0:T(8,128)(2,1)} custom-call(s32[14]{0:T(128)S(1)} %pad_add_fusion.1.scalars, bf16[4,10,40,640]{3,2,1,0:T(8,128)(2,1)S(1)} %copy-done, s32[40,1]{1,0:T(8,128)S(1)} %copy.28.a_label, s32[1,640]{1,0:T(1,128)S(1)} %get-tuple-element.18.label, bf16[160,640]{1,0:T(8,128)(2,1)S(1)} %fusion.3.to_place), custom_call_target="tpu_custom_call" | custom-call | flops 327680000 | bytes 3145728 | tf_op jit(solution)/shard_map/pallas_call | solution.py:157
  15.8 4.6 %all-to-all-start = ((bf16[8,160,200]{2,1,0:T(8,128)(2,1)}), bf16[8,160,200]{2,1,0:T(8,128)(2,1)S(1)}, u32[]{:S(2)}, u32[]{:S(2)}) async-start(bf16[8,160,200]{2,1,0:T(8,128)(2,1)} %shard_map.64), calls=%async_computation | async-start | bytes 1310720 | tf_op jit(solution)/shard_map/all_to_all | solution.py:279
  20.6 9.4 %copy.29 = bf16[2,80,40,640]{3,2,1,0:T(8,128)(2,1)} copy(bf16[2,80,40,640]{3,0,1,2:T(2,128)(2,1)} %bitcast.59) | data formatting | bytes 16384000 | tf_op jit(solution)/shard_map/transpose | solution.py:280
  30.1 1.2 xor.96
  31.9 0.5 compare_convert_fusion.picks
  32.4 2.2 %broadcast_xor_fusion.row_label = s32[8,200,1]{2,1,0:T(8,128)} fusion(s32[8,200,1]{2,1,0:T(8,128)} %xor.96, s32[200]{0:T(256)S(1)} %xor.93), kind=kLoop, calls=%fused_computation.6 | loop fusion | flops 1600 | bytes 13600 | tf_op jit(solution)/shard_map/xor | solution.py:288
  34.6 1.9 %and_convert_fusion.to_row = bf16[528,1664]{1,0:T(8,128)(2,1)} fusion(s32[1664]{0:T(1024)S(1)} %add_select_fusion, s32[1664]{0:T(1024)S(1)} %eq.140, s32[528]{0:T(1024)S(1)} %get-tuple-element.24, s32[528]{0:T(1024)S(1)} %get-tuple-element.25), kind=kLoop, calls=%fused_computation.1 | loop fusion | flops 3514368 | bytes 1774720 | tf_op jit(solution)/shard_map/convert_element_type | solution.py:295
  36.5 1.5 copy-done.1
  38.0 1.1 copy-done.2
  39.1 3.6 %shard_map.65 = bf16[16,20,880]{2,1,0:T(8,128)(2,1)S(1)} custom-call(bf16[8,160,200]{2,1,0:T(8,128)(2,1)S(1)} %all-to-all-done.x, bf16[160,640]{1,0:T(8,128)(2,1)S(1)} %fusion.3.to_place, s32[8,200,1]{2,1,0:T(8,128)S(1)} %copy-done.2, s32[1,640]{1,0:T(1,128)S(1)} %get-tuple-element.18.label, bf16[528,1664]{1,0:T(8,128)(2,1)S(1)} %copy-done.1), custom_call_target="tpu_custom_call" | custom-call | flops 1124597760 | bytes 3145728 | tf_op jit(solution)/shard_map/pallas_call | solution.py:204
  42.7 21.6 %all_to_all.15 = bf16[16,20,880]{2,1,0:T(8,128)(2,1)S(1)} all-to-all(bf16[16,20,880]{2,1,0:T(8,128)(2,1)S(1)} %shard_map.65), channel_id=1, replica_groups=mesh['pair'=8,'fold'=16] {'fold'}, dimensions={0} | all-to-all | bytes 1126400 | tf_op jit(solution)/shard_map/all_to_all | solution.py:297
  64.3 1.1 all_gather_reshape.3
  66.1 17.5 %shard_map.66.block = bf16[8,880,320]{2,1,0:T(8,128)(2,1)} custom-call(s32[72]{0:T(128)S(1)} %concatenate.10.scalars, bf16[2,40,80,640]{3,2,1,0:T(8,128)(2,1)} %bitcast.58, bf16[80,640]{1,0:T(8,128)(2,1)S(1)} %broadcast_in_dim.126.c_label, bf16[8,640,160]{2,1,0:T(8,128)(2,1)S(1)} %compare_convert_fusion.picks), custom_call_target="tpu_custom_call" | custom-call | flops 2883584000 | bytes 14680064 | tf_op jit(solution)/shard_map/pallas_call | solution.py:84
  83.6 13.4 %all-gather.2.cloned.1.call-done.lhs = bf16[8,320,880]{2,1,0:T(8,128)(2,1)} async-done(((bf16[1,320,880]{2,1,0:T(8,128)(2,1)}), bf16[8,320,880]{2,1,0:T(8,128)(2,1)}) %all-gather.2.cloned.1.call-update) | async-done | bytes 4505616 | tf_op jit(solution)/shard_map/all_gather | solution.py:299
  97.1 13.6 %shard_map.67 = s16[16,88,640]{2,1,0:T(8,128)(2,1)} custom-call(s32[72]{0:T(128)S(1)} %concatenate.10.scalars, bf16[8,320,880]{2,1,0:T(8,128)(2,1)} %all-gather.2.cloned.1.call-done.lhs, bf16[8,880,320]{2,1,0:T(8,128)(2,1)} %shard_map.66.block), custom_call_target="tpu_custom_call" | custom-call | flops 3460300800 | bytes 13631488 | tf_op jit(solution)/shard_map/pallas_call | solution.py:229
  110.7 6.9 %all-to-all-start.2 = ((s16[16,88,640]{2,1,0:T(8,128)(2,1)}), s16[16,88,640]{2,1,0:T(8,128)(2,1)S(1)}, u32[]{:S(2)}, u32[]{:S(2)}) async-start(s16[16,88,640]{2,1,0:T(8,128)(2,1)} %shard_map.67), calls=%async_computation.2 | async-start | bytes 3604480 | tf_op jit(solution)/shard_map/all_to_all | solution.py:315
  117.8 28.6 %all-to-all-done.2 = s16[16,88,640]{2,1,0:T(8,128)(2,1)S(1)} async-done(((s16[16,88,640]{2,1,0:T(8,128)(2,1)}), s16[16,88,640]{2,1,0:T(8,128)(2,1)S(1)}, u32[]{:S(2)}, u32[]{:S(2)}) %all-to-all-start.2) | async-done | bytes 1802272 | tf_op jit(solution)/shard_map/all_to_all | solution.py:315
  146.4 0.5 convert_element_type.44
  147.8 1.1 copy.34
  (52 shorter events, 3.3 us)
Async XLA Ops:
  10.0 1.6 %copy-start = (bf16[4,10,40,640]{3,2,1,0:T(8,128)(2,1)S(1)}, bf16[4,10,40,640]{3,2,1,0:T(8,128)(2,1)}, u32[]{:S(2)}) copy-start(bf16[4,10,40,640]{3,2,1,0:T(8,128)(2,1)} %x.5) | copy-start | bytes 6144004
  15.8 20.7 %all-to-all-start = ((bf16[8,160,200]{2,1,0:T(8,128)(2,1)}), bf16[8,160,200]{2,1,0:T(8,128)(2,1)S(1)}, u32[]{:S(2)}, u32[]{:S(2)}) async-start(bf16[8,160,200]{2,1,0:T(8,128)(2,1)} %shard_map.64), calls=%async_computation | async-start | bytes 1310720 | tf_op jit(solution)/shard_map/all_to_all | solution.py:279
  20.4 76.7 %all-gather.2.cloned.1.call-start = ((), (), s32[]{:S(2)}) async-start(), calls=%async_computation.3 | async-start | bytes 5160960 | tf_op jit(solution)/shard_map/all_gather | solution.py:299
  36.5 1.5 copy-start.1
  38.0 1.1 copy-start.2
  39.1 26.4 %copy-start.3 = (s32[16]{0:T(128)S(1)}, s32[16]{0:T(128)}, u32[]{:S(2)}) copy-start(s32[16]{0:T(128)} %param.11) | copy-start | bytes 196
  110.7 35.7 %all-to-all-start.2 = ((s16[16,88,640]{2,1,0:T(8,128)(2,1)}), s16[16,88,640]{2,1,0:T(8,128)(2,1)S(1)}, u32[]{:S(2)}, u32[]{:S(2)}) async-start(s16[16,88,640]{2,1,0:T(8,128)(2,1)} %shard_map.67), calls=%async_computation.2 | async-start | bytes 3604480 | tf_op jit(solution)/shard_map/all_to_all | solution.py:315
Sparse Core Ops, SparseCore 0:
  65.5 31.4 all-gather.1

commit v8 on v7

--- a/solution.py
+++ b/solution.py
@@ -98,8 +98,35 @@
     )(scalars, cycle, c_label, picks)
 
 
-def grouped_kernel(scalars, lhs, block, out, rows, total, packed, *, bounds, irreps, halves, window):
+def gather_pieces(v, n_pair):
+    def send(value, step):
+        return lax.ppermute(value, "pair", [(p, (p + step) % n_pair) for p in range(n_pair)])
+
+    half = v.shape[0] // 2
+    up, down = send(v, 2), send(v, -2)
+    far_up, far_down = send(up[:half], 2), send(down[half:], -2)
+    pieces = [v, up, down, far_up, far_down]
+    return pieces + [lax.ppermute(p, "pair", [(q, q ^ 1) for q in range(n_pair)]) for p in pieces]
+
+
+def grouped_kernel(scalars, *refs, bounds, irreps, halves, window, me):
+    pieces, (block, out, lhs, rows, total, packed, sems) = refs[:10], refs[10:]
     step = pl.program_id(0)
+
+    @pl.when(step == 0)
+    def _():
+        y, core = scalars[me] // 2, scalars[me] % 2
+        half = lhs.shape[1] // 2
+        copies = []
+        for n, piece in enumerate(pieces):
+            away = (0, -1, 1, 2, 2)[n % 5]
+            first = half if n % 5 == 4 else 0
+            g = lax.rem(y + away + 4, 4) * 2 + (core if n < 5 else 1 - core)
+            copies.append(pltpu.make_async_copy(piece, lhs.at[g, pl.ds(first, piece.shape[0]), :], sems.at[n]))
+            copies[-1].start()
+        for copy in copies:
+            copy.wait()
+
     groups, n_rows, _ = lhs.shape
     n_i, width = groups // halves, block.shape[2]
     spans = []
@@ -220,33 +247,36 @@
     return pl.BlockSpec(shape, lambda r, s: (0,) * len(shape))
 
 
-def grouped_product(scalars, lhs, block, n_fold, *, bounds, irreps, halves, window):
-    groups, n_rows, depth = lhs.shape
+def grouped_product(scalars, pieces, block, n_fold, groups, *, bounds, irreps, halves, window, me):
+    n_rows, depth = pieces[0].shape
     width = block.shape[2]
     n_i = groups // halves
     share = (n_i * n_rows // n_fold, halves * width)
     shape = (n_fold, share[0] + 8, share[1])
     return pl.pallas_call(
         functools.partial(
-            grouped_kernel, bounds=bounds, irreps=irreps, halves=halves, window=window
+            grouped_kernel, bounds=bounds, irreps=irreps, halves=halves, window=window, me=me
         ),
         out_shape=jax.ShapeDtypeStruct(shape, jnp.int16),
         grid_spec=pltpu.PrefetchScalarGridSpec(
             num_scalar_prefetch=1,
             grid=(irreps,),
-            in_specs=[whole(lhs.shape), pl.BlockSpec((1, depth, width), lambda r, s: (r, 0, 0))],
+            in_specs=[pl.BlockSpec(memory_space=pl.ANY)] * len(pieces)
+            + [pl.BlockSpec((1, depth, width), lambda r, s: (r, 0, 0))],
             out_specs=whole(shape),
             scratch_shapes=[
+                pltpu.VMEM((groups, n_rows, depth), BF16),
                 pltpu.VMEM((groups * window, depth), BF16),
                 pltpu.VMEM((groups, n_rows, width), F32),
                 pltpu.VMEM(share, F32),
+                pltpu.SemaphoreType.DMA((len(pieces),)),
             ],
         ),
         compiler_params=pltpu.CompilerParams(vmem_limit_bytes=48 * 2**20),
         cost_estimate=pl.CostEstimate(
             flops=2 * irreps * groups * window * depth * width, bytes_accessed=13 * 2**20, transcendentals=0
         ),
-    )(scalars, lhs, block)
+    )(scalars, *pieces, block)
 
 
 def body(amplitudes, cycle_block, occ_sizes, vir_sizes, window_i, window_occ):
@@ -278,10 +308,7 @@
     )
     narrow = lax.all_to_all(narrow, "pair", split_axis=0, concat_axis=0, tiled=True)
     cycle = cycle_block.transpose(2, 1, 0, 3).reshape(j_local, occ_total // 2, 2 * c_local, vir_total)
-    code = (vir * vmax + vir_place)[None, :, None]
-    spots = jnp.arange(irreps * vmax, dtype=jnp.int32).reshape(irreps, 1, vmax)
-    picks = (code == spots).astype(BF16)
-    narrow, cycle, picks = lax.optimization_barrier((narrow, cycle, picks))
+    narrow, cycle = lax.optimization_barrier((narrow, cycle))
 
     i_mine = lax.dynamic_index_in_dim(i_labels, pair // halves, keepdims=False)
     a_mine = lax.dynamic_slice_in_dim(vir, fold * a_local + (pair % halves) * a_part, a_part)
@@ -295,22 +322,28 @@
     to_row = ((row // a_rows == k_kappa) & (row % a_rows == column)).astype(BF16)
     short = narrow_k(narrow, to_place, x, vir[None, :], to_row, n_fold, a_part, c_local)
     short = lax.all_to_all(short, "fold", split_axis=0, concat_axis=0, tiled=True)
-    short = short.reshape(n_fold * a_part, kappas * c_local)
-    lhs = lax.all_gather(short, "pair", axis=0)
-
+
+    code = (vir * vmax + vir_place)[None, :, None]
+    spots = jnp.arange(irreps * vmax, dtype=jnp.int32).reshape(irreps, 1, vmax)
+    picks = (code == spots).astype(BF16)
     inside = starts % a_local
     bounds = [starts // a_local * a_part + jnp.clip(inside - h * a_part, 0, a_part) for h in range(halves)]
-    scalars = jnp.concatenate([i_labels, k_from // 2, j_labels] + bounds + [own_vir]).astype(jnp.int32)
+    scalars = jnp.concatenate([i_labels, k_from // 2, j_labels] + bounds + [own_vir, pair[None]]).astype(jnp.int32)
     low = n_i + irreps + j_local
+    me = low + halves * (irreps + 1) + c_local
     c_label = jnp.broadcast_to(jnp.tile(own_vir.astype(F32), 2)[:, None], (2 * c_local, vir_total)).astype(BF16)
     blocks = class_blocks(
         scalars, cycle, c_label, picks, n_i=n_i, irreps=irreps, owns=low + halves * (irreps + 1), k_pairs=kappas // 2
     )
+    short, blocks = lax.optimization_barrier((short, blocks))
+
+    short = short.reshape(n_fold * a_part, kappas * c_local)
+    lhs = gather_pieces(short, n_pair)
 
     most = min(vmax, -(-vmax // a_local) * a_part)
     window = min(-(-(most + 15) // 16) * 16, n_fold * a_part)
     coded = grouped_product(
-        scalars, lhs, blocks, n_fold, bounds=low, irreps=irreps, halves=halves, window=window
+        scalars, lhs, blocks, n_fold, n_pair, bounds=low, irreps=irreps, halves=halves, window=window, me=me
     )
     coded = lax.all_to_all(coded, "fold", split_axis=0, concat_axis=0, tiled=True).astype(F32)
     shares = coded[:, :-8] * (jnp.exp2(coded[:, -8:-7] * 0.25) / TOP)

time: 156 us -> 138 us (0.88)
  blocking collectives: 21.6 us -> 0 us
  starting transfers between devices: 11.5 us -> 28.2 us
  between operations: 13.6 us -> 0.27 us
  waiting for transfers between devices: 42.1 us -> 50.1 us
  local copies, waits for them, and re-layouts: 18.9 us -> 14.7 us
  other arithmetic: 8.69 us -> 5.39 us
    ppermute x0 -> x9, waiting for transfers between devices: none -> 21.9 us  [the longest x4 20.3 us: send(): lax.ppermute(value, 'pair', [(p, (p + step) % n_pair) for p in range(n_pa...]
    all_to_all x1 -> x0, blocking collectives: 21.6 us -> none  [body(): lax.all_to_all(short, 'fold', split_axis=0, concat_axis=0, tiled=True)]
    all_gather x1 -> x0, waiting for transfers between devices: 13.4 us -> none  [body(): lhs = lax.all_gather(short, 'pair', axis=0)]
    ppermute x0 -> x9, starting transfers between devices: none -> 7.91 us  [the longest x4 7.32 us: send(): lax.ppermute(value, 'pair', [(p, (p + step) % n_pair) for p in range(n_pa...]
    all_to_all x0 -> x1, starting transfers between devices: none -> 7.88 us  [body(): lax.all_to_all(short, 'fold', split_axis=0, concat_axis=0, tiled=True)]
    unnamed x9 -> x5, local copies, waits for them, and re-layouts: 4.19 us -> 1.58 us
    xor x2, other arithmetic: 2.84 us -> 0.82 us  [body(): i_mine ^ occ[:, None] ^ a_mine[None, :]]
  transfers between devices with their start and end apart: 3 -> 12, of which waited for: 2 -> 5; matrix products, arithmetic and copies ran while one was open for 11% -> 9% of each run, Pallas kernels for 11% -> 13%
where the time goes in v8:
time: 138 us
  waiting for transfers between devices  50.1 us (36%)
  Pallas kernels  39.4 us (29%)
  starting transfers between devices  28.2 us (20%)
  local copies, waits for them, and re-layouts  14.7 us (11%)
  other arithmetic  5.39 us (4%)
    all_to_all x1, waiting for transfers between devices, body(): lax.all_to_all(coded, 'fold', split_axis=0, concat_axis=0, tiled=True)  28.2 us
    ppermute x4, waiting for transfers between devices, send(): lax.ppermute(value, 'pair', [(p, (p + step) % n_pair) for p in range(n_pa...  20.3 us
    pallas_call x1, Pallas kernels, class_blocks(): pl.pallas_call(functools.partial(block_kernel, n_i=n_i, irreps=irreps, ow...  17.4 us
    pallas_call x1, Pallas kernels, grouped_product(): pl.pallas_call(functools.partial(grouped_kernel, bounds=bounds, irreps=ir...  13.3 us
    transpose x1, local copies, waits for them, and re-layouts, body(): cycle_block.transpose(2, 1, 0, 3)  9.39 us
    all_to_all x1, starting transfers between devices, body(): lax.all_to_all(short, 'fold', split_axis=0, concat_axis=0, tiled=True)  7.88 us
    all_to_all x1, starting transfers between devices, body(): lax.all_to_all(coded, 'fold', split_axis=0, concat_axis=0, tiled=True)  7.87 us
    ppermute x4, starting transfers between devices, send(): lax.ppermute(value, 'pair', [(p, (p + step) % n_pair) for p in range(n_pa...  7.32 us
  transfers between devices with their start and end apart: 12, of which 5 were waited for; matrix products, arithmetic and copies ran while one was open for 9% of the time, Pallas kernels for 13%

profile of v8, /device:TPU:0, one launch (start us, length us, event | category | flops | bytes accessed | tf_op | source)
XLA Modules:
  0.0 138.4 jit_solution(11845836584028403021)
XLA Ops:
  0.0 0.7 pad_add_fusion
  1.0 0.8 select_reduce_fusion.3
  1.8 0.7 dynamic_slice.22
  2.5 0.7 xor_reduce_fusion
  3.6 1.6 %copy-done = bf16[4,10,40,640]{3,2,1,0:T(8,128)(2,1)S(1)} copy-done((bf16[4,10,40,640]{3,2,1,0:T(8,128)(2,1)S(1)}, bf16[4,10,40,640]{3,2,1,0:T(8,128)(2,1)}, u32[]{:S(2)}) %copy-start) | copy-done | bytes 2048024
  5.2 4.3 %shard_map.64 = bf16[8,160,200]{2,1,0:T(8,128)(2,1)} custom-call(s32[14]{0:T(128)S(1)} %pad_add_fusion.1.scalars, bf16[4,10,40,640]{3,2,1,0:T(8,128)(2,1)S(1)} %copy-done, s32[40,1]{1,0:T(8,128)S(1)} %copy.22.a_label, s32[1,640]{1,0:T(1,128)S(1)} %get-tuple-element.20.label, bf16[160,640]{1,0:T(8,128)(2,1)S(1)} %fusion.3.to_place), custom_call_target="tpu_custom_call" | custom-call | flops 327680000 | bytes 3145728 | tf_op jit(solution)/shard_map/pallas_call | solution.py:184
  9.4 4.6 %all-to-all-start = ((bf16[8,160,200]{2,1,0:T(8,128)(2,1)}), bf16[8,160,200]{2,1,0:T(8,128)(2,1)S(1)}, u32[]{:S(2)}, u32[]{:S(2)}) async-start(bf16[8,160,200]{2,1,0:T(8,128)(2,1)} %shard_map.64), calls=%async_computation | async-start | bytes 1310720 | tf_op jit(solution)/shard_map/all_to_all | solution.py:309
  15.7 9.4 %copy.23 = bf16[2,80,40,640]{3,2,1,0:T(8,128)(2,1)} copy(bf16[2,80,40,640]{3,0,1,2:T(2,128)(2,1)} %bitcast.60) | data formatting | bytes 16384000 | tf_op jit(solution)/shard_map/transpose | solution.py:310
  25.3 0.6 and_convert_fusion.to_row
  25.9 4.4 %shard_map.65 = bf16[16,20,880]{2,1,0:T(8,128)(2,1)} custom-call(bf16[8,160,200]{2,1,0:T(8,128)(2,1)S(1)} %all-to-all-done.x, bf16[160,640]{1,0:T(8,128)(2,1)S(1)} %fusion.3.to_place, s32[8,200,1]{2,1,0:T(8,128)S(1)} %broadcast_xor_fusion.row_label, s32[1,640]{1,0:T(1,128)S(1)} %get-tuple-element.20.label, bf16[528,1664]{1,0:T(8,128)(2,1)S(1)} %and_convert_fusion.to_row), custom_call_target="tpu_custom_call" | custom-call | flops 1124597760 | bytes 3145728 | tf_op jit(solution)/shard_map/pallas_call | solution.py:231
  30.4 7.9 %all-to-all-start.1 = ((bf16[16,20,880]{2,1,0:T(8,128)(2,1)}), bf16[16,20,880]{2,1,0:T(8,128)(2,1)S(1)}, u32[]{:S(2)}, u32[]{:S(2)}) async-start(bf16[16,20,880]{2,1,0:T(8,128)(2,1)} %shard_map.65), calls=%async_computation.1 | async-start | bytes 1376256 | tf_op jit(solution)/shard_map/all_to_all | solution.py:324
  38.3 0.5 compare_convert_fusion.picks
  38.8 17.4 %shard_map.66.refs_10_ = bf16[8,880,320]{2,1,0:T(8,128)(2,1)} custom-call(s32[73]{0:T(128)S(1)} %concatenate.10.scalars, bf16[2,40,80,640]{3,2,1,0:T(8,128)(2,1)} %bitcast.59, bf16[80,640]{1,0:T(8,128)(2,1)S(1)} %broadcast_in_dim.130.c_label, bf16[8,640,160]{2,1,0:T(8,128)(2,1)S(1)} %compare_convert_fusion.picks), custom_call_target="tpu_custom_call" | custom-call | flops 2883584000 | bytes 14680064 | tf_op jit(solution)/shard_map/pallas_call | solution.py:84
  56.5 3.3 %collective-permute-start.1 = (bf16[320,880]{1,0:T(8,128)(2,1)S(1)}, bf16[320,880]{1,0:T(8,128)(2,1)S(1)}, u32[]{:S(2)}, u32[]{:S(2)}) collective-permute-start(bf16[320,880]{1,0:T(8,128)(2,1)S(1)} %reshape.242.refs_0_), channel_id=1, source_target_pairs={{0,96},{16,112},{32,0},{48,16},{64,32},{80,48},{96,64},{112,80},{1... | collective-permute-start | bytes 1689608 | tf_op jit(solution)/shard_map/ppermute | solution.py:103
  59.8 12.3 %collective-permute-done.1.refs_2_ = bf16[320,880]{1,0:T(8,128)(2,1)S(1)} collective-permute-done((bf16[320,880]{1,0:T(8,128)(2,1)S(1)}, bf16[320,880]{1,0:T(8,128)(2,1)S(1)}, u32[]{:S(2)}, u32[]{:S(2)}) %collective-permute-start.1) | collective-permute-done | bytes 563232 | tf_op jit(solution)/shard_map/ppermute | solution.py:103
  72.1 3.8 %collective-permute-start.3 = (bf16[160,880]{1,0:T(8,128)(2,1)S(1)}, bf16[160,880]{1,0:T(8,128)(2,1)S(1)}, u32[]{:S(2)}, u32[]{:S(2)}) collective-permute-start(bf16[160,880]{1,0:T(8,128)(2,1)S(1)} %slice.46), channel_id=1, source_target_pairs={{0,96},{16,112},{32,0},{48,16},{64,32},{80,48},{96,64},{112,80},{1... | collective-permute-start | bytes 844808 | tf_op jit(solution)/shard_map/ppermute | solution.py:103
  76.3 0.5 collective-permute-start.5
  76.8 4.4 %collective-permute-done.3.refs_4_ = bf16[160,880]{1,0:T(8,128)(2,1)S(1)} collective-permute-done((bf16[160,880]{1,0:T(8,128)(2,1)S(1)}, bf16[160,880]{1,0:T(8,128)(2,1)S(1)}, u32[]{:S(2)}, u32[]{:S(2)}) %collective-permute-start.3) | collective-permute-done | bytes 281632 | tf_op jit(solution)/shard_map/ppermute | solution.py:103
  81.1 3.7 %collective-permute-done.2.refs_3_ = bf16[160,880]{1,0:T(8,128)(2,1)S(1)} collective-permute-done((bf16[160,880]{1,0:T(8,128)(2,1)S(1)}, bf16[160,880]{1,0:T(8,128)(2,1)S(1)}, u32[]{:S(2)}, u32[]{:S(2)}) %collective-permute-start.2) | collective-permute-done | bytes 281632 | tf_op jit(solution)/shard_map/ppermute | solution.py:103
  84.8 1.5 %collective-permute-done.7.refs_8_ = bf16[160,880]{1,0:T(8,128)(2,1)S(1)} collective-permute-done((bf16[160,880]{1,0:T(8,128)(2,1)S(1)}, bf16[160,880]{1,0:T(8,128)(2,1)S(1)}, u32[]{:S(2)}, u32[]{:S(2)}) %collective-permute-start.7) | collective-permute-done | bytes 281632 | tf_op jit(solution)/shard_map/ppermute | solution.py:109
  86.4 13.3 %shard_map.67 = s16[16,88,640]{2,1,0:T(8,128)(2,1)} custom-call(s32[73]{0:T(128)S(1)} %concatenate.10.scalars, bf16[320,880]{1,0:T(8,128)(2,1)S(1)} %reshape.242.refs_0_, bf16[320,880]{1,0:T(8,128)(2,1)S(1)} %collective-permute-done.refs_1_, bf16[320,880]{1,0:T(8,128)(2,1)S(1)} %collective-permute-done.1.refs_2_, ...), custom_call_target="tpu_custom_call" | custom-call | flops 3460300800 | bytes 13631488 | tf_op jit(solution)/shard_map/pallas_call | solution.py:256
  99.7 7.9 %all-to-all-start.2 = ((s16[16,88,640]{2,1,0:T(8,128)(2,1)}), s16[16,88,640]{2,1,0:T(8,128)(2,1)S(1)}, u32[]{:S(2)}, u32[]{:S(2)}) async-start(s16[16,88,640]{2,1,0:T(8,128)(2,1)} %shard_map.67), calls=%async_computation.2 | async-start | bytes 3604480 | tf_op jit(solution)/shard_map/all_to_all | solution.py:348
  107.7 28.2 %all-to-all-done.2 = s16[16,88,640]{2,1,0:T(8,128)(2,1)S(1)} async-done(((s16[16,88,640]{2,1,0:T(8,128)(2,1)}), s16[16,88,640]{2,1,0:T(8,128)(2,1)S(1)}, u32[]{:S(2)}, u32[]{:S(2)}) %all-to-all-start.2) | async-done | bytes 1802272 | tf_op jit(solution)/shard_map/all_to_all | solution.py:348
  137.3 1.1 copy.28
  (66 shorter events, 4.8 us)
Async XLA Ops:
  0.0 14.3 %copy-start.1 = (s32[16]{0:T(128)S(1)}, s32[16]{0:T(128)}, u32[]{:S(2)}) copy-start(s32[16]{0:T(128)} %param.11) | copy-start | bytes 196
  3.6 1.6 %copy-start = (bf16[4,10,40,640]{3,2,1,0:T(8,128)(2,1)S(1)}, bf16[4,10,40,640]{3,2,1,0:T(8,128)(2,1)}, u32[]{:S(2)}) copy-start(bf16[4,10,40,640]{3,2,1,0:T(8,128)(2,1)} %x.5) | copy-start | bytes 6144004
  9.4 16.5 %all-to-all-start = ((bf16[8,160,200]{2,1,0:T(8,128)(2,1)}), bf16[8,160,200]{2,1,0:T(8,128)(2,1)S(1)}, u32[]{:S(2)}, u32[]{:S(2)}) async-start(bf16[8,160,200]{2,1,0:T(8,128)(2,1)} %shard_map.64), calls=%async_computation | async-start | bytes 1310720 | tf_op jit(solution)/shard_map/all_to_all | solution.py:309
  30.4 25.9 %all-to-all-start.1 = ((bf16[16,20,880]{2,1,0:T(8,128)(2,1)}), bf16[16,20,880]{2,1,0:T(8,128)(2,1)S(1)}, u32[]{:S(2)}, u32[]{:S(2)}) async-start(bf16[16,20,880]{2,1,0:T(8,128)(2,1)} %shard_map.65), calls=%async_computation.1 | async-start | bytes 1376256 | tf_op jit(solution)/shard_map/all_to_all | solution.py:324
  56.5 15.6 %collective-permute-start.1 = (bf16[320,880]{1,0:T(8,128)(2,1)S(1)}, bf16[320,880]{1,0:T(8,128)(2,1)S(1)}, u32[]{:S(2)}, u32[]{:S(2)}) collective-permute-start(bf16[320,880]{1,0:T(8,128)(2,1)S(1)} %reshape.242.refs_0_), channel_id=1, source_target_pairs={{0,96},{16,112},{32,0},{48,16},{64,32},{80,48},{96,64},{112,80},{1... | collective-permute-start | bytes 1689608 | tf_op jit(solution)/shard_map/ppermute | solution.py:103
  59.8 16.1 %collective-permute-start = (bf16[320,880]{1,0:T(8,128)(2,1)S(1)}, bf16[320,880]{1,0:T(8,128)(2,1)S(1)}, u32[]{:S(2)}, u32[]{:S(2)}) collective-permute-start(bf16[320,880]{1,0:T(8,128)(2,1)S(1)} %reshape.242.refs_0_), channel_id=1, source_target_pairs={{0,32},{16,48},{32,64},{48,80},{64,96},{80,112},{96,0},{112,16},{1... | collective-permute-start | bytes 1689608 | tf_op jit(solution)/shard_map/ppermute | solution.py:103
  59.8 25.0 %collective-permute-start.4 = (bf16[320,880]{1,0:T(8,128)(2,1)S(1)}, bf16[320,880]{1,0:T(8,128)(2,1)S(1)}, u32[]{:S(2)}, u32[]{:S(2)}) collective-permute-start(bf16[320,880]{1,0:T(8,128)(2,1)S(1)} %reshape.242.refs_0_), channel_id=1, source_target_pairs={{0,16},{16,0},{32,48},{48,32},{64,80},{80,64},{96,112},{112,96},{1... | collective-permute-start | bytes 1689608 | tf_op jit(solution)/shard_map/ppermute | solution.py:109
  72.1 9.0 %collective-permute-start.3 = (bf16[160,880]{1,0:T(8,128)(2,1)S(1)}, bf16[160,880]{1,0:T(8,128)(2,1)S(1)}, u32[]{:S(2)}, u32[]{:S(2)}) collective-permute-start(bf16[160,880]{1,0:T(8,128)(2,1)S(1)} %slice.46), channel_id=1, source_target_pairs={{0,96},{16,112},{32,0},{48,16},{64,32},{80,48},{96,64},{112,80},{1... | collective-permute-start | bytes 844808 | tf_op jit(solution)/shard_map/ppermute | solution.py:103
  75.9 8.9 %collective-permute-start.2 = (bf16[160,880]{1,0:T(8,128)(2,1)S(1)}, bf16[160,880]{1,0:T(8,128)(2,1)S(1)}, u32[]{:S(2)}, u32[]{:S(2)}) collective-permute-start(bf16[160,880]{1,0:T(8,128)(2,1)S(1)} %slice.45), channel_id=1, source_target_pairs={{0,32},{16,48},{32,64},{48,80},{64,96},{80,112},{96,0},{112,16},{1... | collective-permute-start | bytes 844808 | tf_op jit(solution)/shard_map/ppermute | solution.py:103
  76.2 8.7 %collective-permute-start.6 = (bf16[320,880]{1,0:T(8,128)(2,1)S(1)}, bf16[320,880]{1,0:T(8,128)(2,1)S(1)}, u32[]{:S(2)}, u32[]{:S(2)}) collective-permute-start(bf16[320,880]{1,0:T(8,128)(2,1)S(1)} %collective-permute-done.1.refs_2_), channel_id=1, source_target_pairs={{0,16},{16,0},{32,48},{48,32},{64,80},{80,64},{96,112},{112,96},{1... | collective-permute-start | bytes 1689608 | tf_op jit(solution)/shard_map/ppermute | solution.py:109
  76.3 10.1 %collective-permute-start.5 = (bf16[320,880]{1,0:T(8,128)(2,1)S(1)}, bf16[320,880]{1,0:T(8,128)(2,1)S(1)}, u32[]{:S(2)}, u32[]{:S(2)}) collective-permute-start(bf16[320,880]{1,0:T(8,128)(2,1)S(1)} %collective-permute-done.refs_1_), channel_id=1, source_target_pairs={{0,16},{16,0},{32,48},{48,32},{64,80},{80,64},{96,112},{112,96},{1... | collective-permute-start | bytes 1689608 | tf_op jit(solution)/shard_map/ppermute | solution.py:109
  81.1 3.7 %collective-permute-start.8 = (bf16[160,880]{1,0:T(8,128)(2,1)S(1)}, bf16[160,880]{1,0:T(8,128)(2,1)S(1)}, u32[]{:S(2)}, u32[]{:S(2)}) collective-permute-start(bf16[160,880]{1,0:T(8,128)(2,1)S(1)} %collective-permute-done.3.refs_4_), channel_id=1, source_target_pairs={{0,16},{16,0},{32,48},{48,32},{64,80},{80,64},{96,112},{112,96},{1... | collective-permute-start | bytes 844808 | tf_op jit(solution)/shard_map/ppermute | solution.py:109
  84.8 1.6 %collective-permute-start.7 = (bf16[160,880]{1,0:T(8,128)(2,1)S(1)}, bf16[160,880]{1,0:T(8,128)(2,1)S(1)}, u32[]{:S(2)}, u32[]{:S(2)}) collective-permute-start(bf16[160,880]{1,0:T(8,128)(2,1)S(1)} %collective-permute-done.2.refs_3_), channel_id=1, source_target_pairs={{0,16},{16,0},{32,48},{48,32},{64,80},{80,64},{96,112},{112,96},{1... | collective-permute-start | bytes 844808 | tf_op jit(solution)/shard_map/ppermute | solution.py:109
  99.7 36.3 %all-to-all-start.2 = ((s16[16,88,640]{2,1,0:T(8,128)(2,1)}), s16[16,88,640]{2,1,0:T(8,128)(2,1)S(1)}, u32[]{:S(2)}, u32[]{:S(2)}) async-start(s16[16,88,640]{2,1,0:T(8,128)(2,1)} %shard_map.67), calls=%async_computation.2 | async-start | bytes 3604480 | tf_op jit(solution)/shard_map/all_to_all | solution.py:348

commit v9 on v8

--- a/solution.py
+++ b/solution.py
@@ -49,8 +49,8 @@
     return spans
 
 
-def block_kernel(scalars, cycle, c_label, picks, out, chosen, *, n_i, irreps, owns):
-    step = pl.program_id(0)
+def block_kernel(scalars, cycle, c_label, picks, out, chosen, *, n_i, irreps, owns, first_class):
+    step = pl.program_id(0) + first_class
     n_j, _, pair_rows, vir_total = cycle.shape
     k_pairs, width = chosen.shape[1], picks.shape[2]
     for tile, runs in enumerate(tile_spans(pair_rows // 2)):
@@ -77,40 +77,40 @@
         out[0, :, j * width:(j + 1) * width] = narrow.astype(BF16)
 
 
-def class_blocks(scalars, cycle, c_label, picks, *, n_i, irreps, owns, k_pairs):
+def class_blocks(scalars, cycle, c_label, picks, first_class, *, n_i, irreps, owns, k_pairs):
     n_j, _, pair_rows, vir_total = cycle.shape
     width = picks.shape[2]
     depth = k_pairs * pair_rows
     return pl.pallas_call(
-        functools.partial(block_kernel, n_i=n_i, irreps=irreps, owns=owns),
-        out_shape=jax.ShapeDtypeStruct((irreps, depth, n_j * width), BF16),
+        functools.partial(block_kernel, n_i=n_i, irreps=irreps, owns=owns, first_class=first_class),
+        out_shape=jax.ShapeDtypeStruct((irreps // 2, depth, n_j * width), BF16),
         grid_spec=pltpu.PrefetchScalarGridSpec(
             num_scalar_prefetch=1,
-            grid=(irreps,),
+            grid=(irreps // 2,),
             in_specs=[whole(cycle.shape), whole(c_label.shape), whole(picks.shape)],
             out_specs=pl.BlockSpec((1, depth, n_j * width), lambda r, s: (r, 0, 0)),
             scratch_shapes=[pltpu.VMEM((n_j, k_pairs, pair_rows, vir_total), BF16)],
         ),
         compiler_params=pltpu.CompilerParams(vmem_limit_bytes=48 * 2**20),
         cost_estimate=pl.CostEstimate(
-            flops=2 * irreps * depth * n_j * vir_total * width, bytes_accessed=14 * 2**20, transcendentals=0
+            flops=irreps * depth * n_j * vir_total * width, bytes_accessed=11 * 2**20, transcendentals=0
         ),
     )(scalars, cycle, c_label, picks)
 
 
-def gather_pieces(v, n_pair):
+def gather_pieces(v, beside, n_pair):
     def send(value, step):
         return lax.ppermute(value, "pair", [(p, (p + step) % n_pair) for p in range(n_pair)])
 
     half = v.shape[0] // 2
-    up, down = send(v, 2), send(v, -2)
+    up, down, beside = lax.optimization_barrier((send(v, 2), send(v, -2), beside))
     far_up, far_down = send(up[:half], 2), send(down[half:], -2)
     pieces = [v, up, down, far_up, far_down]
-    return pieces + [lax.ppermute(p, "pair", [(q, q ^ 1) for q in range(n_pair)]) for p in pieces]
+    return pieces + [lax.ppermute(p, "pair", [(q, q ^ 1) for q in range(n_pair)]) for p in pieces], beside
 
 
 def grouped_kernel(scalars, *refs, bounds, irreps, halves, window, me):
-    pieces, (block, out, lhs, rows, total, packed, sems) = refs[:10], refs[10:]
+    pieces, (early, late, out, lhs, rows, total, packed, block, sems) = refs[:10], refs[10:]
     step = pl.program_id(0)
 
     @pl.when(step == 0)
@@ -128,7 +128,16 @@
             copy.wait()
 
     groups, n_rows, _ = lhs.shape
-    n_i, width = groups // halves, block.shape[2]
+    n_i, width = groups // halves, block.shape[1]
+
+    @pl.when(step < irreps // 2)
+    def _():
+        block[...] = early[0]
+
+    @pl.when(step >= irreps // 2)
+    def _():
+        block[...] = late[0]
+
     spans = []
     for g in range(groups):
         at = bounds + (g % halves) * (irreps + 1) + (step ^ scalars[g // halves])
@@ -136,7 +145,7 @@
         base = pl.multiple_of(jnp.minimum(low // 16 * 16, n_rows - window), 16)
         rows[g * window:(g + 1) * window, :] = lhs[g, pl.ds(base, window), :]
         spans.append((low, high, base))
-    product = jnp.dot(rows[...], block[0], preferred_element_type=F32)
+    product = jnp.dot(rows[...], block[...], preferred_element_type=F32)
     for g, (low, high, base) in enumerate(spans):
         piece = product[g * window:(g + 1) * window]
         row = base + lax.broadcasted_iota(jnp.int32, piece.shape, 0)
@@ -196,7 +205,7 @@
             out_specs=pl.BlockSpec((halves, width, rows // halves), lambda i, s: (i, 0, 0)),
             scratch_shapes=[pltpu.VMEM((rows, vir_total), F32), pltpu.VMEM((width, rows // halves), F32)],
         ),
-        compiler_params=pltpu.CompilerParams(vmem_limit_bytes=32 * 2**20),
+        compiler_params=pltpu.CompilerParams(vmem_limit_bytes=60 * 2**20),
         cost_estimate=pl.CostEstimate(
             flops=2 * x.size * width, bytes_accessed=3 * 2**20, transcendentals=0
         ),
@@ -247,9 +256,9 @@
     return pl.BlockSpec(shape, lambda r, s: (0,) * len(shape))
 
 
-def grouped_product(scalars, pieces, block, n_fold, groups, *, bounds, irreps, halves, window, me):
+def grouped_product(scalars, pieces, early, late, n_fold, groups, *, bounds, irreps, halves, window, me):
     n_rows, depth = pieces[0].shape
-    width = block.shape[2]
+    width, half = early.shape[2], early.shape[0]
     n_i = groups // halves
     share = (n_i * n_rows // n_fold, halves * width)
     shape = (n_fold, share[0] + 8, share[1])
@@ -262,13 +271,17 @@
             num_scalar_prefetch=1,
             grid=(irreps,),
             in_specs=[pl.BlockSpec(memory_space=pl.ANY)] * len(pieces)
-            + [pl.BlockSpec((1, depth, width), lambda r, s: (r, 0, 0))],
+            + [
+                pl.BlockSpec((1, depth, width), lambda r, s: (jnp.minimum(r, half - 1), 0, 0)),
+                pl.BlockSpec((1, depth, width), lambda r, s: (jnp.maximum(r - half, 0), 0, 0)),
+            ],
             out_specs=whole(shape),
             scratch_shapes=[
                 pltpu.VMEM((groups, n_rows, depth), BF16),
                 pltpu.VMEM((groups * window, depth), BF16),
                 pltpu.VMEM((groups, n_rows, width), F32),
                 pltpu.VMEM(share, F32),
+                pltpu.VMEM((depth, width), BF16),
                 pltpu.SemaphoreType.DMA((len(pieces),)),
             ],
         ),
@@ -276,7 +289,7 @@
         cost_estimate=pl.CostEstimate(
             flops=2 * irreps * groups * window * depth * width, bytes_accessed=13 * 2**20, transcendentals=0
         ),
-    )(scalars, *pieces, block)
+    )(scalars, *pieces, early, late)
 
 
 def body(amplitudes, cycle_block, occ_sizes, vir_sizes, window_i, window_occ):
@@ -332,18 +345,20 @@
     low = n_i + irreps + j_local
     me = low + halves * (irreps + 1) + c_local
     c_label = jnp.broadcast_to(jnp.tile(own_vir.astype(F32), 2)[:, None], (2 * c_local, vir_total)).astype(BF16)
-    blocks = class_blocks(
-        scalars, cycle, c_label, picks, n_i=n_i, irreps=irreps, owns=low + halves * (irreps + 1), k_pairs=kappas // 2
-    )
-    short, blocks = lax.optimization_barrier((short, blocks))
+    make_blocks = functools.partial(
+        class_blocks, n_i=n_i, irreps=irreps, owns=low + halves * (irreps + 1), k_pairs=kappas // 2
+    )
+    early = make_blocks(scalars, cycle, c_label, picks, 0)
+    short, early = lax.optimization_barrier((short, early))
+    late = make_blocks(scalars, cycle, c_label, picks, irreps // 2)
 
     short = short.reshape(n_fold * a_part, kappas * c_local)
-    lhs = gather_pieces(short, n_pair)
+    lhs, late = gather_pieces(short, late, n_pair)
 
     most = min(vmax, -(-vmax // a_local) * a_part)
     window = min(-(-(most + 15) // 16) * 16, n_fold * a_part)
     coded = grouped_product(
-        scalars, lhs, blocks, n_fold, n_pair, bounds=low, irreps=irreps, halves=halves, window=window, me=me
+        scalars, lhs, early, late, n_fold, n_pair, bounds=low, irreps=irreps, halves=halves, window=window, me=me
     )
     coded = lax.all_to_all(coded, "fold", split_axis=0, concat_axis=0, tiled=True).astype(F32)
     shares = coded[:, :-8] * (jnp.exp2(coded[:, -8:-7] * 0.25) / TOP)

time: 138 us -> 137 us (level); the launches traced: 138 us -> 135 us
  waiting for transfers between devices: 50.1 us -> 42.9 us
  starting transfers between devices: 28.2 us -> 23.4 us
  local copies, waits for them, and re-layouts: 14.7 us -> 18.7 us
  Pallas kernels: 39.4 us -> 43.1 us
    ppermute x4, waiting for transfers between devices: 20.3 us -> 10.9 us  [send(): lax.ppermute(value, 'pair', [(p, (p + step) % n_pair) for p in range(n_pa...]
    all_to_all x1, starting transfers between devices: 7.87 us -> 5.31 us  [body(): lax.all_to_all(coded, 'fold', split_axis=0, concat_axis=0, tiled=True)]
    all_to_all x1, waiting for transfers between devices: 0.01 us -> 2.22 us  [body(): lax.all_to_all(short, 'fold', split_axis=0, concat_axis=0, tiled=True)]
    ppermute x4, starting transfers between devices: 7.32 us -> 5.12 us  [send(): lax.ppermute(value, 'pair', [(p, (p + step) % n_pair) for p in range(n_pa...]
    unnamed x5 -> x13, local copies, waits for them, and re-layouts: 1.58 us -> 3.24 us
    pallas_call x1 -> x2, Pallas kernels: 17.4 us -> 19 us  [class_blocks(): pl.pallas_call(functools.partial(block_kernel, n_i=n_i, irreps=irreps, ow...]
    pallas_call x1, Pallas kernels: 4.26 us -> 5.88 us  [narrow_c(): pl.pallas_call(functools.partial(narrow_c_kernel, n_i=n_i, a_local=a_loca...]
  transfers between devices with their start and end apart: 12 -> 12, of which waited for: 5 -> 7; matrix products, arithmetic and copies ran while one was open for 9% -> 10% of each run, Pallas kernels for 13% -> 14%
where the time goes in v9:
time: 137 us; the launch traced here: 135 us
  Pallas kernels  43.1 us (31%)
  waiting for transfers between devices  42.9 us (31%)
  starting transfers between devices  23.4 us (17%)
  local copies, waits for them, and re-layouts  18.7 us (14%)
  other arithmetic  6.56 us (5%)
    all_to_all x1, waiting for transfers between devices, body(): lax.all_to_all(coded, 'fold', split_axis=0, concat_axis=0, tiled=True)  28.2 us
    pallas_call x2, Pallas kernels, class_blocks(): pl.pallas_call(functools.partial(block_kernel, n_i=n_i, irreps=irreps, ow...  19 us
    pallas_call x1, Pallas kernels, grouped_product(): pl.pallas_call(functools.partial(grouped_kernel, bounds=bounds, irreps=ir...  13.7 us
    ppermute x4, waiting for transfers between devices, send(): lax.ppermute(value, 'pair', [(p, (p + step) % n_pair) for p in range(n_pa...  10.9 us
    transpose x1, local copies, waits for them, and re-layouts, body(): cycle_block.transpose(2, 1, 0, 3)  9.39 us
    all_to_all x1, starting transfers between devices, body(): lax.all_to_all(short, 'fold', split_axis=0, concat_axis=0, tiled=True)  7.92 us
    pallas_call x1, Pallas kernels, narrow_c(): pl.pallas_call(functools.partial(narrow_c_kernel, n_i=n_i, a_local=a_loca...  5.88 us
    all_to_all x1, starting transfers between devices, body(): lax.all_to_all(coded, 'fold', split_axis=0, concat_axis=0, tiled=True)  5.31 us
  transfers between devices with their start and end apart: 12, of which 7 were waited for; matrix products, arithmetic and copies ran while one was open for 10% of the time, Pallas kernels for 14%

profile of v9, /device:TPU:0, one launch (start us, length us, event | category | flops | bytes accessed | tf_op | source)
XLA Modules:
  0.0 135.3 jit_solution(43528729973179145)
XLA Ops:
  1.0 0.8 select_reduce_fusion.3
  4.6 0.7 fusion.3.to_place
  5.3 5.9 %shard_map.64 = bf16[8,160,200]{2,1,0:T(8,128)(2,1)} custom-call(s32[14]{0:T(128)} %pad_add_fusion.1.scalars, bf16[4,10,40,640]{3,2,1,0:T(8,128)(2,1)} %x.5, s32[40,1]{1,0:T(8,128)} %copy.22.a_label, s32[1,640]{1,0:T(1,128)} %copy-done.3, bf16[160,640]{1,0:T(8,128)(2,1)} %fusion.3.to_place), custom_call_target="tpu_custom_call" | custom-call | flops 327680000 | bytes 3145728 | tf_op jit(solution)/shard_map/pallas_call | solution.py:193
  11.2 4.6 %all-to-all-start = ((bf16[8,160,200]{2,1,0:T(8,128)(2,1)}), bf16[8,160,200]{2,1,0:T(8,128)(2,1)S(1)}, u32[]{:S(2)}, u32[]{:S(2)}) async-start(bf16[8,160,200]{2,1,0:T(8,128)(2,1)} %shard_map.64), calls=%async_computation | async-start | bytes 1310720 | tf_op jit(solution)/shard_map/all_to_all | solution.py:322
  16.4 0.7 fusion.27
  18.1 9.4 %copy.23 = bf16[2,80,40,640]{3,2,1,0:T(8,128)(2,1)} copy(bf16[2,80,40,640]{3,0,1,2:T(2,128)(2,1)} %bitcast.61) | data formatting | bytes 16384000 | tf_op jit(solution)/shard_map/transpose | solution.py:323
  28.4 4.4 %shard_map.65 = bf16[16,20,880]{2,1,0:T(8,128)(2,1)} custom-call(bf16[8,160,200]{2,1,0:T(8,128)(2,1)S(1)} %all-to-all-done.x, bf16[160,640]{1,0:T(8,128)(2,1)S(1)} %copy-done.2, s32[8,200,1]{2,1,0:T(8,128)S(1)} %broadcast_xor_fusion.row_label, s32[1,640]{1,0:T(1,128)S(1)} %copy-done.4, bf16[528,1664]{1,0:T(8,128)(2,1)S(1)} %and_convert_fusion.to_row), custom_call_target="tpu_custom_call" | custom-call | flops 1124597760 | bytes 3145728 | tf_op jit(solution)/shard_map/pallas_call | solution.py:240
  32.9 7.9 %all-to-all-start.1 = ((bf16[16,20,880]{2,1,0:T(8,128)(2,1)}), bf16[16,20,880]{2,1,0:T(8,128)(2,1)}, u32[]{:S(2)}, u32[]{:S(2)}) async-start(bf16[16,20,880]{2,1,0:T(8,128)(2,1)} %shard_map.65), calls=%async_computation.1 | async-start | bytes 1376256 | tf_op jit(solution)/shard_map/all_to_all | solution.py:337
  41.4 9.6 %shard_map.66.refs_10_ = bf16[4,880,320]{2,1,0:T(8,128)(2,1)S(1)} custom-call(s32[73]{0:T(128)S(1)} %concatenate.10.scalars, bf16[2,40,80,640]{3,2,1,0:T(8,128)(2,1)} %bitcast.59, bf16[80,640]{1,0:T(8,128)(2,1)S(1)} %broadcast_in_dim.130.c_label, bf16[8,640,160]{2,1,0:T(8,128)(2,1)S(1)} %compare_convert_fusion.picks), custom_call_target="tpu_custom_call" | custom-call | flops 1441792000 | bytes 11534336 | tf_op jit(solution)/shard_map/pallas_call | solution.py:84
  51.0 1.6 %copy-done = bf16[4,880,320]{2,1,0:T(8,128)(2,1)} copy-done((bf16[4,880,320]{2,1,0:T(8,128)(2,1)}, bf16[4,880,320]{2,1,0:T(8,128)(2,1)S(1)}, u32[]{:S(2)}) %copy-start) | copy-done | bytes 2252824
  52.6 2.2 %all-to-all-done.1 = bf16[16,20,880]{2,1,0:T(8,128)(2,1)} async-done(((bf16[16,20,880]{2,1,0:T(8,128)(2,1)}), bf16[16,20,880]{2,1,0:T(8,128)(2,1)}, u32[]{:S(2)}, u32[]{:S(2)}) %all-to-all-start.1) | async-done | bytes 563232 | tf_op jit(solution)/shard_map/all_to_all | solution.py:337
  54.8 1.4 %reshape.242.refs_0_ = bf16[320,880]{1,0:T(8,128)(2,1)S(1)} reshape(bf16[16,20,880]{2,1,0:T(8,128)(2,1)} %all-to-all-done.1) | data formatting | bytes 1126400 | tf_op jit(solution)/shard_map/reshape | solution.py:355
  56.2 3.0 %collective-permute-start.1 = (bf16[320,880]{1,0:T(8,128)(2,1)S(1)}, bf16[320,880]{1,0:T(8,128)(2,1)S(1)}, u32[]{:S(2)}, u32[]{:S(2)}) collective-permute-start(bf16[320,880]{1,0:T(8,128)(2,1)S(1)} %reshape.242.refs_0_), channel_id=1, source_target_pairs={{0,96},{16,112},{32,0},{48,16},{64,32},{80,48},{96,64},{112,80},{1... | collective-permute-start | bytes 1689608 | tf_op jit(solution)/shard_map/ppermute | solution.py:103
  59.2 9.5 %shard_map.67.refs_11_ = bf16[4,880,320]{2,1,0:T(8,128)(2,1)S(1)} custom-call(s32[73]{0:T(128)S(1)} %concatenate.10.scalars, bf16[2,40,80,640]{3,2,1,0:T(8,128)(2,1)} %bitcast.60, bf16[80,640]{1,0:T(8,128)(2,1)S(1)} %broadcast_in_dim.130.c_label, bf16[8,640,160]{2,1,0:T(8,128)(2,1)S(1)} %compare_convert_fusion.picks), custom_call_target="tpu_custom_call" | custom-call | flops 1441792000 | bytes 11534336 | tf_op jit(solution)/shard_map/pallas_call | solution.py:84
  68.7 1.5 %copy-done.1 = bf16[4,880,320]{2,1,0:T(8,128)(2,1)} copy-done((bf16[4,880,320]{2,1,0:T(8,128)(2,1)}, bf16[4,880,320]{2,1,0:T(8,128)(2,1)S(1)}, u32[]{:S(2)}) %copy-start.1) | copy-done | bytes 2252824
  70.3 3.4 %collective-permute-done.refs_1_ = bf16[320,880]{1,0:T(8,128)(2,1)S(1)} collective-permute-done((bf16[320,880]{1,0:T(8,128)(2,1)S(1)}, bf16[320,880]{1,0:T(8,128)(2,1)S(1)}, u32[]{:S(2)}, u32[]{:S(2)}) %collective-permute-start) | collective-permute-done | bytes 563232 | tf_op jit(solution)/shard_map/ppermute | solution.py:103
  74.1 1.8 %collective-permute-start.2 = (bf16[160,880]{1,0:T(8,128)(2,1)S(1)}, bf16[160,880]{1,0:T(8,128)(2,1)S(1)}, u32[]{:S(2)}, u32[]{:S(2)}) collective-permute-start(bf16[160,880]{1,0:T(8,128)(2,1)S(1)} %slice.38), channel_id=1, source_target_pairs={{0,32},{16,48},{32,64},{48,80},{64,96},{80,112},{96,0},{112,16},{1... | collective-permute-start | bytes 844808 | tf_op jit(solution)/shard_map/ppermute | solution.py:103
  76.5 4.0 %collective-permute-done.3.refs_4_ = bf16[160,880]{1,0:T(8,128)(2,1)S(1)} collective-permute-done((bf16[160,880]{1,0:T(8,128)(2,1)S(1)}, bf16[160,880]{1,0:T(8,128)(2,1)S(1)}, u32[]{:S(2)}, u32[]{:S(2)}) %collective-permute-start.3) | collective-permute-done | bytes 281632 | tf_op jit(solution)/shard_map/ppermute | solution.py:103
  80.5 3.3 %collective-permute-done.2.refs_3_ = bf16[160,880]{1,0:T(8,128)(2,1)S(1)} collective-permute-done((bf16[160,880]{1,0:T(8,128)(2,1)S(1)}, bf16[160,880]{1,0:T(8,128)(2,1)S(1)}, u32[]{:S(2)}, u32[]{:S(2)}) %collective-permute-start.2) | collective-permute-done | bytes 281632 | tf_op jit(solution)/shard_map/ppermute | solution.py:103
  83.8 1.6 %collective-permute-done.7.refs_8_ = bf16[160,880]{1,0:T(8,128)(2,1)S(1)} collective-permute-done((bf16[160,880]{1,0:T(8,128)(2,1)S(1)}, bf16[160,880]{1,0:T(8,128)(2,1)S(1)}, u32[]{:S(2)}, u32[]{:S(2)}) %collective-permute-start.7) | collective-permute-done | bytes 281632 | tf_op jit(solution)/shard_map/ppermute | solution.py:109
  85.4 13.7 %shard_map.68 = s16[16,88,640]{2,1,0:T(8,128)(2,1)} custom-call(s32[73]{0:T(128)S(1)} %concatenate.10.scalars, bf16[320,880]{1,0:T(8,128)(2,1)S(1)} %reshape.242.refs_0_, bf16[320,880]{1,0:T(8,128)(2,1)S(1)} %collective-permute-done.refs_1_, bf16[320,880]{1,0:T(8,128)(2,1)S(1)} %collective-permute-done.1.refs_2_, ...), custom_call_target="tpu_custom_call" | custom-call | flops 3460300800 | bytes 13631488 | tf_op jit(solution)/shard_map/pallas_call | solution.py:265
  99.1 5.3 %all-to-all-start.2 = ((s16[16,88,640]{2,1,0:T(8,128)(2,1)}), s16[16,88,640]{2,1,0:T(8,128)(2,1)S(1)}, u32[]{:S(2)}, u32[]{:S(2)}) async-start(s16[16,88,640]{2,1,0:T(8,128)(2,1)} %shard_map.68), calls=%async_computation.2 | async-start | bytes 3604480 | tf_op jit(solution)/shard_map/all_to_all | solution.py:363
  104.5 28.2 %all-to-all-done.2 = s16[16,88,640]{2,1,0:T(8,128)(2,1)S(1)} async-done(((s16[16,88,640]{2,1,0:T(8,128)(2,1)}), s16[16,88,640]{2,1,0:T(8,128)(2,1)S(1)}, u32[]{:S(2)}, u32[]{:S(2)}) %all-to-all-start.2) | async-done | bytes 1802272 | tf_op jit(solution)/shard_map/all_to_all | solution.py:363
  134.2 1.1 copy.28
  (75 shorter events, 9.3 us)
Async XLA Ops:
  0.0 16.0 %copy-start.5 = (s32[16]{0:T(128)S(1)}, s32[16]{0:T(128)}, u32[]{:S(2)}) copy-start(s32[16]{0:T(128)} %param.11) | copy-start | bytes 196
  3.8 1.5 %copy-start.3 = (s32[1,640]{1,0:T(1,128)}, s32[1,640]{1,0:T(1,128)S(1)}, u32[]{:S(2)}) copy-start(s32[1,640]{1,0:T(1,128)S(1)} %get-tuple-element.26.label) | copy-start | bytes 7684
  11.2 17.2 %all-to-all-start = ((bf16[8,160,200]{2,1,0:T(8,128)(2,1)}), bf16[8,160,200]{2,1,0:T(8,128)(2,1)S(1)}, u32[]{:S(2)}, u32[]{:S(2)}) async-start(bf16[8,160,200]{2,1,0:T(8,128)(2,1)} %shard_map.64), calls=%async_computation | async-start | bytes 1310720 | tf_op jit(solution)/shard_map/all_to_all | solution.py:322
  27.5 0.9 copy-start.2
  27.5 0.9 copy-start.4
  32.9 21.9 %all-to-all-start.1 = ((bf16[16,20,880]{2,1,0:T(8,128)(2,1)}), bf16[16,20,880]{2,1,0:T(8,128)(2,1)}, u32[]{:S(2)}, u32[]{:S(2)}) async-start(bf16[16,20,880]{2,1,0:T(8,128)(2,1)} %shard_map.65), calls=%async_computation.1 | async-start | bytes 1376256 | tf_op jit(solution)/shard_map/all_to_all | solution.py:337
  51.0 1.6 %copy-start = (bf16[4,880,320]{2,1,0:T(8,128)(2,1)}, bf16[4,880,320]{2,1,0:T(8,128)(2,1)S(1)}, u32[]{:S(2)}) copy-start(bf16[4,880,320]{2,1,0:T(8,128)(2,1)S(1)} %shard_map.66.refs_10_) | copy-start | bytes 6758404
  56.2 14.1 %collective-permute-start.1 = (bf16[320,880]{1,0:T(8,128)(2,1)S(1)}, bf16[320,880]{1,0:T(8,128)(2,1)S(1)}, u32[]{:S(2)}, u32[]{:S(2)}) collective-permute-start(bf16[320,880]{1,0:T(8,128)(2,1)S(1)} %reshape.242.refs_0_), channel_id=1, source_target_pairs={{0,96},{16,112},{32,0},{48,16},{64,32},{80,48},{96,64},{112,80},{1... | collective-permute-start | bytes 1689608 | tf_op jit(solution)/shard_map/ppermute | solution.py:103
  59.2 14.6 %collective-permute-start = (bf16[320,880]{1,0:T(8,128)(2,1)S(1)}, bf16[320,880]{1,0:T(8,128)(2,1)S(1)}, u32[]{:S(2)}, u32[]{:S(2)}) collective-permute-start(bf16[320,880]{1,0:T(8,128)(2,1)S(1)} %reshape.242.refs_0_), channel_id=1, source_target_pairs={{0,32},{16,48},{32,64},{48,80},{64,96},{80,112},{96,0},{112,16},{1... | collective-permute-start | bytes 1689608 | tf_op jit(solution)/shard_map/ppermute | solution.py:103
  68.7 1.5 %copy-start.1 = (bf16[4,880,320]{2,1,0:T(8,128)(2,1)}, bf16[4,880,320]{2,1,0:T(8,128)(2,1)S(1)}, u32[]{:S(2)}) copy-start(bf16[4,880,320]{2,1,0:T(8,128)(2,1)S(1)} %shard_map.67.refs_11_) | copy-start | bytes 6758404
  70.2 13.6 %collective-permute-start.4 = (bf16[320,880]{1,0:T(8,128)(2,1)S(1)}, bf16[320,880]{1,0:T(8,128)(2,1)S(1)}, u32[]{:S(2)}, u32[]{:S(2)}) collective-permute-start(bf16[320,880]{1,0:T(8,128)(2,1)S(1)} %reshape.242.refs_0_), channel_id=1, source_target_pairs={{0,16},{16,0},{32,48},{48,32},{64,80},{80,64},{96,112},{112,96},{1... | collective-permute-start | bytes 1689608 | tf_op jit(solution)/shard_map/ppermute | solution.py:109
  73.8 6.7 %collective-permute-start.3 = (bf16[160,880]{1,0:T(8,128)(2,1)S(1)}, bf16[160,880]{1,0:T(8,128)(2,1)S(1)}, u32[]{:S(2)}, u32[]{:S(2)}) collective-permute-start(bf16[160,880]{1,0:T(8,128)(2,1)S(1)} %slice.39), channel_id=1, source_target_pairs={{0,96},{16,112},{32,0},{48,16},{64,32},{80,48},{96,64},{112,80},{1... | collective-permute-start | bytes 844808 | tf_op jit(solution)/shard_map/ppermute | solution.py:103
  74.1 9.6 %collective-permute-start.2 = (bf16[160,880]{1,0:T(8,128)(2,1)S(1)}, bf16[160,880]{1,0:T(8,128)(2,1)S(1)}, u32[]{:S(2)}, u32[]{:S(2)}) collective-permute-start(bf16[160,880]{1,0:T(8,128)(2,1)S(1)} %slice.38), channel_id=1, source_target_pairs={{0,32},{16,48},{32,64},{48,80},{64,96},{80,112},{96,0},{112,16},{1... | collective-permute-start | bytes 844808 | tf_op jit(solution)/shard_map/ppermute | solution.py:103
  76.0 9.4 %collective-permute-start.5 = (bf16[320,880]{1,0:T(8,128)(2,1)S(1)}, bf16[320,880]{1,0:T(8,128)(2,1)S(1)}, u32[]{:S(2)}, u32[]{:S(2)}) collective-permute-start(bf16[320,880]{1,0:T(8,128)(2,1)S(1)} %collective-permute-done.refs_1_), channel_id=1, source_target_pairs={{0,16},{16,0},{32,48},{48,32},{64,80},{80,64},{96,112},{112,96},{1... | collective-permute-start | bytes 1689608 | tf_op jit(solution)/shard_map/ppermute | solution.py:109
  76.0 9.4 %collective-permute-start.6 = (bf16[320,880]{1,0:T(8,128)(2,1)S(1)}, bf16[320,880]{1,0:T(8,128)(2,1)S(1)}, u32[]{:S(2)}, u32[]{:S(2)}) collective-permute-start(bf16[320,880]{1,0:T(8,128)(2,1)S(1)} %collective-permute-done.1.refs_2_), channel_id=1, source_target_pairs={{0,16},{16,0},{32,48},{48,32},{64,80},{80,64},{96,112},{112,96},{1... | collective-permute-start | bytes 1689608 | tf_op jit(solution)/shard_map/ppermute | solution.py:109
  80.5 3.3 %collective-permute-start.8 = (bf16[160,880]{1,0:T(8,128)(2,1)S(1)}, bf16[160,880]{1,0:T(8,128)(2,1)S(1)}, u32[]{:S(2)}, u32[]{:S(2)}) collective-permute-start(bf16[160,880]{1,0:T(8,128)(2,1)S(1)} %collective-permute-done.3.refs_4_), channel_id=1, source_target_pairs={{0,16},{16,0},{32,48},{48,32},{64,80},{80,64},{96,112},{112,96},{1... | collective-permute-start | bytes 844808 | tf_op jit(solution)/shard_map/ppermute | solution.py:109
  83.8 1.6 %collective-permute-start.7 = (bf16[160,880]{1,0:T(8,128)(2,1)S(1)}, bf16[160,880]{1,0:T(8,128)(2,1)S(1)}, u32[]{:S(2)}, u32[]{:S(2)}) collective-permute-start(bf16[160,880]{1,0:T(8,128)(2,1)S(1)} %collective-permute-done.2.refs_3_), channel_id=1, source_target_pairs={{0,16},{16,0},{32,48},{48,32},{64,80},{80,64},{96,112},{112,96},{1... | collective-permute-start | bytes 844808 | tf_op jit(solution)/shard_map/ppermute | solution.py:109
  99.1 33.7 %all-to-all-start.2 = ((s16[16,88,640]{2,1,0:T(8,128)(2,1)}), s16[16,88,640]{2,1,0:T(8,128)(2,1)S(1)}, u32[]{:S(2)}, u32[]{:S(2)}) async-start(s16[16,88,640]{2,1,0:T(8,128)(2,1)} %shard_map.68), calls=%async_computation.2 | async-start | bytes 3604480 | tf_op jit(solution)/shard_map/all_to_all | solution.py:363

commit v10 on v9

--- a/solution.py
+++ b/solution.py
@@ -91,7 +91,7 @@
             out_specs=pl.BlockSpec((1, depth, n_j * width), lambda r, s: (r, 0, 0)),
             scratch_shapes=[pltpu.VMEM((n_j, k_pairs, pair_rows, vir_total), BF16)],
         ),
-        compiler_params=pltpu.CompilerParams(vmem_limit_bytes=48 * 2**20),
+        compiler_params=pltpu.CompilerParams(vmem_limit_bytes=60 * 2**20),
         cost_estimate=pl.CostEstimate(
             flops=irreps * depth * n_j * vir_total * width, bytes_accessed=11 * 2**20, transcendentals=0
         ),
@@ -103,14 +103,17 @@
         return lax.ppermute(value, "pair", [(p, (p + step) % n_pair) for p in range(n_pair)])
 
     half = v.shape[0] // 2
-    up, down, beside = lax.optimization_barrier((send(v, 2), send(v, -2), beside))
-    far_up, far_down = send(up[:half], 2), send(down[half:], -2)
-    pieces = [v, up, down, far_up, far_down]
+    upper, lower = v[:half], v[half:]
+    up_first, down_first = send(upper, 2), send(lower, -2)
+    up_then, down_then = send(lower, 2), send(upper, -2)
+    up_first, down_first, beside = lax.optimization_barrier((up_first, down_first, beside))
+    far_up, far_down = send(up_first, 2), send(down_first, -2)
+    pieces = [v, up_first, up_then, down_then, down_first, far_up, far_down]
     return pieces + [lax.ppermute(p, "pair", [(q, q ^ 1) for q in range(n_pair)]) for p in pieces], beside
 
 
 def grouped_kernel(scalars, *refs, bounds, irreps, halves, window, me):
-    pieces, (early, late, out, lhs, rows, total, packed, block, sems) = refs[:10], refs[10:]
+    pieces, (early, late, out, lhs, rows, total, packed, block, sems) = refs[:14], refs[14:]
     step = pl.program_id(0)
 
     @pl.when(step == 0)
@@ -119,9 +122,9 @@
         half = lhs.shape[1] // 2
         copies = []
         for n, piece in enumerate(pieces):
-            away = (0, -1, 1, 2, 2)[n % 5]
-            first = half if n % 5 == 4 else 0
-            g = lax.rem(y + away + 4, 4) * 2 + (core if n < 5 else 1 - core)
+            away = (0, -1, -1, 1, 1, 2, 2)[n % 7]
+            first = half if n % 7 in (2, 4, 6) else 0
+            g = lax.rem(y + away + 4, 4) * 2 + (core if n < 7 else 1 - core)
             copies.append(pltpu.make_async_copy(piece, lhs.at[g, pl.ds(first, piece.shape[0]), :], sems.at[n]))
             copies[-1].start()
         for copy in copies:
@@ -205,7 +208,7 @@
             out_specs=pl.BlockSpec((halves, width, rows // halves), lambda i, s: (i, 0, 0)),
             scratch_shapes=[pltpu.VMEM((rows, vir_total), F32), pltpu.VMEM((width, rows // halves), F32)],
         ),
-        compiler_params=pltpu.CompilerParams(vmem_limit_bytes=60 * 2**20),
+        compiler_params=pltpu.CompilerParams(vmem_limit_bytes=32 * 2**20),
         cost_estimate=pl.CostEstimate(
             flops=2 * x.size * width, bytes_accessed=3 * 2**20, transcendentals=0
         ),

time: 137 us -> 136 us (level); the launches traced: 135 us -> 136 us
  starting transfers between devices: 23.4 us -> 31 us
  waiting for transfers between devices: 42.9 us -> 36.5 us
  local copies, waits for them, and re-layouts: 18.7 us -> 16.1 us
  Pallas kernels: 43.1 us -> 45.2 us
    ppermute x4 -> x6, waiting for transfers between devices: 10.9 us -> 6.82 us  [send(): lax.ppermute(value, 'pair', [(p, (p + step) % n_pair) for p in range(n_pa...]
    pallas_call x2, Pallas kernels: 19 us -> 22.7 us  [class_blocks(): pl.pallas_call(functools.partial(block_kernel, n_i=n_i, irreps=irreps, ow...]
    ppermute x4 -> x6, starting transfers between devices: 5.12 us -> 8.64 us  [send(): lax.ppermute(value, 'pair', [(p, (p + step) % n_pair) for p in range(n_pa...]
    all_to_all x1, starting transfers between devices: 5.31 us -> 8.1 us  [body(): lax.all_to_all(coded, 'fold', split_axis=0, concat_axis=0, tiled=True)]
    all_to_all x1, waiting for transfers between devices: 2.22 us -> 0.01 us  [body(): lax.all_to_all(short, 'fold', split_axis=0, concat_axis=0, tiled=True)]
    unnamed x13 -> x7, local copies, waits for them, and re-layouts: 3.24 us -> 1.58 us
    pallas_call x1, Pallas kernels: 5.88 us -> 4.26 us  [narrow_c(): pl.pallas_call(functools.partial(narrow_c_kernel, n_i=n_i, a_local=a_loca...]
    convert_element_type x1, other arithmetic: 0.49 us -> 1.98 us  [body(): picks = (code == spots).astype(BF16)]
  transfers between devices with their start and end apart: 12 -> 16, of which waited for: 7 -> 4; matrix products, arithmetic and copies ran while one was open for 10% -> 11% of each run, Pallas kernels for 14% -> 17%
where the time goes in v10:
time: 136 us
  Pallas kernels  45.2 us (33%)
  waiting for transfers between devices  36.5 us (27%)
  starting transfers between devices  31 us (23%)
  local copies, waits for them, and re-layouts  16.1 us (12%)
  other arithmetic  6.88 us (5%)
    all_to_all x1, waiting for transfers between devices, body(): lax.all_to_all(coded, 'fold', split_axis=0, concat_axis=0, tiled=True)  28.2 us
    pallas_call x2, Pallas kernels, class_blocks(): pl.pallas_call(functools.partial(block_kernel, n_i=n_i, irreps=irreps, ow...  22.7 us
    pallas_call x1, Pallas kernels, grouped_product(): pl.pallas_call(functools.partial(grouped_kernel, bounds=bounds, irreps=ir...  13.7 us
    transpose x1, local copies, waits for them, and re-layouts, body(): cycle_block.transpose(2, 1, 0, 3)  9.39 us
    ppermute x6, starting transfers between devices, send(): lax.ppermute(value, 'pair', [(p, (p + step) % n_pair) for p in range(n_pa...  8.64 us
    all_to_all x1, starting transfers between devices, body(): lax.all_to_all(coded, 'fold', split_axis=0, concat_axis=0, tiled=True)  8.1 us
    all_to_all x1, starting transfers between devices, body(): lax.all_to_all(short, 'fold', split_axis=0, concat_axis=0, tiled=True)  7.88 us
    ppermute x6, waiting for transfers between devices, send(): lax.ppermute(value, 'pair', [(p, (p + step) % n_pair) for p in range(n_pa...  6.82 us
  transfers between devices with their start and end apart: 16, of which 4 were waited for; matrix products, arithmetic and copies ran while one was open for 11% of the time, Pallas kernels for 17%

profile of v10, /device:TPU:0, one launch (start us, length us, event | category | flops | bytes accessed | tf_op | source)
XLA Modules:
  0.0 136.2 jit_solution(7460871735126972477)
XLA Ops:
  0.0 0.7 pad_add_fusion
  1.0 0.8 select_reduce_fusion.3
  2.5 0.7 xor_reduce_fusion
  3.6 1.6 %copy-done = bf16[4,10,40,640]{3,2,1,0:T(8,128)(2,1)S(1)} copy-done((bf16[4,10,40,640]{3,2,1,0:T(8,128)(2,1)S(1)}, bf16[4,10,40,640]{3,2,1,0:T(8,128)(2,1)}, u32[]{:S(2)}) %copy-start) | copy-done | bytes 2048024
  5.2 4.3 %shard_map.64 = bf16[8,160,200]{2,1,0:T(8,128)(2,1)} custom-call(s32[14]{0:T(128)S(1)} %pad_add_fusion.1.scalars, bf16[4,10,40,640]{3,2,1,0:T(8,128)(2,1)S(1)} %copy-done, s32[40,1]{1,0:T(8,128)S(1)} %copy.22.a_label, s32[1,640]{1,0:T(1,128)S(1)} %get-tuple-element.28.label, bf16[160,640]{1,0:T(8,128)(2,1)S(1)} %fusion.3.to_place), custom_call_target="tpu_custom_call" | custom-call | flops 327680000 | bytes 3145728 | tf_op jit(solution)/shard_map/pallas_call | solution.py:196
  9.4 4.6 %all-to-all-start = ((bf16[8,160,200]{2,1,0:T(8,128)(2,1)}), bf16[8,160,200]{2,1,0:T(8,128)(2,1)S(1)}, u32[]{:S(2)}, u32[]{:S(2)}) async-start(bf16[8,160,200]{2,1,0:T(8,128)(2,1)} %shard_map.64), calls=%async_computation | async-start | bytes 1310720 | tf_op jit(solution)/shard_map/all_to_all | solution.py:325
  15.7 9.4 %copy.23 = bf16[2,80,40,640]{3,2,1,0:T(8,128)(2,1)} copy(bf16[2,80,40,640]{3,0,1,2:T(2,128)(2,1)} %bitcast.61) | data formatting | bytes 16384000 | tf_op jit(solution)/shard_map/transpose | solution.py:326
  26.4 4.5 %shard_map.65 = bf16[16,20,880]{2,1,0:T(8,128)(2,1)} custom-call(bf16[8,160,200]{2,1,0:T(8,128)(2,1)S(1)} %all-to-all-done.x, bf16[160,640]{1,0:T(8,128)(2,1)S(1)} %fusion.3.to_place, s32[8,200,1]{2,1,0:T(8,128)S(1)} %broadcast_xor_fusion.row_label, s32[1,640]{1,0:T(1,128)S(1)} %get-tuple-element.28.label, bf16[528,1664]{1,0:T(8,128)(2,1)S(1)} %and_convert_fusion.to_row), custom_call_target="tpu_custom_call" | custom-call | flops 1124597760 | bytes 3145728 | tf_op jit(solution)/shard_map/pallas_call | solution.py:243
  31.0 7.9 %all-to-all-start.1 = ((bf16[16,20,880]{2,1,0:T(8,128)(2,1)}), bf16[16,20,880]{2,1,0:T(8,128)(2,1)S(1)}, u32[]{:S(2)}, u32[]{:S(2)}) async-start(bf16[16,20,880]{2,1,0:T(8,128)(2,1)} %shard_map.65), calls=%async_computation.1 | async-start | bytes 1376256 | tf_op jit(solution)/shard_map/all_to_all | solution.py:340
  38.9 2.0 %compare_convert_fusion.picks = bf16[8,640,160]{2,1,0:T(8,128)(2,1)} fusion(s32[8,160]{1,0:T(8,128)S(1)} %multiply_add_fusion, s32[640]{0:T(1024)S(1)} %multiply_add_fusion.1), kind=kLoop, calls=%fused_computation | loop fusion | flops 1638400 | bytes 1646080 | tf_op jit(solution)/shard_map/convert_element_type | solution.py:344
  40.8 0.7 broadcast_in_dim.130.c_label
  41.5 11.3 %shard_map.66.refs_14_ = bf16[4,880,320]{2,1,0:T(8,128)(2,1)} custom-call(s32[73]{0:T(128)} %concatenate.10.scalars, bf16[2,40,80,640]{3,2,1,0:T(8,128)(2,1)} %bitcast.59, bf16[80,640]{1,0:T(8,128)(2,1)} %broadcast_in_dim.130.c_label, bf16[8,640,160]{2,1,0:T(8,128)(2,1)} %compare_convert_fusion.picks), custom_call_target="tpu_custom_call" | custom-call | flops 1441792000 | bytes 11534336 | tf_op jit(solution)/shard_map/pallas_call | solution.py:84
  53.1 2.1 %collective-permute-start = (bf16[160,880]{1,0:T(8,128)(2,1)S(1)}, bf16[160,880]{1,0:T(8,128)(2,1)S(1)}, u32[]{:S(2)}, u32[]{:S(2)}) collective-permute-start(bf16[160,880]{1,0:T(8,128)(2,1)S(1)} %slice.45), channel_id=1, source_target_pairs={{0,32},{16,48},{32,64},{48,80},{64,96},{80,112},{96,0},{112,16},{1... | collective-permute-start | bytes 844808 | tf_op jit(solution)/shard_map/ppermute | solution.py:103
  55.2 1.3 collective-permute-start.1
  56.5 1.9 %collective-permute-start.3 = (bf16[160,880]{1,0:T(8,128)(2,1)S(1)}, bf16[160,880]{1,0:T(8,128)(2,1)S(1)}, u32[]{:S(2)}, u32[]{:S(2)}) collective-permute-start(bf16[160,880]{1,0:T(8,128)(2,1)S(1)} %slice.45), channel_id=1, source_target_pairs={{0,96},{16,112},{32,0},{48,16},{64,32},{80,48},{96,64},{112,80},{1... | collective-permute-start | bytes 844808 | tf_op jit(solution)/shard_map/ppermute | solution.py:103
  58.5 11.4 %shard_map.67.refs_15_ = bf16[4,880,320]{2,1,0:T(8,128)(2,1)} custom-call(s32[73]{0:T(128)} %concatenate.10.scalars, bf16[2,40,80,640]{3,2,1,0:T(8,128)(2,1)} %bitcast.60, bf16[80,640]{1,0:T(8,128)(2,1)} %broadcast_in_dim.130.c_label, bf16[8,640,160]{2,1,0:T(8,128)(2,1)} %compare_convert_fusion.picks), custom_call_target="tpu_custom_call" | custom-call | flops 1441792000 | bytes 11534336 | tf_op jit(solution)/shard_map/pallas_call | solution.py:84
  71.0 0.7 collective-permute-start.4
  71.7 2.5 %collective-permute-start.5 = (bf16[160,880]{1,0:T(8,128)(2,1)S(1)}, bf16[160,880]{1,0:T(8,128)(2,1)S(1)}, u32[]{:S(2)}, u32[]{:S(2)}) collective-permute-start(bf16[160,880]{1,0:T(8,128)(2,1)S(1)} %collective-permute-done.1.refs_4_), channel_id=1, source_target_pairs={{0,96},{16,112},{32,0},{48,16},{64,32},{80,48},{96,64},{112,80},{1... | collective-permute-start | bytes 844808 | tf_op jit(solution)/shard_map/ppermute | solution.py:103
  74.7 6.8 %collective-permute-done.4.refs_5_ = bf16[160,880]{1,0:T(8,128)(2,1)S(1)} collective-permute-done((bf16[160,880]{1,0:T(8,128)(2,1)S(1)}, bf16[160,880]{1,0:T(8,128)(2,1)S(1)}, u32[]{:S(2)}, u32[]{:S(2)}) %collective-permute-start.4) | collective-permute-done | bytes 281632 | tf_op jit(solution)/shard_map/ppermute | solution.py:103
  82.1 1.0 collective-permute-done.11.refs_12_
  83.5 13.7 %shard_map.68 = s16[16,88,640]{2,1,0:T(8,128)(2,1)} custom-call(s32[73]{0:T(128)S(1)} %copy-done.1, bf16[320,880]{1,0:T(8,128)(2,1)S(1)} %reshape.244.refs_0_, bf16[160,880]{1,0:T(8,128)(2,1)S(1)} %collective-permute-done.refs_1_, bf16[160,880]{1,0:T(8,128)(2,1)S(1)} %collective-permute-done.2.refs_2_, bf16[160,880]{1,0:T(8,128)(2,1)S(1)} %collective-permute-done.3.refs_3_, ...), custom_call_target="tpu_custom_call" | custom-call | flops 3460300800 | bytes 13631488 | tf_op jit(solution)/shard_map/pallas_call | solution.py:268
  97.3 8.1 %all-to-all-start.2 = ((s16[16,88,640]{2,1,0:T(8,128)(2,1)}), s16[16,88,640]{2,1,0:T(8,128)(2,1)S(1)}, u32[]{:S(2)}, u32[]{:S(2)}) async-start(s16[16,88,640]{2,1,0:T(8,128)(2,1)} %shard_map.68), calls=%async_computation.2 | async-start | bytes 3604480 | tf_op jit(solution)/shard_map/all_to_all | solution.py:366
  105.5 28.2 %all-to-all-done.2 = s16[16,88,640]{2,1,0:T(8,128)(2,1)S(1)} async-done(((s16[16,88,640]{2,1,0:T(8,128)(2,1)}), s16[16,88,640]{2,1,0:T(8,128)(2,1)S(1)}, u32[]{:S(2)}, u32[]{:S(2)}) %all-to-all-start.2) | async-done | bytes 1802272 | tf_op jit(solution)/shard_map/all_to_all | solution.py:366
  135.2 1.1 copy.28
  (78 shorter events, 8.6 us)
Async XLA Ops:
  0.0 14.3 %copy-start.2 = (s32[16]{0:T(128)S(1)}, s32[16]{0:T(128)}, u32[]{:S(2)}) copy-start(s32[16]{0:T(128)} %param.11) | copy-start | bytes 196
  3.6 1.6 %copy-start = (bf16[4,10,40,640]{3,2,1,0:T(8,128)(2,1)S(1)}, bf16[4,10,40,640]{3,2,1,0:T(8,128)(2,1)}, u32[]{:S(2)}) copy-start(bf16[4,10,40,640]{3,2,1,0:T(8,128)(2,1)} %x.5) | copy-start | bytes 6144004
  9.4 17.0 %all-to-all-start = ((bf16[8,160,200]{2,1,0:T(8,128)(2,1)}), bf16[8,160,200]{2,1,0:T(8,128)(2,1)S(1)}, u32[]{:S(2)}, u32[]{:S(2)}) async-start(bf16[8,160,200]{2,1,0:T(8,128)(2,1)} %shard_map.64), calls=%async_computation | async-start | bytes 1310720 | tf_op jit(solution)/shard_map/all_to_all | solution.py:325
  31.0 21.9 %all-to-all-start.1 = ((bf16[16,20,880]{2,1,0:T(8,128)(2,1)}), bf16[16,20,880]{2,1,0:T(8,128)(2,1)S(1)}, u32[]{:S(2)}, u32[]{:S(2)}) async-start(bf16[16,20,880]{2,1,0:T(8,128)(2,1)} %shard_map.65), calls=%async_computation.1 | async-start | bytes 1376256 | tf_op jit(solution)/shard_map/all_to_all | solution.py:340
  53.1 30.4 %copy-start.1 = (s32[73]{0:T(128)S(1)}, s32[73]{0:T(128)}, u32[]{:S(2)}) copy-start(s32[73]{0:T(128)} %concatenate.10.scalars) | copy-start | bytes 880
  53.1 17.2 %collective-permute-start = (bf16[160,880]{1,0:T(8,128)(2,1)S(1)}, bf16[160,880]{1,0:T(8,128)(2,1)S(1)}, u32[]{:S(2)}, u32[]{:S(2)}) collective-permute-start(bf16[160,880]{1,0:T(8,128)(2,1)S(1)} %slice.45), channel_id=1, source_target_pairs={{0,32},{16,48},{32,64},{48,80},{64,96},{80,112},{96,0},{112,16},{1... | collective-permute-start | bytes 844808 | tf_op jit(solution)/shard_map/ppermute | solution.py:103
  55.2 15.1 %collective-permute-start.1 = (bf16[160,880]{1,0:T(8,128)(2,1)S(1)}, bf16[160,880]{1,0:T(8,128)(2,1)S(1)}, u32[]{:S(2)}, u32[]{:S(2)}) collective-permute-start(bf16[160,880]{1,0:T(8,128)(2,1)S(1)} %slice.47), channel_id=1, source_target_pairs={{0,96},{16,112},{32,0},{48,16},{64,32},{80,48},{96,64},{112,80},{1... | collective-permute-start | bytes 844808 | tf_op jit(solution)/shard_map/ppermute | solution.py:103
  56.5 13.8 %collective-permute-start.3 = (bf16[160,880]{1,0:T(8,128)(2,1)S(1)}, bf16[160,880]{1,0:T(8,128)(2,1)S(1)}, u32[]{:S(2)}, u32[]{:S(2)}) collective-permute-start(bf16[160,880]{1,0:T(8,128)(2,1)S(1)} %slice.45), channel_id=1, source_target_pairs={{0,96},{16,112},{32,0},{48,16},{64,32},{80,48},{96,64},{112,80},{1... | collective-permute-start | bytes 844808 | tf_op jit(solution)/shard_map/ppermute | solution.py:103
  58.4 12.4 %collective-permute-start.2 = (bf16[160,880]{1,0:T(8,128)(2,1)S(1)}, bf16[160,880]{1,0:T(8,128)(2,1)S(1)}, u32[]{:S(2)}, u32[]{:S(2)}) collective-permute-start(bf16[160,880]{1,0:T(8,128)(2,1)S(1)} %slice.47), channel_id=1, source_target_pairs={{0,32},{16,48},{32,64},{48,80},{64,96},{80,112},{96,0},{112,16},{1... | collective-permute-start | bytes 844808 | tf_op jit(solution)/shard_map/ppermute | solution.py:103
  70.2 11.9 %collective-permute-start.6 = (bf16[320,880]{1,0:T(8,128)(2,1)S(1)}, bf16[320,880]{1,0:T(8,128)(2,1)S(1)}, u32[]{:S(2)}, u32[]{:S(2)}) collective-permute-start(bf16[320,880]{1,0:T(8,128)(2,1)S(1)} %reshape.244.refs_0_), channel_id=1, source_target_pairs={{0,16},{16,0},{32,48},{48,32},{64,80},{80,64},{96,112},{112,96},{1... | collective-permute-start | bytes 1689608 | tf_op jit(solution)/shard_map/ppermute | solution.py:112
  70.3 3.9 %collective-permute-start.9 = (bf16[160,880]{1,0:T(8,128)(2,1)S(1)}, bf16[160,880]{1,0:T(8,128)(2,1)S(1)}, u32[]{:S(2)}, u32[]{:S(2)}) collective-permute-start(bf16[160,880]{1,0:T(8,128)(2,1)S(1)} %collective-permute-done.3.refs_3_), channel_id=1, source_target_pairs={{0,16},{16,0},{32,48},{48,32},{64,80},{80,64},{96,112},{112,96},{1... | collective-permute-start | bytes 844808 | tf_op jit(solution)/shard_map/ppermute | solution.py:112
  70.9 3.4 %collective-permute-start.8 = (bf16[160,880]{1,0:T(8,128)(2,1)S(1)}, bf16[160,880]{1,0:T(8,128)(2,1)S(1)}, u32[]{:S(2)}, u32[]{:S(2)}) collective-permute-start(bf16[160,880]{1,0:T(8,128)(2,1)S(1)} %collective-permute-done.2.refs_2_), channel_id=1, source_target_pairs={{0,16},{16,0},{32,48},{48,32},{64,80},{80,64},{96,112},{112,96},{1... | collective-permute-start | bytes 844808 | tf_op jit(solution)/shard_map/ppermute | solution.py:112
  71.0 10.6 %collective-permute-start.4 = (bf16[160,880]{1,0:T(8,128)(2,1)S(1)}, bf16[160,880]{1,0:T(8,128)(2,1)S(1)}, u32[]{:S(2)}, u32[]{:S(2)}) collective-permute-start(bf16[160,880]{1,0:T(8,128)(2,1)S(1)} %collective-permute-done.refs_1_), channel_id=1, source_target_pairs={{0,32},{16,48},{32,64},{48,80},{64,96},{80,112},{96,0},{112,16},{1... | collective-permute-start | bytes 844808 | tf_op jit(solution)/shard_map/ppermute | solution.py:103
  71.7 9.8 %collective-permute-start.5 = (bf16[160,880]{1,0:T(8,128)(2,1)S(1)}, bf16[160,880]{1,0:T(8,128)(2,1)S(1)}, u32[]{:S(2)}, u32[]{:S(2)}) collective-permute-start(bf16[160,880]{1,0:T(8,128)(2,1)S(1)} %collective-permute-done.1.refs_4_), channel_id=1, source_target_pairs={{0,96},{16,112},{32,0},{48,16},{64,32},{80,48},{96,64},{112,80},{1... | collective-permute-start | bytes 844808 | tf_op jit(solution)/shard_map/ppermute | solution.py:103
  74.2 7.8 %collective-permute-start.7 = (bf16[160,880]{1,0:T(8,128)(2,1)S(1)}, bf16[160,880]{1,0:T(8,128)(2,1)S(1)}, u32[]{:S(2)}, u32[]{:S(2)}) collective-permute-start(bf16[160,880]{1,0:T(8,128)(2,1)S(1)} %collective-permute-done.refs_1_), channel_id=1, source_target_pairs={{0,16},{16,0},{32,48},{48,32},{64,80},{80,64},{96,112},{112,96},{1... | collective-permute-start | bytes 844808 | tf_op jit(solution)/shard_map/ppermute | solution.py:112
  74.3 7.8 %collective-permute-start.10 = (bf16[160,880]{1,0:T(8,128)(2,1)S(1)}, bf16[160,880]{1,0:T(8,128)(2,1)S(1)}, u32[]{:S(2)}, u32[]{:S(2)}) collective-permute-start(bf16[160,880]{1,0:T(8,128)(2,1)S(1)} %collective-permute-done.1.refs_4_), channel_id=1, source_target_pairs={{0,16},{16,0},{32,48},{48,32},{64,80},{80,64},{96,112},{112,96},{1... | collective-permute-start | bytes 844808 | tf_op jit(solution)/shard_map/ppermute | solution.py:112
  81.5 1.6 %collective-permute-start.11 = (bf16[160,880]{1,0:T(8,128)(2,1)S(1)}, bf16[160,880]{1,0:T(8,128)(2,1)S(1)}, u32[]{:S(2)}, u32[]{:S(2)}) collective-permute-start(bf16[160,880]{1,0:T(8,128)(2,1)S(1)} %collective-permute-done.4.refs_5_), channel_id=1, source_target_pairs={{0,16},{16,0},{32,48},{48,32},{64,80},{80,64},{96,112},{112,96},{1... | collective-permute-start | bytes 844808 | tf_op jit(solution)/shard_map/ppermute | solution.py:112
  81.6 2.0 %collective-permute-start.12 = (bf16[160,880]{1,0:T(8,128)(2,1)S(1)}, bf16[160,880]{1,0:T(8,128)(2,1)S(1)}, u32[]{:S(2)}, u32[]{:S(2)}) collective-permute-start(bf16[160,880]{1,0:T(8,128)(2,1)S(1)} %collective-permute-done.5.refs_6_), channel_id=1, source_target_pairs={{0,16},{16,0},{32,48},{48,32},{64,80},{80,64},{96,112},{112,96},{1... | collective-permute-start | bytes 844808 | tf_op jit(solution)/shard_map/ppermute | solution.py:112
  97.3 36.5 %all-to-all-start.2 = ((s16[16,88,640]{2,1,0:T(8,128)(2,1)}), s16[16,88,640]{2,1,0:T(8,128)(2,1)S(1)}, u32[]{:S(2)}, u32[]{:S(2)}) async-start(s16[16,88,640]{2,1,0:T(8,128)(2,1)} %shard_map.68), calls=%async_computation.2 | async-start | bytes 3604480 | tf_op jit(solution)/shard_map/all_to_all | solution.py:366

commit v11 on v8

--- a/solution.py
+++ b/solution.py
@@ -98,15 +98,15 @@
     )(scalars, cycle, c_label, picks)
 
 
-def gather_pieces(v, n_pair):
+def gather_pieces(v, beside, n_pair):
     def send(value, step):
         return lax.ppermute(value, "pair", [(p, (p + step) % n_pair) for p in range(n_pair)])
 
     half = v.shape[0] // 2
-    up, down = send(v, 2), send(v, -2)
+    up, down, beside = lax.optimization_barrier((send(v, 2), send(v, -2), beside))
     far_up, far_down = send(up[:half], 2), send(down[half:], -2)
     pieces = [v, up, down, far_up, far_down]
-    return pieces + [lax.ppermute(p, "pair", [(q, q ^ 1) for q in range(n_pair)]) for p in pieces]
+    return pieces + [lax.ppermute(p, "pair", [(q, q ^ 1) for q in range(n_pair)]) for p in pieces], beside
 
 
 def grouped_kernel(scalars, *refs, bounds, irreps, halves, window, me):
@@ -335,10 +335,8 @@
     blocks = class_blocks(
         scalars, cycle, c_label, picks, n_i=n_i, irreps=irreps, owns=low + halves * (irreps + 1), k_pairs=kappas // 2
     )
-    short, blocks = lax.optimization_barrier((short, blocks))
-
     short = short.reshape(n_fold * a_part, kappas * c_local)
-    lhs = gather_pieces(short, n_pair)
+    lhs, blocks = gather_pieces(short, blocks, n_pair)
 
     most = min(vmax, -(-vmax // a_local) * a_part)
     window = min(-(-(most + 15) // 16) * 16, n_fold * a_part)

time: 138 us -> 134 us (0.971)
  starting transfers between devices: 28.2 us -> 24.3 us
    ppermute x4, waiting for transfers between devices: 20.3 us -> 6.43 us  [send(): lax.ppermute(value, 'pair', [(p, (p + step) % n_pair) for p in range(n_pa...]
    all_to_all x1, waiting for transfers between devices: 0.01 us -> 13.7 us  [body(): lax.all_to_all(short, 'fold', split_axis=0, concat_axis=0, tiled=True)]
    all_to_all x1, starting transfers between devices: 7.87 us -> 3.98 us  [body(): lax.all_to_all(coded, 'fold', split_axis=0, concat_axis=0, tiled=True)]
    pallas_call x1, Pallas kernels: 17.4 us -> 16 us  [class_blocks(): pl.pallas_call(functools.partial(block_kernel, n_i=n_i, irreps=irreps, ow...]
  transfers between devices with their start and end apart: 12 -> 12, of which waited for: 5 -> 6; matrix products, arithmetic and copies ran while one was open for 9% -> 9% of each run, Pallas kernels for 13% -> 12%
where the time goes in v11:
time: 134 us; the launch traced here: 133 us
  waiting for transfers between devices  50 us (37%)
  Pallas kernels  38.1 us (28%)
  starting transfers between devices  24.3 us (18%)
  local copies, waits for them, and re-layouts  14.7 us (11%)
  other arithmetic  5.38 us (4%)
    all_to_all x1, waiting for transfers between devices, body(): lax.all_to_all(coded, 'fold', split_axis=0, concat_axis=0, tiled=True)  28.3 us
    pallas_call x1, Pallas kernels, class_blocks(): pl.pallas_call(functools.partial(block_kernel, n_i=n_i, irreps=irreps, ow...  16 us
    all_to_all x1, waiting for transfers between devices, body(): lax.all_to_all(short, 'fold', split_axis=0, concat_axis=0, tiled=True)  13.7 us
    pallas_call x1, Pallas kernels, grouped_product(): pl.pallas_call(functools.partial(grouped_kernel, bounds=bounds, irreps=ir...  13.3 us
    transpose x1, local copies, waits for them, and re-layouts, body(): cycle_block.transpose(2, 1, 0, 3)  9.39 us
    all_to_all x1, starting transfers between devices, body(): lax.all_to_all(short, 'fold', split_axis=0, concat_axis=0, tiled=True)  7.87 us
    ppermute x4, starting transfers between devices, send(): lax.ppermute(value, 'pair', [(p, (p + step) % n_pair) for p in range(n_pa...  6.86 us
    ppermute x4, waiting for transfers between devices, send(): lax.ppermute(value, 'pair', [(p, (p + step) % n_pair) for p in range(n_pa...  6.43 us
  transfers between devices with their start and end apart: 12, of which 6 were waited for; matrix products, arithmetic and copies ran while one was open for 9% of the time, Pallas kernels for 12%

profile of v11, /device:TPU:0, one launch (start us, length us, event | category | flops | bytes accessed | tf_op | source)
XLA Modules:
  0.0 133.1 jit_solution(9856314735267305278)
XLA Ops:
  0.0 0.7 pad_add_fusion
  1.0 0.8 select_reduce_fusion.3
  1.8 0.7 dynamic_slice.22
  2.5 0.7 xor_reduce_fusion
  3.6 1.6 %copy-done = bf16[4,10,40,640]{3,2,1,0:T(8,128)(2,1)S(1)} copy-done((bf16[4,10,40,640]{3,2,1,0:T(8,128)(2,1)S(1)}, bf16[4,10,40,640]{3,2,1,0:T(8,128)(2,1)}, u32[]{:S(2)}) %copy-start) | copy-done | bytes 2048024
  5.2 4.3 %shard_map.64 = bf16[8,160,200]{2,1,0:T(8,128)(2,1)} custom-call(s32[14]{0:T(128)S(1)} %pad_add_fusion.1.scalars, bf16[4,10,40,640]{3,2,1,0:T(8,128)(2,1)S(1)} %copy-done, s32[40,1]{1,0:T(8,128)S(1)} %copy.22.a_label, s32[1,640]{1,0:T(1,128)S(1)} %get-tuple-element.22.label, bf16[160,640]{1,0:T(8,128)(2,1)S(1)} %fusion.3.to_place), custom_call_target="tpu_custom_call" | custom-call | flops 327680000 | bytes 3145728 | tf_op jit(solution)/shard_map/pallas_call | solution.py:184
  9.4 4.6 %all-to-all-start = ((bf16[8,160,200]{2,1,0:T(8,128)(2,1)}), bf16[8,160,200]{2,1,0:T(8,128)(2,1)S(1)}, u32[]{:S(2)}, u32[]{:S(2)}) async-start(bf16[8,160,200]{2,1,0:T(8,128)(2,1)} %shard_map.64), calls=%async_computation | async-start | bytes 1310720 | tf_op jit(solution)/shard_map/all_to_all | solution.py:309
  14.1 9.4 %copy.23 = bf16[2,80,40,640]{3,2,1,0:T(8,128)(2,1)} copy(bf16[2,80,40,640]{3,0,1,2:T(2,128)(2,1)} %bitcast.60) | data formatting | bytes 16384000 | tf_op jit(solution)/shard_map/transpose | solution.py:310
  25.0 0.6 and_convert_fusion.to_row
  25.7 4.6 %shard_map.65 = bf16[16,20,880]{2,1,0:T(8,128)(2,1)} custom-call(bf16[8,160,200]{2,1,0:T(8,128)(2,1)S(1)} %all-to-all-done.x, bf16[160,640]{1,0:T(8,128)(2,1)S(1)} %fusion.3.to_place, s32[8,200,1]{2,1,0:T(8,128)S(1)} %broadcast_xor_fusion.row_label, s32[1,640]{1,0:T(1,128)S(1)} %get-tuple-element.22.label, bf16[528,1664]{1,0:T(8,128)(2,1)S(1)} %and_convert_fusion.to_row), custom_call_target="tpu_custom_call" | custom-call | flops 1124597760 | bytes 3145728 | tf_op jit(solution)/shard_map/pallas_call | solution.py:231
  30.3 7.9 %all-to-all-start.1 = ((bf16[16,20,880]{2,1,0:T(8,128)(2,1)}), bf16[16,20,880]{2,1,0:T(8,128)(2,1)S(1)}, u32[]{:S(2)}, u32[]{:S(2)}) async-start(bf16[16,20,880]{2,1,0:T(8,128)(2,1)} %shard_map.65), calls=%async_computation.1 | async-start | bytes 1376256 | tf_op jit(solution)/shard_map/all_to_all | solution.py:324
  38.3 13.7 %all-to-all-done.1 = bf16[16,20,880]{2,1,0:T(8,128)(2,1)S(1)} async-done(((bf16[16,20,880]{2,1,0:T(8,128)(2,1)}), bf16[16,20,880]{2,1,0:T(8,128)(2,1)S(1)}, u32[]{:S(2)}, u32[]{:S(2)}) %all-to-all-start.1) | async-done | bytes 563232 | tf_op jit(solution)/shard_map/all_to_all | solution.py:324
  52.2 1.7 %collective-permute-start = (bf16[320,880]{1,0:T(8,128)(2,1)S(1)}, bf16[320,880]{1,0:T(8,128)(2,1)S(1)}, u32[]{:S(2)}, u32[]{:S(2)}) collective-permute-start(bf16[320,880]{1,0:T(8,128)(2,1)S(1)} %reshape.239.refs_0_), channel_id=1, source_target_pairs={{0,32},{16,48},{32,64},{48,80},{64,96},{80,112},{96,0},{112,16},{1... | collective-permute-start | bytes 1689608 | tf_op jit(solution)/shard_map/ppermute | solution.py:103
  54.0 1.6 %collective-permute-start.1 = (bf16[320,880]{1,0:T(8,128)(2,1)S(1)}, bf16[320,880]{1,0:T(8,128)(2,1)S(1)}, u32[]{:S(2)}, u32[]{:S(2)}) collective-permute-start(bf16[320,880]{1,0:T(8,128)(2,1)S(1)} %reshape.239.refs_0_), channel_id=1, source_target_pairs={{0,96},{16,112},{32,0},{48,16},{64,32},{80,48},{96,64},{112,80},{1... | collective-permute-start | bytes 1689608 | tf_op jit(solution)/shard_map/ppermute | solution.py:103
  56.4 16.0 %shard_map.66.refs_10_ = bf16[8,880,320]{2,1,0:T(8,128)(2,1)} custom-call(s32[73]{0:T(128)S(1)} %concatenate.10.scalars, bf16[2,40,80,640]{3,2,1,0:T(8,128)(2,1)} %bitcast.59, bf16[80,640]{1,0:T(8,128)(2,1)S(1)} %broadcast_in_dim.130.c_label, bf16[8,640,160]{2,1,0:T(8,128)(2,1)S(1)} %compare_convert_fusion.picks), custom_call_target="tpu_custom_call" | custom-call | flops 2883584000 | bytes 14680064 | tf_op jit(solution)/shard_map/pallas_call | solution.py:84
  72.4 0.5 collective-permute-start.2
  73.0 3.0 %collective-permute-start.3 = (bf16[160,880]{1,0:T(8,128)(2,1)S(1)}, bf16[160,880]{1,0:T(8,128)(2,1)S(1)}, u32[]{:S(2)}, u32[]{:S(2)}) collective-permute-start(bf16[160,880]{1,0:T(8,128)(2,1)S(1)} %slice.39), channel_id=1, source_target_pairs={{0,96},{16,112},{32,0},{48,16},{64,32},{80,48},{96,64},{112,80},{1... | collective-permute-start | bytes 844808 | tf_op jit(solution)/shard_map/ppermute | solution.py:103
  76.5 6.4 %collective-permute-done.2.refs_3_ = bf16[160,880]{1,0:T(8,128)(2,1)S(1)} collective-permute-done((bf16[160,880]{1,0:T(8,128)(2,1)S(1)}, bf16[160,880]{1,0:T(8,128)(2,1)S(1)}, u32[]{:S(2)}, u32[]{:S(2)}) %collective-permute-start.2) | collective-permute-done | bytes 281632 | tf_op jit(solution)/shard_map/ppermute | solution.py:103
  82.9 0.5 collective-permute-start.8
  83.4 1.1 collective-permute-done.7.refs_8_
  84.9 13.3 %shard_map.67 = s16[16,88,640]{2,1,0:T(8,128)(2,1)} custom-call(s32[73]{0:T(128)S(1)} %concatenate.10.scalars, bf16[320,880]{1,0:T(8,128)(2,1)S(1)} %reshape.239.refs_0_, bf16[320,880]{1,0:T(8,128)(2,1)S(1)} %collective-permute-done.refs_1_, bf16[320,880]{1,0:T(8,128)(2,1)S(1)} %collective-permute-done.1.refs_2_, ...), custom_call_target="tpu_custom_call" | custom-call | flops 3460300800 | bytes 13631488 | tf_op jit(solution)/shard_map/pallas_call | solution.py:256
  98.2 4.0 %all-to-all-start.2 = ((s16[16,88,640]{2,1,0:T(8,128)(2,1)}), s16[16,88,640]{2,1,0:T(8,128)(2,1)S(1)}, u32[]{:S(2)}, u32[]{:S(2)}) async-start(s16[16,88,640]{2,1,0:T(8,128)(2,1)} %shard_map.67), calls=%async_computation.2 | async-start | bytes 3604480 | tf_op jit(solution)/shard_map/all_to_all | solution.py:346
  102.3 28.3 %all-to-all-done.2 = s16[16,88,640]{2,1,0:T(8,128)(2,1)S(1)} async-done(((s16[16,88,640]{2,1,0:T(8,128)(2,1)}), s16[16,88,640]{2,1,0:T(8,128)(2,1)S(1)}, u32[]{:S(2)}, u32[]{:S(2)}) %all-to-all-start.2) | async-done | bytes 1802272 | tf_op jit(solution)/shard_map/all_to_all | solution.py:346
  132.0 1.1 copy.28
  (66 shorter events, 6.0 us)
Async XLA Ops:
  3.6 1.6 %copy-start = (bf16[4,10,40,640]{3,2,1,0:T(8,128)(2,1)S(1)}, bf16[4,10,40,640]{3,2,1,0:T(8,128)(2,1)}, u32[]{:S(2)}) copy-start(bf16[4,10,40,640]{3,2,1,0:T(8,128)(2,1)} %x.5) | copy-start | bytes 6144004
  9.4 16.3 %all-to-all-start = ((bf16[8,160,200]{2,1,0:T(8,128)(2,1)}), bf16[8,160,200]{2,1,0:T(8,128)(2,1)S(1)}, u32[]{:S(2)}, u32[]{:S(2)}) async-start(bf16[8,160,200]{2,1,0:T(8,128)(2,1)} %shard_map.64), calls=%async_computation | async-start | bytes 1310720 | tf_op jit(solution)/shard_map/all_to_all | solution.py:309
  14.1 9.4 %copy-start.1 = (s32[16]{0:T(128)S(1)}, s32[16]{0:T(128)}, u32[]{:S(2)}) copy-start(s32[16]{0:T(128)} %param.11) | copy-start | bytes 196
  30.3 21.7 %all-to-all-start.1 = ((bf16[16,20,880]{2,1,0:T(8,128)(2,1)}), bf16[16,20,880]{2,1,0:T(8,128)(2,1)S(1)}, u32[]{:S(2)}, u32[]{:S(2)}) async-start(bf16[16,20,880]{2,1,0:T(8,128)(2,1)} %shard_map.65), calls=%async_computation.1 | async-start | bytes 1376256 | tf_op jit(solution)/shard_map/all_to_all | solution.py:324
  52.2 20.2 %collective-permute-start = (bf16[320,880]{1,0:T(8,128)(2,1)S(1)}, bf16[320,880]{1,0:T(8,128)(2,1)S(1)}, u32[]{:S(2)}, u32[]{:S(2)}) collective-permute-start(bf16[320,880]{1,0:T(8,128)(2,1)S(1)} %reshape.239.refs_0_), channel_id=1, source_target_pairs={{0,32},{16,48},{32,64},{48,80},{64,96},{80,112},{96,0},{112,16},{1... | collective-permute-start | bytes 1689608 | tf_op jit(solution)/shard_map/ppermute | solution.py:103
  54.0 18.4 %collective-permute-start.1 = (bf16[320,880]{1,0:T(8,128)(2,1)S(1)}, bf16[320,880]{1,0:T(8,128)(2,1)S(1)}, u32[]{:S(2)}, u32[]{:S(2)}) collective-permute-start(bf16[320,880]{1,0:T(8,128)(2,1)S(1)} %reshape.239.refs_0_), channel_id=1, source_target_pairs={{0,96},{16,112},{32,0},{48,16},{64,32},{80,48},{96,64},{112,80},{1... | collective-permute-start | bytes 1689608 | tf_op jit(solution)/shard_map/ppermute | solution.py:103
  72.4 11.1 %collective-permute-start.4 = (bf16[320,880]{1,0:T(8,128)(2,1)S(1)}, bf16[320,880]{1,0:T(8,128)(2,1)S(1)}, u32[]{:S(2)}, u32[]{:S(2)}) collective-permute-start(bf16[320,880]{1,0:T(8,128)(2,1)S(1)} %reshape.239.refs_0_), channel_id=1, source_target_pairs={{0,16},{16,0},{32,48},{48,32},{64,80},{80,64},{96,112},{112,96},{1... | collective-permute-start | bytes 1689608 | tf_op jit(solution)/shard_map/ppermute | solution.py:109
  72.4 10.5 %collective-permute-start.2 = (bf16[160,880]{1,0:T(8,128)(2,1)S(1)}, bf16[160,880]{1,0:T(8,128)(2,1)S(1)}, u32[]{:S(2)}, u32[]{:S(2)}) collective-permute-start(bf16[160,880]{1,0:T(8,128)(2,1)S(1)} %slice.38), channel_id=1, source_target_pairs={{0,32},{16,48},{32,64},{48,80},{64,96},{80,112},{96,0},{112,16},{1... | collective-permute-start | bytes 844808 | tf_op jit(solution)/shard_map/ppermute | solution.py:103
  73.0 10.0 %collective-permute-start.3 = (bf16[160,880]{1,0:T(8,128)(2,1)S(1)}, bf16[160,880]{1,0:T(8,128)(2,1)S(1)}, u32[]{:S(2)}, u32[]{:S(2)}) collective-permute-start(bf16[160,880]{1,0:T(8,128)(2,1)S(1)} %slice.39), channel_id=1, source_target_pairs={{0,96},{16,112},{32,0},{48,16},{64,32},{80,48},{96,64},{112,80},{1... | collective-permute-start | bytes 844808 | tf_op jit(solution)/shard_map/ppermute | solution.py:103
  76.0 8.9 %collective-permute-start.5 = (bf16[320,880]{1,0:T(8,128)(2,1)S(1)}, bf16[320,880]{1,0:T(8,128)(2,1)S(1)}, u32[]{:S(2)}, u32[]{:S(2)}) collective-permute-start(bf16[320,880]{1,0:T(8,128)(2,1)S(1)} %collective-permute-done.refs_1_), channel_id=1, source_target_pairs={{0,16},{16,0},{32,48},{48,32},{64,80},{80,64},{96,112},{112,96},{1... | collective-permute-start | bytes 1689608 | tf_op jit(solution)/shard_map/ppermute | solution.py:109
  76.0 8.9 %collective-permute-start.6 = (bf16[320,880]{1,0:T(8,128)(2,1)S(1)}, bf16[320,880]{1,0:T(8,128)(2,1)S(1)}, u32[]{:S(2)}, u32[]{:S(2)}) collective-permute-start(bf16[320,880]{1,0:T(8,128)(2,1)S(1)} %collective-permute-done.1.refs_2_), channel_id=1, source_target_pairs={{0,16},{16,0},{32,48},{48,32},{64,80},{80,64},{96,112},{112,96},{1... | collective-permute-start | bytes 1689608 | tf_op jit(solution)/shard_map/ppermute | solution.py:109
  82.9 1.6 %collective-permute-start.7 = (bf16[160,880]{1,0:T(8,128)(2,1)S(1)}, bf16[160,880]{1,0:T(8,128)(2,1)S(1)}, u32[]{:S(2)}, u32[]{:S(2)}) collective-permute-start(bf16[160,880]{1,0:T(8,128)(2,1)S(1)} %collective-permute-done.2.refs_3_), channel_id=1, source_target_pairs={{0,16},{16,0},{32,48},{48,32},{64,80},{80,64},{96,112},{112,96},{1... | collective-permute-start | bytes 844808 | tf_op jit(solution)/shard_map/ppermute | solution.py:109
  82.9 2.0 %collective-permute-start.8 = (bf16[160,880]{1,0:T(8,128)(2,1)S(1)}, bf16[160,880]{1,0:T(8,128)(2,1)S(1)}, u32[]{:S(2)}, u32[]{:S(2)}) collective-permute-start(bf16[160,880]{1,0:T(8,128)(2,1)S(1)} %collective-permute-done.3.refs_4_), channel_id=1, source_target_pairs={{0,16},{16,0},{32,48},{48,32},{64,80},{80,64},{96,112},{112,96},{1... | collective-permute-start | bytes 844808 | tf_op jit(solution)/shard_map/ppermute | solution.py:109
  98.2 32.4 %all-to-all-start.2 = ((s16[16,88,640]{2,1,0:T(8,128)(2,1)}), s16[16,88,640]{2,1,0:T(8,128)(2,1)S(1)}, u32[]{:S(2)}, u32[]{:S(2)}) async-start(s16[16,88,640]{2,1,0:T(8,128)(2,1)} %shard_map.67), calls=%async_computation.2 | async-start | bytes 3604480 | tf_op jit(solution)/shard_map/all_to_all | solution.py:346

commit v12 on v11

--- a/solution.py
+++ b/solution.py
@@ -326,6 +326,7 @@
     code = (vir * vmax + vir_place)[None, :, None]
     spots = jnp.arange(irreps * vmax, dtype=jnp.int32).reshape(irreps, 1, vmax)
     picks = (code == spots).astype(BF16)
+    short, picks = lax.optimization_barrier((short, picks))
     inside = starts % a_local
     bounds = [starts // a_local * a_part + jnp.clip(inside - h * a_part, 0, a_part) for h in range(halves)]
     scalars = jnp.concatenate([i_labels, k_from // 2, j_labels] + bounds + [own_vir, pair[None]]).astype(jnp.int32)

time: 134 us -> 138 us (1.030)
  local copies, waits for them, and re-layouts: 14.7 us -> 17.8 us
    slice x2, local copies, waits for them, and re-layouts: 0.05 us -> 1.96 us  [gather_pieces(): far_up, far_down = (send(up[:half], 2), send(down[half:], -2))]
  transfers between devices with their start and end apart: 12 -> 12, of which waited for: 6 -> 7; matrix products, arithmetic and copies ran while one was open for 9% -> 11% of each run, Pallas kernels for 12% -> 12%
where the time goes in v12:
time: 138 us; the launch traced here: 136 us
  waiting for transfers between devices  49 us (36%)
  Pallas kernels  38.7 us (28%)
  starting transfers between devices  24.3 us (18%)
  local copies, waits for them, and re-layouts  17.8 us (13%)
  other arithmetic  5.39 us (4%)
    all_to_all x1, waiting for transfers between devices, body(): lax.all_to_all(coded, 'fold', split_axis=0, concat_axis=0, tiled=True)  28.3 us
    pallas_call x1, Pallas kernels, class_blocks(): pl.pallas_call(functools.partial(block_kernel, n_i=n_i, irreps=irreps, ow...  16.1 us
    pallas_call x1, Pallas kernels, grouped_product(): pl.pallas_call(functools.partial(grouped_kernel, bounds=bounds, irreps=ir...  13.7 us
    all_to_all x1, waiting for transfers between devices, body(): lax.all_to_all(short, 'fold', split_axis=0, concat_axis=0, tiled=True)  13.2 us
    transpose x1, local copies, waits for them, and re-layouts, body(): cycle_block.transpose(2, 1, 0, 3)  9.39 us
    all_to_all x1, starting transfers between devices, body(): lax.all_to_all(short, 'fold', split_axis=0, concat_axis=0, tiled=True)  7.93 us
    ppermute x4, starting transfers between devices, send(): lax.ppermute(value, 'pair', [(p, (p + step) % n_pair) for p in range(n_pa...  6.86 us
    ppermute x4, waiting for transfers between devices, send(): lax.ppermute(value, 'pair', [(p, (p + step) % n_pair) for p in range(n_pa...  5.96 us
  transfers between devices with their start and end apart: 12, of which 7 were waited for; matrix products, arithmetic and copies ran while one was open for 11% of the time, Pallas kernels for 12%

profile of v12, /device:TPU:0, one launch (start us, length us, event | category | flops | bytes accessed | tf_op | source)
XLA Modules:
  0.0 135.8 jit_solution(11536546246018190835)
XLA Ops:
  0.0 0.7 pad_add_fusion
  1.0 0.8 select_reduce_fusion.3
  2.5 0.7 xor_reduce_fusion
  3.6 1.6 %copy-done = bf16[4,10,40,640]{3,2,1,0:T(8,128)(2,1)S(1)} copy-done((bf16[4,10,40,640]{3,2,1,0:T(8,128)(2,1)S(1)}, bf16[4,10,40,640]{3,2,1,0:T(8,128)(2,1)}, u32[]{:S(2)}) %copy-start) | copy-done | bytes 2048024
  5.2 4.3 %shard_map.64 = bf16[8,160,200]{2,1,0:T(8,128)(2,1)} custom-call(s32[14]{0:T(128)S(1)} %pad_add_fusion.1.scalars, bf16[4,10,40,640]{3,2,1,0:T(8,128)(2,1)S(1)} %copy-done, s32[40,1]{1,0:T(8,128)S(1)} %copy.22.a_label, s32[1,640]{1,0:T(1,128)S(1)} %get-tuple-element.26.label, bf16[160,640]{1,0:T(8,128)(2,1)S(1)} %fusion.3.to_place), custom_call_target="tpu_custom_call" | custom-call | flops 327680000 | bytes 3145728 | tf_op jit(solution)/shard_map/pallas_call | solution.py:184
  9.4 4.6 %all-to-all-start = ((bf16[8,160,200]{2,1,0:T(8,128)(2,1)}), bf16[8,160,200]{2,1,0:T(8,128)(2,1)S(1)}, u32[]{:S(2)}, u32[]{:S(2)}) async-start(bf16[8,160,200]{2,1,0:T(8,128)(2,1)} %shard_map.64), calls=%async_computation | async-start | bytes 1310720 | tf_op jit(solution)/shard_map/all_to_all | solution.py:309
  14.1 9.4 %copy.23 = bf16[2,80,40,640]{3,2,1,0:T(8,128)(2,1)} copy(bf16[2,80,40,640]{3,0,1,2:T(2,128)(2,1)} %bitcast.60) | data formatting | bytes 16384000 | tf_op jit(solution)/shard_map/transpose | solution.py:310
  25.7 4.6 %shard_map.65 = bf16[16,20,880]{2,1,0:T(8,128)(2,1)} custom-call(bf16[8,160,200]{2,1,0:T(8,128)(2,1)S(1)} %all-to-all-done.x, bf16[160,640]{1,0:T(8,128)(2,1)S(1)} %fusion.3.to_place, s32[8,200,1]{2,1,0:T(8,128)S(1)} %broadcast_xor_fusion.row_label, s32[1,640]{1,0:T(1,128)S(1)} %get-tuple-element.26.label, bf16[528,1664]{1,0:T(8,128)(2,1)S(1)} %and_convert_fusion.to_row), custom_call_target="tpu_custom_call" | custom-call | flops 1124597760 | bytes 3145728 | tf_op jit(solution)/shard_map/pallas_call | solution.py:231
  30.3 7.9 %all-to-all-start.1 = ((bf16[16,20,880]{2,1,0:T(8,128)(2,1)}), bf16[16,20,880]{2,1,0:T(8,128)(2,1)}, u32[]{:S(2)}, u32[]{:S(2)}) async-start(bf16[16,20,880]{2,1,0:T(8,128)(2,1)} %shard_map.65), calls=%async_computation.1 | async-start | bytes 1376256 | tf_op jit(solution)/shard_map/all_to_all | solution.py:324
  38.9 13.2 %all-to-all-done.1 = bf16[16,20,880]{2,1,0:T(8,128)(2,1)} async-done(((bf16[16,20,880]{2,1,0:T(8,128)(2,1)}), bf16[16,20,880]{2,1,0:T(8,128)(2,1)}, u32[]{:S(2)}, u32[]{:S(2)}) %all-to-all-start.1) | async-done | bytes 563232 | tf_op jit(solution)/shard_map/all_to_all | solution.py:324
  52.1 1.4 %reshape.242.refs_0_ = bf16[320,880]{1,0:T(8,128)(2,1)S(1)} reshape(bf16[16,20,880]{2,1,0:T(8,128)(2,1)} %all-to-all-done.1) | data formatting | bytes 1126400 | tf_op jit(solution)/shard_map/reshape | solution.py:339
  53.5 1.7 %collective-permute-start = (bf16[320,880]{1,0:T(8,128)(2,1)S(1)}, bf16[320,880]{1,0:T(8,128)(2,1)}, u32[]{:S(2)}, u32[]{:S(2)}) collective-permute-start(bf16[320,880]{1,0:T(8,128)(2,1)S(1)} %reshape.242.refs_0_), channel_id=1, source_target_pairs={{0,32},{16,48},{32,64},{48,80},{64,96},{80,112},{96,0},{112,16},{1... | collective-permute-start | bytes 1689608 | tf_op jit(solution)/shard_map/ppermute | solution.py:103
  55.2 1.6 %collective-permute-start.1 = (bf16[320,880]{1,0:T(8,128)(2,1)S(1)}, bf16[320,880]{1,0:T(8,128)(2,1)}, u32[]{:S(2)}, u32[]{:S(2)}) collective-permute-start(bf16[320,880]{1,0:T(8,128)(2,1)S(1)} %reshape.242.refs_0_), channel_id=1, source_target_pairs={{0,96},{16,112},{32,0},{48,16},{64,32},{80,48},{96,64},{112,80},{1... | collective-permute-start | bytes 1689608 | tf_op jit(solution)/shard_map/ppermute | solution.py:103
  57.1 16.1 %shard_map.66.refs_10_ = bf16[8,880,320]{2,1,0:T(8,128)(2,1)} custom-call(s32[73]{0:T(128)S(1)} %concatenate.10.scalars, bf16[2,40,80,640]{3,2,1,0:T(8,128)(2,1)} %bitcast.59, bf16[80,640]{1,0:T(8,128)(2,1)S(1)} %broadcast_in_dim.130.c_label, bf16[8,640,160]{2,1,0:T(8,128)(2,1)S(1)} %compare_convert_fusion.picks), custom_call_target="tpu_custom_call" | custom-call | flops 2883584000 | bytes 14680064 | tf_op jit(solution)/shard_map/pallas_call | solution.py:84
  73.2 1.0 slice.38
  74.2 0.7 collective-permute-start.2
  74.9 1.0 slice.39
  75.9 2.9 %collective-permute-start.3 = (bf16[160,880]{1,0:T(8,128)(2,1)S(1)}, bf16[160,880]{1,0:T(8,128)(2,1)S(1)}, u32[]{:S(2)}, u32[]{:S(2)}) collective-permute-start(bf16[160,880]{1,0:T(8,128)(2,1)S(1)} %slice.39), channel_id=1, source_target_pairs={{0,96},{16,112},{32,0},{48,16},{64,32},{80,48},{96,64},{112,80},{1... | collective-permute-start | bytes 844808 | tf_op jit(solution)/shard_map/ppermute | solution.py:103
  79.3 5.6 %collective-permute-done.2.refs_3_ = bf16[160,880]{1,0:T(8,128)(2,1)S(1)} collective-permute-done((bf16[160,880]{1,0:T(8,128)(2,1)S(1)}, bf16[160,880]{1,0:T(8,128)(2,1)S(1)}, u32[]{:S(2)}, u32[]{:S(2)}) %collective-permute-start.2) | collective-permute-done | bytes 281632 | tf_op jit(solution)/shard_map/ppermute | solution.py:103
  85.4 1.1 collective-permute-done.7.refs_8_
  86.9 13.7 %shard_map.67 = s16[16,88,640]{2,1,0:T(8,128)(2,1)} custom-call(s32[73]{0:T(128)S(1)} %concatenate.10.scalars, bf16[320,880]{1,0:T(8,128)(2,1)S(1)} %reshape.242.refs_0_, bf16[320,880]{1,0:T(8,128)(2,1)} %collective-permute-done.refs_1_, bf16[320,880]{1,0:T(8,128)(2,1)} %collective-permute-done.1.refs_2_, ...), custom_call_target="tpu_custom_call" | custom-call | flops 3460300800 | bytes 13631488 | tf_op jit(solution)/shard_map/pallas_call | solution.py:256
  100.6 4.3 %all-to-all-start.2 = ((s16[16,88,640]{2,1,0:T(8,128)(2,1)}), s16[16,88,640]{2,1,0:T(8,128)(2,1)S(1)}, u32[]{:S(2)}, u32[]{:S(2)}) async-start(s16[16,88,640]{2,1,0:T(8,128)(2,1)} %shard_map.67), calls=%async_computation.2 | async-start | bytes 3604480 | tf_op jit(solution)/shard_map/all_to_all | solution.py:347
  105.0 28.3 %all-to-all-done.2 = s16[16,88,640]{2,1,0:T(8,128)(2,1)S(1)} async-done(((s16[16,88,640]{2,1,0:T(8,128)(2,1)}), s16[16,88,640]{2,1,0:T(8,128)(2,1)S(1)}, u32[]{:S(2)}, u32[]{:S(2)}) %all-to-all-start.2) | async-done | bytes 1802272 | tf_op jit(solution)/shard_map/all_to_all | solution.py:347
  134.7 1.1 copy.28
  (66 shorter events, 7.5 us)
Async XLA Ops:
  3.6 1.6 %copy-start = (bf16[4,10,40,640]{3,2,1,0:T(8,128)(2,1)S(1)}, bf16[4,10,40,640]{3,2,1,0:T(8,128)(2,1)}, u32[]{:S(2)}) copy-start(bf16[4,10,40,640]{3,2,1,0:T(8,128)(2,1)} %x.5) | copy-start | bytes 6144004
  9.4 16.3 %all-to-all-start = ((bf16[8,160,200]{2,1,0:T(8,128)(2,1)}), bf16[8,160,200]{2,1,0:T(8,128)(2,1)S(1)}, u32[]{:S(2)}, u32[]{:S(2)}) async-start(bf16[8,160,200]{2,1,0:T(8,128)(2,1)} %shard_map.64), calls=%async_computation | async-start | bytes 1310720 | tf_op jit(solution)/shard_map/all_to_all | solution.py:309
  14.1 10.5 %copy-start.1 = (s32[16]{0:T(128)S(1)}, s32[16]{0:T(128)}, u32[]{:S(2)}) copy-start(s32[16]{0:T(128)} %param.11) | copy-start | bytes 196
  30.3 21.8 %all-to-all-start.1 = ((bf16[16,20,880]{2,1,0:T(8,128)(2,1)}), bf16[16,20,880]{2,1,0:T(8,128)(2,1)}, u32[]{:S(2)}, u32[]{:S(2)}) async-start(bf16[16,20,880]{2,1,0:T(8,128)(2,1)} %shard_map.65), calls=%async_computation.1 | async-start | bytes 1376256 | tf_op jit(solution)/shard_map/all_to_all | solution.py:324
  53.5 19.7 %collective-permute-start = (bf16[320,880]{1,0:T(8,128)(2,1)S(1)}, bf16[320,880]{1,0:T(8,128)(2,1)}, u32[]{:S(2)}, u32[]{:S(2)}) collective-permute-start(bf16[320,880]{1,0:T(8,128)(2,1)S(1)} %reshape.242.refs_0_), channel_id=1, source_target_pairs={{0,32},{16,48},{32,64},{48,80},{64,96},{80,112},{96,0},{112,16},{1... | collective-permute-start | bytes 1689608 | tf_op jit(solution)/shard_map/ppermute | solution.py:103
  55.2 18.0 %collective-permute-start.1 = (bf16[320,880]{1,0:T(8,128)(2,1)S(1)}, bf16[320,880]{1,0:T(8,128)(2,1)}, u32[]{:S(2)}, u32[]{:S(2)}) collective-permute-start(bf16[320,880]{1,0:T(8,128)(2,1)S(1)} %reshape.242.refs_0_), channel_id=1, source_target_pairs={{0,96},{16,112},{32,0},{48,16},{64,32},{80,48},{96,64},{112,80},{1... | collective-permute-start | bytes 1689608 | tf_op jit(solution)/shard_map/ppermute | solution.py:103
  57.0 28.4 %collective-permute-start.4 = (bf16[320,880]{1,0:T(8,128)(2,1)S(1)}, bf16[320,880]{1,0:T(8,128)(2,1)S(1)}, u32[]{:S(2)}, u32[]{:S(2)}) collective-permute-start(bf16[320,880]{1,0:T(8,128)(2,1)S(1)} %reshape.242.refs_0_), channel_id=1, source_target_pairs={{0,16},{16,0},{32,48},{48,32},{64,80},{80,64},{96,112},{112,96},{1... | collective-permute-start | bytes 1689608 | tf_op jit(solution)/shard_map/ppermute | solution.py:109
  74.2 10.7 %collective-permute-start.2 = (bf16[160,880]{1,0:T(8,128)(2,1)S(1)}, bf16[160,880]{1,0:T(8,128)(2,1)S(1)}, u32[]{:S(2)}, u32[]{:S(2)}) collective-permute-start(bf16[160,880]{1,0:T(8,128)(2,1)S(1)} %slice.38), channel_id=1, source_target_pairs={{0,32},{16,48},{32,64},{48,80},{64,96},{80,112},{96,0},{112,16},{1... | collective-permute-start | bytes 844808 | tf_op jit(solution)/shard_map/ppermute | solution.py:103
  75.9 9.3 %collective-permute-start.3 = (bf16[160,880]{1,0:T(8,128)(2,1)S(1)}, bf16[160,880]{1,0:T(8,128)(2,1)S(1)}, u32[]{:S(2)}, u32[]{:S(2)}) collective-permute-start(bf16[160,880]{1,0:T(8,128)(2,1)S(1)} %slice.39), channel_id=1, source_target_pairs={{0,96},{16,112},{32,0},{48,16},{64,32},{80,48},{96,64},{112,80},{1... | collective-permute-start | bytes 844808 | tf_op jit(solution)/shard_map/ppermute | solution.py:103
  78.8 8.1 %collective-permute-start.5 = (bf16[320,880]{1,0:T(8,128)(2,1)}, bf16[320,880]{1,0:T(8,128)(2,1)S(1)}, u32[]{:S(2)}, u32[]{:S(2)}) collective-permute-start(bf16[320,880]{1,0:T(8,128)(2,1)} %collective-permute-done.refs_1_), channel_id=1, source_target_pairs={{0,16},{16,0},{32,48},{48,32},{64,80},{80,64},{96,112},{112,96},{1... | collective-permute-start | bytes 1689608 | tf_op jit(solution)/shard_map/ppermute | solution.py:109
  78.8 8.1 %collective-permute-start.6 = (bf16[320,880]{1,0:T(8,128)(2,1)}, bf16[320,880]{1,0:T(8,128)(2,1)S(1)}, u32[]{:S(2)}, u32[]{:S(2)}) collective-permute-start(bf16[320,880]{1,0:T(8,128)(2,1)} %collective-permute-done.1.refs_2_), channel_id=1, source_target_pairs={{0,16},{16,0},{32,48},{48,32},{64,80},{80,64},{96,112},{112,96},{1... | collective-permute-start | bytes 1689608 | tf_op jit(solution)/shard_map/ppermute | solution.py:109
  84.9 1.6 %collective-permute-start.7 = (bf16[160,880]{1,0:T(8,128)(2,1)S(1)}, bf16[160,880]{1,0:T(8,128)(2,1)S(1)}, u32[]{:S(2)}, u32[]{:S(2)}) collective-permute-start(bf16[160,880]{1,0:T(8,128)(2,1)S(1)} %collective-permute-done.2.refs_3_), channel_id=1, source_target_pairs={{0,16},{16,0},{32,48},{48,32},{64,80},{80,64},{96,112},{112,96},{1... | collective-permute-start | bytes 844808 | tf_op jit(solution)/shard_map/ppermute | solution.py:109
  85.2 1.7 %collective-permute-start.8 = (bf16[160,880]{1,0:T(8,128)(2,1)S(1)}, bf16[160,880]{1,0:T(8,128)(2,1)S(1)}, u32[]{:S(2)}, u32[]{:S(2)}) collective-permute-start(bf16[160,880]{1,0:T(8,128)(2,1)S(1)} %collective-permute-done.3.refs_4_), channel_id=1, source_target_pairs={{0,16},{16,0},{32,48},{48,32},{64,80},{80,64},{96,112},{112,96},{1... | collective-permute-start | bytes 844808 | tf_op jit(solution)/shard_map/ppermute | solution.py:109
  100.6 32.7 %all-to-all-start.2 = ((s16[16,88,640]{2,1,0:T(8,128)(2,1)}), s16[16,88,640]{2,1,0:T(8,128)(2,1)S(1)}, u32[]{:S(2)}, u32[]{:S(2)}) async-start(s16[16,88,640]{2,1,0:T(8,128)(2,1)} %shard_map.67), calls=%async_computation.2 | async-start | bytes 3604480 | tf_op jit(solution)/shard_map/all_to_all | solution.py:347
